TPU v7x, 32 devices: a whole 2x2x4 slice. The times are simulated.
32 devices in a mesh: region: 2 (over y), gx: 16 (over z, x, core).
Axes of the slice: x: 2, y: 2, z: 4, core: 2. Of those that a mesh axis runs over, the one named last changes fastest.
Arguments:
- latent: float32 [16, 512, 2048], P(None, 'gx', 'region'), parts along dimension 2, may hold values from -6 to 6
- counts: int32 [16, 512, 2048], P(None, 'gx', 'region'), parts along dimension 2, may hold values from 0 to 4
- land_mask: int32 [512, 2048], P('gx', 'region'), parts along dimension 1, may hold values 0 or 1
- region_ids: int32 [512, 2048], P('gx', 'region'), parts along dimension 1, may hold values from 0 to 7
- kappa_sq: float32 [512, 2048], P('gx', 'region'), parts along dimension 1, may hold values from 0.05 to 2
- covariates: bfloat16 [32, 512, 2048], P(None, 'gx', 'region'), parts along dimension 2, may hold values from -6 to 6
- effects: bfloat16 [64], P('region'), parts along dimension 0, may hold values from -4 to 4
- intercepts: float32 [16], P('region'), parts along dimension 0, may hold values from -2 to 0.5
Outputs:
- newton_step: float32 [16, 512, 2048], P(None, 'gx', 'region'), parts along dimension 2
- residual: float32 [16, 512, 2048], P(None, 'gx', 'region'), parts along dimension 2
There are 2 independent parts, one for each index of `region`. A program takes and returns all parts, laid end to end along the dimension named above; each array names one. Nothing has to cross between parts.
All inputs are finite; a program needn't handle non-finite values. No bound on the sum of `land_mask` on one device may be relied on, other than what follows from the above.
Results may differ from a plain program's by a relative error of at most 0.0003.
Values sent between devices are 32-bit elements; how exact they have to be, the bound alone decides.
No kernel may reach another device: no remote copies, remote signals or barrier semaphores. Data moves between devices by JAX's collectives and lax.ppermute only.
A program may use at most 64 MiB of HBM per device.

v0:
```python
import jax
import jax.numpy as jnp
from jax import lax
from jax.sharding import PartitionSpec as P

TRIALS = 4
ITERS = 2


prior_scale = 0.04
time_coupling = 0.5


def padded(cells, sides, width):
    for axis, dim in sides:
        count = lax.axis_size(axis)
        ends = count - 1
        head = lax.slice_in_dim(cells, 0, width, axis=dim)
        tail = lax.slice_in_dim(cells, cells.shape[dim] - width, cells.shape[dim], axis=dim)
        cells = jnp.concatenate(
            [
                lax.ppermute(tail, axis, [(i, (i + 1) % count) for i in range(ends)]),
                cells,
                lax.ppermute(head, axis, [((i + 1) % count, i) for i in range(ends)]),
            ],
            axis=dim,
        )
    return cells


def stencil(extended, kappa_rows):
    center = extended[:, 1:-1, :]
    side = jnp.pad(center, ((0, 0), (0, 0), (1, 1)))
    beside_all = extended[:, 2:, :] + extended[:, :-2, :] + side[:, :, 2:] + side[:, :, :-2]
    return (kappa_rows + 4.0) * center - beside_all


def temporal(field):
    before = jnp.concatenate([field[:1], field[:-1]], axis=0)
    after = jnp.concatenate([field[1:], field[-1:]], axis=0)
    return 2.0 * field - before - after


def shards(latent, counts, land_mask, region_ids, kappa_sq, covariates, effects, intercepts):

    def prior(field):
        extended = padded(field, (("gx", 1),), 1)
        inner_image = stencil(extended, kappa_sq)
        widened = padded(inner_image, (("gx", 1),), 1)
        outer_image = stencil(widened, kappa_sq)
        return prior_scale * outer_image + time_coupling * temporal(field)

    cov_term = jnp.einsum("k,kxy->xy", effects, covariates, preferred_element_type=jnp.float32)
    offset_sum = jnp.zeros(kappa_sq.shape, jnp.float32)
    for zone in range(intercepts.shape[0]):
        offset_sum = offset_sum + jnp.where(region_ids == zone, intercepts[zone], 0.0)
    predictor = latent + (cov_term + offset_sum)[None]
    probability = jax.nn.sigmoid(predictor)
    land = land_mask.astype(jnp.float32)[None]
    weight = land * float(TRIALS) * probability * (1.0 - probability)
    gradient = land * (counts.astype(jnp.float32) - float(TRIALS) * probability) - prior(latent)
    inverse_diag = 1.0 / (
        prior_scale * ((kappa_sq + 4.0) ** 2 + 4.0) + 2.0 * time_coupling + weight
    )
    newton_step = jnp.zeros_like(latent)
    residual = gradient
    scaled = inverse_diag * residual
    search = scaled
    product_now = lax.psum(jnp.sum(residual * scaled), "gx")
    for iteration in range(ITERS):
        image = prior(search) + weight * search
        step_size = product_now / lax.psum(jnp.sum(search * image), "gx")
        newton_step = newton_step + step_size * search
        residual = residual - step_size * image
        if iteration + 1 < ITERS:
            scaled = inverse_diag * residual
            product_next = lax.psum(jnp.sum(residual * scaled), "gx")
            search = scaled + product_next / product_now * search
            product_now = product_next
    return (newton_step, residual)


def solution(mesh):
    placed = (
        P(None, "gx", "region"),
        P(None, "gx", "region"),
        P("gx", "region"),
        P("gx", "region"),
        P("gx", "region"),
        P(None, "gx", "region"),
        P("region"),
        P("region"),
    )
    return jax.shard_map(
        shards,
        mesh=mesh,
        in_specs=placed,
        out_specs=(P(None, "gx", "region"), P(None, "gx", "region")),
        check_vma=False,
    )
```

profile of v0, /device:TPU:0, one launch (start us, length us, event | category | flops | bytes accessed | tf_op | source)
XLA Modules:
  0.0 190.2 jit_solution(13875874345970649683)
XLA Ops:
  0.6 0.0 copy-start
  0.6 1.4 fusion.56
  2.1 1.3 collective-permute-start
  3.4 3.0 %collective-permute-start.1 = (f32[16,1,1024]{2,1,0:T(1,128)S(1)}, f32[16,1,1024]{2,1,0:T(1,128)S(1)}, u32[]{:S(2)}, u32[]{:S(2)}) collective-permute-start(f32[16,1,1024]{2,1,0:T(1,128)S(1)} %get-tuple-element.32), channel_id=1, source_target_pairs={{0,1},{1,2},{2,3},{3,4},{4,5},{5,6},{6,7},{7,8},{8,9},{9,10},{10,1... | collective-permute-start | bytes 196616 | tf_op jit(solution)/shard_map/ppermute | solution.py:22
  6.4 1.0 fusion.57
  7.4 0.0 copy-start.10
  7.4 0.0 copy-start.8
  7.5 2.5 %fusion.58 = (f32[15,32,1024]{2,1,0:T(8,128)S(1)}, f32[15,32,1024]{2,1,0:T(8,128)S(1)}) fusion(f32[16,32,1024]{2,1,0:T(8,128)} %param.8), kind=kLoop, calls=%fused_computation.97 | loop fusion | bytes 7864320 | tf_op jit(solution)/shard_map/slice | solution.py:39
  10.0 0.0 copy-start.1
  10.0 0.7 fusion.59
  10.7 2.3 %fusion.39 = f32[1,32,1024]{2,0,1:T(1,128)S(1)} fusion(bf16[32,32,1024]{2,1,0:T(8,128)(2,1)S(1)} %copy-done, bf16[32]{0:T(256)(128)(2,1)S(1)} %copy-done.11), kind=kOutput, calls=%fused_computation.66 | convolution fusion | flops 2097152 | bytes 2228288 | tf_op jit(solution)/shard_map/k,kxy->xy/dot_general | solution.py:53
  13.0 5.3 %bitcast_add_fusion = f32[32,1024]{1,0:T(8,128)S(1)} fusion(f32[1,32,1024]{2,0,1:T(1,128)S(1)} %fusion.39, s32[32,1024]{1,0:T(8,128)S(1)} %copy-done.9, f32[]{:T(128)} %bitcast.9, f32[]{:T(128)} %bitcast.8, f32[]{:T(128)} %bitcast.7, f32[]{:T(128)} %bitcast.6, f32[]{:T(128)} %bitcast.5, f32[]{:T(128)} %bitcast.4, f32[]{:T(128)} %bitcast.3, f32[]{:T(128)} %bitcast.2), kind=kLoop, calls=%fused_computation.81 | loop fusion | flops 786432 | bytes 393248 | tf_op jit(solution)/shard_map/add | solution.py:57
  18.3 0.0 copy-start.7
  18.4 0.0 copy-start.6
  18.4 1.4 fusion.2
  19.8 0.1 fusion.55
  19.9 1.3 collective-permute-start.2
  21.2 5.1 %collective-permute-start.3 = (f32[16,1,1024]{2,1,0:T(1,128)S(1)}, f32[16,1,1024]{2,1,0:T(1,128)S(1)}, u32[]{:S(2)}, u32[]{:S(2)}) collective-permute-start(f32[16,1,1024]{2,1,0:T(1,128)S(1)} %get-tuple-element.30), channel_id=1, source_target_pairs={{0,1},{1,2},{2,3},{3,4},{4,5},{5,6},{6,7},{7,8},{8,9},{9,10},{10,1... | collective-permute-start | bytes 196616 | tf_op jit(solution)/shard_map/ppermute | solution.py:22
  26.3 0.8 collective-permute-done.3
  27.2 3.4 %fusion.42 = (f32[16,32,1024]{2,1,0:T(8,128)S(1)}, f32[16,32,1024]{2,1,0:T(8,128)S(1)}) fusion(f32[32,1024]{1,0:T(8,128)S(1)} %get-tuple-element.38, f32[16,32,1024]{2,1,0:T(8,128)S(1)} %copy-done.1, f32[32,1024]{1,0:T(8,128)S(1)} %bitcast_add_fusion, f32[32,1024]{1,0:T(8,128)S(1)} %broadcast_multiply_fusion, f32[1,32,1024]{2,1,0:T(8,128)S(1)} %get-tuple-element.34, ...), kind=kLoop, calls=%fused_computation.80 | loop fusion | flops 15728640 | bytes 15466496 | tf_op jit(solution)/shard_map/mul | solution.py:67
  30.5 0.1 fusion.52
  30.7 1.3 collective-permute-start.4
  32.0 5.2 %collective-permute-start.5 = (f32[16,1,1024]{2,1,0:T(1,128)S(1)}, f32[16,1,1024]{2,1,0:T(1,128)S(1)}, u32[]{:S(2)}, u32[]{:S(2)}) collective-permute-start(f32[16,1,1024]{2,1,0:T(1,128)S(1)} %get-tuple-element.24), channel_id=1, source_target_pairs={{0,1},{1,2},{2,3},{3,4},{4,5},{5,6},{6,7},{7,8},{8,9},{9,10},{10,1... | collective-permute-start | bytes 196616 | tf_op jit(solution)/shard_map/ppermute | solution.py:22
  37.1 0.5 fusion.54
  37.7 0.4 collective-permute-done.5
  38.0 1.4 fusion.11
  39.4 0.1 fusion.51
  39.5 1.3 collective-permute-start.6
  40.8 6.0 %collective-permute-start.7 = (f32[16,1,1024]{2,1,0:T(1,128)S(1)}, f32[16,1,1024]{2,1,0:T(1,128)S(1)}, u32[]{:S(2)}, u32[]{:S(2)}) collective-permute-start(f32[16,1,1024]{2,1,0:T(1,128)S(1)} %get-tuple-element.22), channel_id=1, source_target_pairs={{0,1},{1,2},{2,3},{3,4},{4,5},{5,6},{6,7},{7,8},{8,9},{9,10},{10,1... | collective-permute-start | bytes 196616 | tf_op jit(solution)/shard_map/ppermute | solution.py:22
  46.9 0.8 collective-permute-done.7
  47.7 4.9 %multiply_reduce_fusion.2 = (f32[]{:T(128)}, f32[]{:T(128)}, f32[16,32,1024]{2,1,0:T(8,128)}) fusion(f32[16,32,1024]{2,1,0:T(8,128)S(1)} %get-tuple-element.11, f32[16,32,1024]{2,1,0:T(8,128)S(1)} %get-tuple-element.12, f32[16,32,1024]{2,1,0:T(8,128)S(1)} %copy-done.1, f32[32,1024]{1,0:T(8,128)S(1)} %bitcast_add_fusion, ...), kind=kLoop, calls=%fused_computation.74 | loop fusion | flops 14680062 | bytes 15204360 | tf_op jit(solution)/shard_map/reduce_sum | solution.py:72
  52.6 36.2 %all-reduce.6 = (f32[]{:T(128)}, f32[]{:T(128)}) all-reduce(f32[]{:T(128)} %get-tuple-element.3, f32[]{:T(128)} %get-tuple-element.2), channel_id=1, replica_groups=mesh['region'=2,'gx'=16] {'gx'}, use_global_device_ids=true, to_apply=%region_1.2 | all-reduce | flops 2 | bytes 16 | tf_op jit(solution)/shard_map/psum | solution.py:69
  90.1 5.9 %multiply_reduce_fusion.1 = (f32[]{:T(128)}, f32[16,32,1024]{2,1,0:T(8,128)}) fusion(f32[32,1024]{1,0:T(8,128)S(1)} %get-tuple-element.38, f32[16,32,1024]{2,1,0:T(8,128)} %param.8, f32[32,1024]{1,0:T(8,128)S(1)} %bitcast_add_fusion, f32[32,1024]{1,0:T(8,128)S(1)} %broadcast_multiply_fusion, f32[16,32,1024]{2,1,0:T(8,128)} %copy-done.5, ...), kind=kLoop, calls=%fused_computation.72 | loop fusion | flops 7340031 | bytes 8781832 | tf_op jit(solution)/shard_map/reduce_sum | solution.py:77
  96.0 30.3 %psum.30 = f32[]{:T(128)} all-reduce(f32[]{:T(128)} %get-tuple-element.8), channel_id=1, replica_groups=mesh['region'=2,'gx'=16] {'gx'}, use_global_device_ids=true, to_apply=%region_5.6 | all-reduce | flops 1 | bytes 8 | tf_op jit(solution)/shard_map/psum | solution.py:77
  127.6 3.8 %multiply_add_fusion.1 = f32[16,32,1024]{2,1,0:T(8,128)S(1)} fusion(f32[16,32,1024]{2,1,0:T(8,128)} %copy-done.3, f32[]{:T(128)S(6)} %div.18, f32[16,32,1024]{2,1,0:T(8,128)} %get-tuple-element.9, f32[32,1024]{1,0:T(8,128)S(1)} %get-tuple-element.38, f32[16,32,1024]{2,1,0:T(8,128)} %param.8, f32[32,1024]{1,0:T(8,128)S(1)} %bitcast_add_fusion, ...), kind=kLoop, calls=%fused_computation.71 | loop fusion | flops 6291456 | bytes 8781828 | tf_op jit(solution)/shard_map/add | solution.py:78
  131.3 0.1 fusion.48
  131.4 1.3 collective-permute-start.8
  132.7 3.0 %collective-permute-start.9 = (f32[16,1,1024]{2,1,0:T(1,128)S(1)}, f32[16,1,1024]{2,1,0:T(1,128)S(1)}, u32[]{:S(2)}, u32[]{:S(2)}) collective-permute-start(f32[16,1,1024]{2,1,0:T(1,128)S(1)} %get-tuple-element.16), channel_id=1, source_target_pairs={{0,1},{1,2},{2,3},{3,4},{4,5},{5,6},{6,7},{7,8},{8,9},{9,10},{10,1... | collective-permute-start | bytes 196616 | tf_op jit(solution)/shard_map/ppermute | solution.py:22
  135.8 0.5 fusion.50
  136.3 0.3 collective-permute-done.9
  136.7 1.4 fusion.20
  138.1 0.1 fusion.47
  138.2 1.3 collective-permute-start.10
  139.5 4.1 %collective-permute-start.11 = (f32[16,1,1024]{2,1,0:T(1,128)S(1)}, f32[16,1,1024]{2,1,0:T(1,128)S(1)}, u32[]{:S(2)}, u32[]{:S(2)}) collective-permute-start(f32[16,1,1024]{2,1,0:T(1,128)S(1)} %get-tuple-element.14), channel_id=1, source_target_pairs={{0,1},{1,2},{2,3},{3,4},{4,5},{5,6},{6,7},{7,8},{8,9},{9,10},{10,1... | collective-permute-start | bytes 196616 | tf_op jit(solution)/shard_map/ppermute | solution.py:22
  143.6 0.8 collective-permute-done.11
  144.4 4.6 %multiply_reduce_fusion = (f32[]{:T(128)}, f32[16,32,1024]{2,1,0:T(8,128)}) fusion(f32[16,32,1024]{2,1,0:T(8,128)S(1)} %multiply_add_fusion.1, f32[16,32,1024]{2,1,0:T(8,128)S(1)} %copy-done.2, f32[32,1024]{1,0:T(8,128)S(1)} %bitcast_add_fusion, f32[32,1024]{1,0:T(8,128)S(1)} %broadcast_multiply_fusion, f32[1,32,1024]{2,1,0:T(8,128)S(1)} %get-tuple-element.18, ...), kind=kLoop, calls=%fused_computation.70 | loop fusion | flops 13631487 | bytes 13107204 | tf_op jit(solution)/shard_map/reduce_sum | solution.py:72
  149.0 33.0 %psum.31 = f32[]{:T(128)} all-reduce(f32[]{:T(128)} %get-tuple-element.6), channel_id=1, replica_groups=mesh['region'=2,'gx'=16] {'gx'}, use_global_device_ids=true, to_apply=%region_7.8 | all-reduce | flops 1 | bytes 8 | tf_op jit(solution)/shard_map/psum | solution.py:72
  183.2 6.9 %multiply_subtract_fusion = (f32[16,32,1024]{2,1,0:T(8,128)}, f32[16,32,1024]{2,1,0:T(8,128)}) fusion(f32[16,32,1024]{2,1,0:T(8,128)} %get-tuple-element.9, f32[16,32,1024]{2,1,0:T(8,128)} %get-tuple-element.7, f32[]{:T(128)S(6)} %div.19, f32[16,32,1024]{2,1,0:T(8,128)} %copy-done.4, f32[16,32,1024]{2,1,0:T(8,128)} %copy-done.3, f32[]{:T(128)S(6)} %div.17), kind=kLoop, calls=%fused_computation.68 | loop fusion | flops 2621440 | bytes 12582920 | tf_op jit(solution)/shard_map/sub | solution.py:74
  (30 shorter events, 0.2 us)
Async XLA Ops:
  0.6 10.1 %copy-start = (bf16[32,32,1024]{2,1,0:T(8,128)(2,1)S(1)}, bf16[32,32,1024]{2,1,0:T(8,128)(2,1)}, u32[]{:S(2)}) copy-start(bf16[32,32,1024]{2,1,0:T(8,128)(2,1)} %param.13) | copy-start | bytes 6291460
  2.1 16.2 %collective-permute-start = (f32[16,1,1024]{2,1,0:T(1,128)S(1)}, f32[16,1,1024]{2,1,0:T(1,128)S(1)}, u32[]{:S(2)}, u32[]{:S(2)}) collective-permute-start(f32[16,1,1024]{2,1,0:T(1,128)S(1)} %get-tuple-element.31), channel_id=1, source_target_pairs={{1,0},{2,1},{3,2},{4,3},{5,4},{6,5},{7,6},{8,7},{9,8},{10,9},{11,1... | collective-permute-start | bytes 196616 | tf_op jit(solution)/shard_map/ppermute | solution.py:24
  3.4 14.9 %collective-permute-start.1 = (f32[16,1,1024]{2,1,0:T(1,128)S(1)}, f32[16,1,1024]{2,1,0:T(1,128)S(1)}, u32[]{:S(2)}, u32[]{:S(2)}) collective-permute-start(f32[16,1,1024]{2,1,0:T(1,128)S(1)} %get-tuple-element.32), channel_id=1, source_target_pairs={{0,1},{1,2},{2,3},{3,4},{4,5},{5,6},{6,7},{7,8},{8,9},{9,10},{10,1... | collective-permute-start | bytes 196616 | tf_op jit(solution)/shard_map/ppermute | solution.py:22
  7.4 2.5 %copy-start.10 = (f32[8]{0:T(128)S(1)}, f32[8]{0:T(128)}, u32[]{:S(2)}) copy-start(f32[8]{0:T(128)} %param.15) | copy-start | bytes 100
  7.4 3.2 %copy-start.8 = (f32[32,1024]{1,0:T(8,128)S(1)}, f32[32,1024]{1,0:T(8,128)}, u32[]{:S(2)}) copy-start(f32[32,1024]{1,0:T(8,128)} %param.12) | copy-start | bytes 393220
  7.5 3.2 %copy-start.11 = (bf16[32]{0:T(256)(128)(2,1)S(1)}, bf16[32]{0:T(256)(128)(2,1)}, u32[]{:S(2)}) copy-start(bf16[32]{0:T(256)(128)(2,1)} %param.14) | copy-start | bytes 196
  9.9 3.1 %copy-start.9 = (s32[32,1024]{1,0:T(8,128)S(1)}, s32[32,1024]{1,0:T(8,128)}, u32[]{:S(2)}) copy-start(s32[32,1024]{1,0:T(8,128)} %param.11) | copy-start | bytes 393220
  10.0 8.4 %copy-start.1 = (f32[16,32,1024]{2,1,0:T(8,128)S(1)}, f32[16,32,1024]{2,1,0:T(8,128)}, u32[]{:S(2)}) copy-start(f32[16,32,1024]{2,1,0:T(8,128)} %param.8) | copy-start | bytes 6291460
  18.3 7.9 %copy-start.7 = (s32[32,1024]{1,0:T(8,128)S(1)}, s32[32,1024]{1,0:T(8,128)}, u32[]{:S(2)}) copy-start(s32[32,1024]{1,0:T(8,128)} %param.10) | copy-start | bytes 393220
  18.4 8.8 %copy-start.6 = (s32[16,32,1024]{2,1,0:T(8,128)S(1)}, s32[16,32,1024]{2,1,0:T(8,128)}, u32[]{:S(2)}) copy-start(s32[16,32,1024]{2,1,0:T(8,128)} %param.9) | copy-start | bytes 6291460
  19.9 6.5 %collective-permute-start.2 = (f32[16,1,1024]{2,1,0:T(1,128)S(1)}, f32[16,1,1024]{2,1,0:T(1,128)S(1)}, u32[]{:S(2)}, u32[]{:S(2)}) collective-permute-start(f32[16,1,1024]{2,1,0:T(1,128)S(1)} %get-tuple-element.29), channel_id=1, source_target_pairs={{1,0},{2,1},{3,2},{4,3},{5,4},{6,5},{7,6},{8,7},{9,8},{10,9},{11,1... | collective-permute-start | bytes 196616 | tf_op jit(solution)/shard_map/ppermute | solution.py:24
  21.2 6.0 %collective-permute-start.3 = (f32[16,1,1024]{2,1,0:T(1,128)S(1)}, f32[16,1,1024]{2,1,0:T(1,128)S(1)}, u32[]{:S(2)}, u32[]{:S(2)}) collective-permute-start(f32[16,1,1024]{2,1,0:T(1,128)S(1)} %get-tuple-element.30), channel_id=1, source_target_pairs={{0,1},{1,2},{2,3},{3,4},{4,5},{5,6},{6,7},{7,8},{8,9},{9,10},{10,1... | collective-permute-start | bytes 196616 | tf_op jit(solution)/shard_map/ppermute | solution.py:22
  30.5 17.2 %copy-start.3 = (f32[16,32,1024]{2,1,0:T(8,128)}, f32[16,32,1024]{2,1,0:T(8,128)S(1)}, u32[]{:S(2)}) copy-start(f32[16,32,1024]{2,1,0:T(8,128)S(1)} %get-tuple-element.11) | copy-start | bytes 6291460
  30.5 17.2 %copy-start.5 = (f32[16,32,1024]{2,1,0:T(8,128)}, f32[16,32,1024]{2,1,0:T(8,128)S(1)}, u32[]{:S(2)}) copy-start(f32[16,32,1024]{2,1,0:T(8,128)S(1)} %get-tuple-element.12) | copy-start | bytes 6291460
  30.7 7.0 %collective-permute-start.4 = (f32[16,1,1024]{2,1,0:T(1,128)S(1)}, f32[16,1,1024]{2,1,0:T(1,128)S(1)}, u32[]{:S(2)}, u32[]{:S(2)}) collective-permute-start(f32[16,1,1024]{2,1,0:T(1,128)S(1)} %get-tuple-element.23), channel_id=1, source_target_pairs={{1,0},{2,1},{3,2},{4,3},{5,4},{6,5},{7,6},{8,7},{9,8},{10,9},{11,1... | collective-permute-start | bytes 196616 | tf_op jit(solution)/shard_map/ppermute | solution.py:24
  32.0 6.1 %collective-permute-start.5 = (f32[16,1,1024]{2,1,0:T(1,128)S(1)}, f32[16,1,1024]{2,1,0:T(1,128)S(1)}, u32[]{:S(2)}, u32[]{:S(2)}) collective-permute-start(f32[16,1,1024]{2,1,0:T(1,128)S(1)} %get-tuple-element.24), channel_id=1, source_target_pairs={{0,1},{1,2},{2,3},{3,4},{4,5},{5,6},{6,7},{7,8},{8,9},{9,10},{10,1... | collective-permute-start | bytes 196616 | tf_op jit(solution)/shard_map/ppermute | solution.py:22
  39.5 7.4 %collective-permute-start.6 = (f32[16,1,1024]{2,1,0:T(1,128)S(1)}, f32[16,1,1024]{2,1,0:T(1,128)S(1)}, u32[]{:S(2)}, u32[]{:S(2)}) collective-permute-start(f32[16,1,1024]{2,1,0:T(1,128)S(1)} %get-tuple-element.21), channel_id=1, source_target_pairs={{1,0},{2,1},{3,2},{4,3},{5,4},{6,5},{7,6},{8,7},{9,8},{10,9},{11,1... | collective-permute-start | bytes 196616 | tf_op jit(solution)/shard_map/ppermute | solution.py:24
  40.8 6.9 %collective-permute-start.7 = (f32[16,1,1024]{2,1,0:T(1,128)S(1)}, f32[16,1,1024]{2,1,0:T(1,128)S(1)}, u32[]{:S(2)}, u32[]{:S(2)}) collective-permute-start(f32[16,1,1024]{2,1,0:T(1,128)S(1)} %get-tuple-element.22), channel_id=1, source_target_pairs={{0,1},{1,2},{2,3},{3,4},{4,5},{5,6},{6,7},{7,8},{8,9},{9,10},{10,1... | collective-permute-start | bytes 196616 | tf_op jit(solution)/shard_map/ppermute | solution.py:22
  131.3 13.1 %copy-start.4 = (f32[16,32,1024]{2,1,0:T(8,128)}, f32[16,32,1024]{2,1,0:T(8,128)S(1)}, u32[]{:S(2)}) copy-start(f32[16,32,1024]{2,1,0:T(8,128)S(1)} %multiply_add_fusion.1) | copy-start | bytes 6291460
  131.4 4.9 %collective-permute-start.8 = (f32[16,1,1024]{2,1,0:T(1,128)S(1)}, f32[16,1,1024]{2,1,0:T(1,128)S(1)}, u32[]{:S(2)}, u32[]{:S(2)}) collective-permute-start(f32[16,1,1024]{2,1,0:T(1,128)S(1)} %get-tuple-element.15), channel_id=1, source_target_pairs={{1,0},{2,1},{3,2},{4,3},{5,4},{6,5},{7,6},{8,7},{9,8},{10,9},{11,1... | collective-permute-start | bytes 196616 | tf_op jit(solution)/shard_map/ppermute | solution.py:24
  132.7 3.9 %collective-permute-start.9 = (f32[16,1,1024]{2,1,0:T(1,128)S(1)}, f32[16,1,1024]{2,1,0:T(1,128)S(1)}, u32[]{:S(2)}, u32[]{:S(2)}) collective-permute-start(f32[16,1,1024]{2,1,0:T(1,128)S(1)} %get-tuple-element.16), channel_id=1, source_target_pairs={{0,1},{1,2},{2,3},{3,4},{4,5},{5,6},{6,7},{7,8},{8,9},{9,10},{10,1... | collective-permute-start | bytes 196616 | tf_op jit(solution)/shard_map/ppermute | solution.py:22
  136.3 8.1 %copy-start.2 = (f32[16,32,1024]{2,1,0:T(8,128)S(1)}, f32[16,32,1024]{2,1,0:T(8,128)}, u32[]{:S(2)}) copy-start(f32[16,32,1024]{2,1,0:T(8,128)} %param.8) | copy-start | bytes 6291460
  138.2 5.4 %collective-permute-start.10 = (f32[16,1,1024]{2,1,0:T(1,128)S(1)}, f32[16,1,1024]{2,1,0:T(1,128)S(1)}, u32[]{:S(2)}, u32[]{:S(2)}) collective-permute-start(f32[16,1,1024]{2,1,0:T(1,128)S(1)} %get-tuple-element.13), channel_id=1, source_target_pairs={{1,0},{2,1},{3,2},{4,3},{5,4},{6,5},{7,6},{8,7},{9,8},{10,9},{11,1... | collective-permute-start | bytes 196616 | tf_op jit(solution)/shard_map/ppermute | solution.py:24
  139.5 4.9 %collective-permute-start.11 = (f32[16,1,1024]{2,1,0:T(1,128)S(1)}, f32[16,1,1024]{2,1,0:T(1,128)S(1)}, u32[]{:S(2)}, u32[]{:S(2)}) collective-permute-start(f32[16,1,1024]{2,1,0:T(1,128)S(1)} %get-tuple-element.14), channel_id=1, source_target_pairs={{0,1},{1,2},{2,3},{3,4},{4,5},{5,6},{6,7},{7,8},{8,9},{9,10},{10,1... | collective-permute-start | bytes 196616 | tf_op jit(solution)/shard_map/ppermute | solution.py:22
where the time goes:
time: 191 us; the launch traced here: 190 us
  blocking collectives  99.5 us (52%)
  other arithmetic  38.9 us (20%)
  starting transfers between devices  34.2 us (18%)
  local copies, waits for them, and re-layouts  7.21 us (4%)
  between operations  4.86 us (3%)
  waiting for transfers between devices  3.22 us (2%)
  matrix products  2.33 us (1%)
    psum x1, blocking collectives, shards(): product_now = lax.psum(jnp.sum(residual * scaled), 'gx')  36.2 us
    psum x1, blocking collectives, shards(): step_size = product_now / lax.psum(jnp.sum(search * image), 'gx')  33 us
    psum x1, blocking collectives, shards(): product_next = lax.psum(jnp.sum(residual * scaled), 'gx')  30.3 us
    ppermute x6, starting transfers between devices, padded(): lax.ppermute(tail, axis, [(i, (i + 1) % count) for i in range(ends)])  26.4 us
    reduce_sum x2, other arithmetic, shards(): step_size = product_now / lax.psum(jnp.sum(search * image), 'gx')  9.44 us
    ppermute x6, starting transfers between devices, padded(): lax.ppermute(head, axis, [((i + 1) % count, i) for i in range(ends)])  7.75 us
    sub x1, other arithmetic, shards(): residual = residual - step_size * image  6.93 us
    reduce_sum x1, other arithmetic, shards(): product_next = lax.psum(jnp.sum(residual * scaled), 'gx')  5.92 us
  transfers between devices with their start and end apart: 12, of which 5 were waited for; matrix products, arithmetic and copies ran while one was open for 7% of the time, Pallas kernels for 0%

commit v1 on v0

v1 whole, which is shorter than its diff:
```python
import jax
import jax.numpy as jnp
from jax import lax
from jax.sharding import PartitionSpec as P

AX = "gx"
prior_scale = 0.04
time_coupling = 0.5


def swap_halos(head, tail):
    count = lax.axis_size(AX)
    odd = lax.axis_index(AX) % 2 == 1
    first = [(i, i ^ 1) for i in range(count) if (i ^ 1) < count]
    second = [(i, ((i + 1) ^ 1) - 1) for i in range(count) if 0 <= ((i + 1) ^ 1) - 1 < count]
    got_first = lax.ppermute(jnp.where(odd, head, tail), AX, first)
    got_second = lax.ppermute(jnp.where(odd, tail, head), AX, second)
    return jnp.where(odd, got_first, got_second), jnp.where(odd, got_second, got_first)


def all_sum(values):
    count = lax.axis_size(AX)
    if count & (count - 1):
        return lax.psum(values, AX)
    step = 1
    while step < count:
        values = values + lax.ppermute(values, AX, [(i, i ^ step) for i in range(count)])
        step *= 2
    return values


def laplace(field, kappa_rows):
    center = field[1:-1]
    side = jnp.pad(center, ((0, 0), (0, 0), (1, 1)))
    beside = field[2:] + field[:-2] + side[:, :, 2:] + side[:, :, :-2]
    return (kappa_rows + 4.0)[:, None] * center - beside


def temporal(field):
    before = jnp.concatenate([field[:, :1], field[:, :-1]], axis=1)
    after = jnp.concatenate([field[:, 1:], field[:, -1:]], axis=1)
    return 2.0 * field - before - after


def shards(latent, counts, land_mask, region_ids, kappa_sq, covariates, effects, intercepts):
    weeks, rows, cols = latent.shape
    me = lax.axis_index(AX)
    field = jnp.transpose(latent, (1, 0, 2))

    def inside(depth):
        place = lax.broadcasted_iota(jnp.int32, (rows + 2 * depth, 1, 1), 0) - depth + me * rows
        return ((place >= 0) & (place < rows * lax.axis_size(AX))).astype(jnp.float32)

    def pack(wide, flat):
        return jnp.concatenate([wide.reshape(-1, cols)] + flat, axis=0)

    land_own = land_mask.astype(jnp.float32)
    above, below = swap_halos(
        pack(field[:2], [kappa_sq[:3], land_own[:2]]), pack(field[-2:], [kappa_sq[-3:], land_own[-2:]])
    )
    cut = 2 * weeks

    cov_term = jnp.einsum("k,kxy->xy", effects, covariates, preferred_element_type=jnp.float32)
    offset = jnp.zeros(kappa_sq.shape, jnp.float32)
    for zone in range(intercepts.shape[0]):
        offset = offset + jnp.where(region_ids == zone, intercepts[zone], 0.0)
    eta = cov_term + offset

    field = jnp.concatenate([above[:cut].reshape(2, weeks, cols), field, below[:cut].reshape(2, weeks, cols)])
    kappa = jnp.concatenate([above[cut : cut + 3], kappa_sq, below[cut : cut + 3]])
    land = jnp.concatenate([above[cut + 3 :], land_own, below[cut + 3 :]])[:, None]
    image = laplace(laplace(field, kappa[2:-2]) * inside(1), kappa_sq)
    own = field[2:-2]
    curve = jnp.tanh(0.5 * (own + eta[:, None]))
    tally = jnp.transpose(counts, (1, 0, 2)).astype(jnp.float32)
    gradient = land[2:-2] * (tally - 2.0 - 2.0 * curve) - prior_scale * image - time_coupling * temporal(own)
    diag_base = prior_scale * ((kappa + 4.0) ** 2 + 4.0) + 2.0 * time_coupling
    weight = land[2:-2] * (1.0 - curve * curve)
    search = gradient / (diag_base[3:-3, None] + weight)

    above, below = swap_halos(pack(search[:4], [eta[:2]]), pack(search[-4:], [eta[-2:]]))
    cut = 4 * weeks
    search_all = jnp.concatenate([above[:cut].reshape(4, weeks, cols), search, below[:cut].reshape(4, weeks, cols)])
    eta_all = jnp.concatenate([above[cut:], eta, below[cut:]])
    curve = jnp.tanh(0.5 * (field + eta_all[:, None]))
    weight = land * (1.0 - curve * curve)
    image = laplace(laplace(search_all, kappa) * inside(3), kappa[1:-1])
    image = prior_scale * image + time_coupling * temporal(search_all[2:-2]) + weight * search_all[2:-2]
    other = inside(2) * (image / (diag_base[1:-1, None] + weight))
    own_image = image[2:-2]
    own_other = other[2:-2]
    other_image = laplace(laplace(other, kappa[2:-2]) * inside(1), kappa_sq)
    other_image = prior_scale * other_image + time_coupling * temporal(own_other) + weight[2:-2] * own_other

    sums = jnp.stack(
        [
            jnp.sum(gradient * search),
            jnp.sum(search * own_image),
            jnp.sum(own_image * own_other),
            jnp.sum(own_other * other_image),
        ]
    )
    rz, pq, cross, last = all_sum(sums)
    first_step = rz / pq
    rz_next = first_step * first_step * cross - rz
    turn = 1.0 + rz_next / rz
    second_step = rz_next / (turn * (turn * pq - 2.0 * first_step * cross) + first_step * first_step * last)
    along = first_step + second_step * turn
    across = second_step * first_step
    newton = along * search - across * own_other
    residual = gradient - along * own_image + across * other_image
    return jnp.transpose(newton, (1, 0, 2)), jnp.transpose(residual, (1, 0, 2))


def solution(mesh):
    placed = (
        P(None, "gx", "region"),
        P(None, "gx", "region"),
        P("gx", "region"),
        P("gx", "region"),
        P("gx", "region"),
        P(None, "gx", "region"),
        P("region"),
        P("region"),
    )
    return jax.shard_map(
        shards,
        mesh=mesh,
        in_specs=placed,
        out_specs=(P(None, "gx", "region"), P(None, "gx", "region")),
        check_vma=False,
    )
```

time: 191 us -> 108 us (0.57)
  blocking collectives: 99.5 us -> 0 us
  local copies, waits for them, and re-layouts: 7.21 us -> 22.5 us
  starting transfers between devices: 34.2 us -> 22.9 us
  other arithmetic: 38.9 us -> 48.2 us
  waiting for transfers between devices: 3.22 us -> 5.66 us
    psum x3 -> x0, blocking collectives: 99.5 us -> none  [the longest x1 36.2 us: shards(): product_now = lax.psum(jnp.sum(residual * scaled), 'gx')]
    mul x2 -> x4, other arithmetic: 3.38 us -> 15.9 us  [the longest x1 11.6 us: shards(): other = inside(2) * (image / (diag_base[1:-1, None] + weight))]
    unnamed x24 -> x35, local copies, waits for them, and re-layouts: 0.07 us -> 11.7 us
    ppermute x12 -> x8, starting transfers between devices: 34.2 us -> 22.9 us  [the longest x4 17 us: all_sum(): lax.ppermute(values, AX, [(i, i ^ step) for i in range(count)])]
    sub x4 -> x0, other arithmetic: 11.1 us -> none  [the longest x1 6.93 us: shards(): residual = residual - step_size * image]
    reduce_sum x3 -> x1, other arithmetic: 15.4 us -> 5.26 us  [shards(): jnp.sum(search * own_image)]
    div x0 -> x1, other arithmetic: none -> 7.48 us  [shards(): search = gradient / (diag_base[3:-3, None] + weight)]
    transpose x0 -> x1, other arithmetic: none -> 4.96 us  [shards(): jnp.transpose(residual, (1, 0, 2))]
  transfers between devices with their start and end apart: 12 -> 8, of which waited for: 5 -> 5; matrix products, arithmetic and copies ran while one was open for 7% -> 10% of each run, Pallas kernels for 0% -> 0%
where the time goes in v1:
time: 108 us
  other arithmetic  48.2 us (45%)
  starting transfers between devices  22.9 us (21%)
  local copies, waits for them, and re-layouts  22.5 us (21%)
  between operations  6.25 us (6%)
  waiting for transfers between devices  5.66 us (5%)
  matrix products  2.33 us (2%)
    ppermute x4, starting transfers between devices, all_sum(): lax.ppermute(values, AX, [(i, i ^ step) for i in range(count)])  17 us
    unnamed x35, local copies, waits for them, and re-layouts  11.7 us
    mul x1, other arithmetic, shards(): other = inside(2) * (image / (diag_base[1:-1, None] + weight))  11.6 us
    div x1, other arithmetic, shards(): search = gradient / (diag_base[3:-3, None] + weight)  7.48 us
    slice x5, local copies, waits for them, and re-layouts, temporal(): before = jnp.concatenate([field[:, :1], field[:, :-1]], axis=1)  5.8 us
    ppermute x4, waiting for transfers between devices, all_sum(): lax.ppermute(values, AX, [(i, i ^ step) for i in range(count)])  5.38 us
    add x1, other arithmetic, shards(): eta = cov_term + offset  5.28 us
    reduce_sum x1, other arithmetic, shards(): jnp.sum(search * own_image)  5.26 us
  transfers between devices with their start and end apart: 8, of which 5 were waited for; matrix products, arithmetic and copies ran while one was open for 10% of the time, Pallas kernels for 0%

profile of v1, /device:TPU:0, one launch (start us, length us, event | category | flops | bytes accessed | tf_op | source)
XLA Modules:
  0.0 107.9 jit_solution(14158721497396090506)
XLA Ops:
  0.7 0.9 fusion.63
  1.6 0.9 convert_element_type.42
  2.5 2.8 %copy.31 = f32[16,32,1024]{2,0,1:T(8,128)S(1)} copy(f32[16,32,1024]{2,1,0:T(8,128)} %param.8) | data formatting | bytes 4194304 | tf_op args[0]
  5.5 0.5 collective-permute-start
  6.0 0.7 collective-permute-start.1
  6.7 0.2 fusion.59
  6.9 2.4 %fusion.60 = (f32[32,15,1024]{2,1,0:T(8,128)}, f32[32,15,1024]{2,1,0:T(8,128)}) fusion(f32[32,16,1024]{2,1,0:T(8,128)S(1)} %bitcast.50), kind=kLoop, calls=%fused_computation.120 | loop fusion | bytes 7864320 | tf_op jit(solution)/shard_map/slice | solution.py:40
  9.3 0.7 fusion.66
  10.0 2.3 %fusion.44 = f32[1,32,1024]{2,0,1:T(1,128)S(1)} fusion(bf16[32,32,1024]{2,1,0:T(8,128)(2,1)S(1)} %copy-done, bf16[32]{0:T(256)(128)(2,1)S(1)} %copy-done.15), kind=kOutput, calls=%fused_computation.76 | convolution fusion | flops 2097152 | bytes 2228288 | tf_op jit(solution)/shard_map/k,kxy->xy/dot_general | solution.py:63
  12.4 5.3 %bitcast_add_fusion = f32[32,1024]{1,0:T(8,128)S(1)} fusion(f32[1,32,1024]{2,0,1:T(1,128)S(1)} %fusion.44, s32[32,1024]{1,0:T(8,128)S(1)} %copy-done.13, f32[]{:T(128)} %bitcast.11, f32[]{:T(128)} %bitcast.10, f32[]{:T(128)} %bitcast.9, f32[]{:T(128)} %bitcast.8, f32[]{:T(128)} %bitcast.7, f32[]{:T(128)} %bitcast.6, f32[]{:T(128)} %bitcast.5, f32[]{:T(128)} %bitcast.4), kind=kLoop, calls=%fused_computation.103 | loop fusion | flops 786432 | bytes 393248 | tf_op jit(solution)/shard_map/add | solution.py:67
  17.9 0.2 pad_maximum_fusion.1
  18.1 0.1 slice.330
  18.3 1.4 %fusion.22 = f32[34,16,1024]{2,1,0:T(8,128)S(1)} fusion(f32[34,16,1024]{2,1,0:T(8,128)S(1)} %slice.330, f32[2,16,1024]{2,1,0:T(8,128)S(1)} %bitcast.62, f32[32,16,1024]{2,1,0:T(8,128)S(1)} %bitcast.52, f32[2,16,1024]{2,1,0:T(8,128)S(1)} %bitcast.59, f32[34]{0:T(128)S(1)} %and_convert_fusion.2, f32[34,1024]{1,0:T(8,128)S(1)} %slice_add_fusion.6), kind=kLoop, calls=%fused_computation.46 | loop fusion | flops 4456448 | bytes 6955144 | tf_op jit(solution)/shard_map/mul | solution.py:72
  19.9 0.6 copy-done.11
  20.5 1.0 copy-done.8
  21.5 0.6 copy-done.9
  22.1 7.5 %add_divide_fusion = (f32[32,16,1024]{2,1,0:T(8,128)S(1)}, f32[32,16,1024]{2,1,0:T(8,128)S(1)}) fusion(f32[32,1024]{1,0:T(8,128)S(1)} %slice.338, f32[32,1024]{1,0:T(8,128)S(1)} %bitcast_add_fusion, f32[32,1024]{1,0:T(8,128)S(1)} %convert_element_type.42, f32[16,32,1024]{2,1,0:T(8,128)S(1)} %copy-done.8, f32[32,1,1024]{2,1,0:T(1,128)S(1)} %get-tuple-element.23, ...), kind=kLoop, calls=%fused_computation.87 | loop fusion | flops 13631488 | bytes 19398656 | tf_op jit(solution)/shard_map/div | solution.py:79
  29.7 3.9 %collective-permute-start.2 = (f32[66,1024]{1,0:T(8,128)S(1)}, f32[66,1024]{1,0:T(8,128)S(1)}, u32[]{:S(2)}, u32[]{:S(2)}) collective-permute-start(f32[66,1024]{1,0:T(8,128)S(1)} %get-tuple-element.30), channel_id=1, source_target_pairs={{0,1},{1,0},{2,3},{3,2},{4,5},{5,4},{6,7},{7,6},{8,9},{9,8},{10,11... | collective-permute-start | bytes 811016 | tf_op jit(solution)/shard_map/ppermute | solution.py:16
  33.6 0.8 collective-permute-start.3
  34.6 0.3 collective-permute-done.2
  35.0 0.3 pad_maximum_fusion
  35.3 0.2 slice.346
  35.5 2.6 %fusion.55 = (f32[36,15,1024]{2,1,0:T(8,128)}, f32[36,15,1024]{2,1,0:T(8,128)}) fusion(f32[40,16,1024]{2,1,0:T(8,128)S(1)} %pad_maximum_fusion), kind=kLoop, calls=%fused_computation.115 | loop fusion | bytes 8847360 | tf_op jit(solution)/shard_map/slice | solution.py:40
  38.1 1.6 %fusion.3 = f32[38,16,1024]{2,1,0:T(8,128)S(1)} fusion(f32[38,16,1024]{2,1,0:T(8,128)S(1)} %slice.346, f32[40,16,1024]{2,1,0:T(8,128)S(1)} %pad_maximum_fusion, f32[38]{0:T(128)S(1)} %and_convert_fusion.1, f32[38,1024]{1,0:T(8,128)S(1)} %get-tuple-element.36), kind=kLoop, calls=%fused_computation.16 | loop fusion | flops 3735552 | bytes 10117272 | tf_op jit(solution)/shard_map/mul | solution.py:87
  39.6 1.8 %slice.349 = f32[36,16,1024]{2,1,0:T(8,128)} slice(f32[38,16,1024]{2,1,0:T(8,128)S(1)} %fusion.3), slice={[1:37], [0:16], [0:1024]} | slice | bytes 4718592 | tf_op jit(solution)/shard_map/slice | solution.py:33
  41.4 11.6 %divide_multiply_fusion = (f32[36,16,1024]{2,1,0:T(8,128)S(1)}, f32[36,16,1024]{2,1,0:T(8,128)}, f32[36,16,1024]{2,1,0:T(8,128)}) fusion(f32[36,1024]{1,0:T(8,128)S(1)} %slice.360, f32[36]{0:T(128)S(1)} %and_convert_fusion, f32[36,15,1024]{2,1,0:T(8,128)} %get-tuple-element.15, f32[36,15,1024]{2,1,0:T(8,128)} %get-tuple-element.14, ...), kind=kLoop, calls=%fused_computation.37 | loop fusion | flops 21823488 | bytes 26509456 | tf_op jit(solution)/shard_map/mul | solution.py:89
  53.0 0.2 fusion.56
  53.2 0.1 slice.362
  53.3 0.4 fusion.57
  53.8 1.4 %fusion.26 = f32[34,16,1024]{2,1,0:T(8,128)S(1)} fusion(f32[34,16,1024]{2,1,0:T(8,128)S(1)} %slice.362, f32[36,16,1024]{2,1,0:T(8,128)S(1)} %get-tuple-element.9, f32[34]{0:T(128)S(1)} %and_convert_fusion.2, f32[34,1024]{1,0:T(8,128)S(1)} %slice_add_fusion.6), kind=kLoop, calls=%fused_computation.50 | loop fusion | flops 3342336 | bytes 9052296 | tf_op jit(solution)/shard_map/mul | solution.py:92
  55.2 0.2 slice.365
  55.4 1.4 %copy-done.6 = f32[36,16,1024]{2,1,0:T(8,128)S(1)} copy-done((f32[36,16,1024]{2,1,0:T(8,128)S(1)}, f32[36,16,1024]{2,1,0:T(8,128)}, u32[]{:S(2)}) %copy-start.6) | copy-done | bytes 2359320
  56.9 5.3 %multiply_reduce_fusion.2 = (f32[]{:T(128)}, f32[]{:T(128)}, f32[]{:T(128)}, f32[]{:T(128)}, f32[32,16,1024]{2,1,0:T(8,128)}) fusion(f32[32,16,1024]{2,1,0:T(8,128)S(1)} %get-tuple-element.12, f32[36,16,1024]{2,1,0:T(8,128)S(1)} %copy-done.6, f32[36,16,1024]{2,1,0:T(8,128)S(1)} %get-tuple-element.9, f32[32,16,1024]{2,1,0:T(8,128)S(1)} %get-tuple-element.13, ...), kind=kLoop, calls=%fused_computation.85 | loop fusion | flops 12058620 | bytes 23199760 | tf_op jit(solution)/shard_map/reduce_sum | solution.py:98
  62.1 2.5 %pad_maximum_fusion.9 = f32[4]{0:T(128)S(1)} fusion(f32[1]{0:T(128)} %bitcast.23, f32[1]{0:T(128)} %bitcast.22, f32[1]{0:T(128)} %bitcast.21, f32[1]{0:T(128)} %bitcast.16), kind=kLoop, calls=%fused_computation.113 | loop fusion | flops 12 | bytes 32 | tf_op jit(solution)/shard_map/stack | solution.py:95
  64.7 9.2 %collective-permute-start.4 = (f32[4]{0:T(128)S(1)}, f32[4]{0:T(128)S(1)}, u32[]{:S(2)}, u32[]{:S(2)}) collective-permute-start(f32[4]{0:T(128)S(1)} %pad_maximum_fusion.9), channel_id=1, source_target_pairs={{0,1},{1,0},{2,3},{3,2},{4,5},{5,4},{6,7},{7,6},{8,9},{9,8},{10,11... | collective-permute-start | bytes 56 | tf_op jit(solution)/shard_map/ppermute | solution.py:27
  73.8 0.8 collective-permute-done.4
  74.7 2.5 %fusion.67 = f32[4]{0:T(128)S(1)} fusion(f32[4]{0:T(128)S(1)} %collective-permute-done.4, f32[1]{0:T(128)} %bitcast.23, f32[1]{0:T(128)} %bitcast.22, f32[1]{0:T(128)} %bitcast.21, f32[1]{0:T(128)} %bitcast.16), kind=kLoop, calls=%fused_computation.127 | loop fusion | flops 16 | bytes 48 | tf_op jit(solution)/shard_map/add | solution.py:27
  77.2 2.7 %collective-permute-start.5 = (f32[4]{0:T(128)S(1)}, f32[4]{0:T(128)S(1)}, u32[]{:S(2)}, u32[]{:S(2)}) collective-permute-start(f32[4]{0:T(128)S(1)} %fusion.67), channel_id=1, source_target_pairs={{0,2},{1,3},{2,0},{3,1},{4,6},{5,7},{6,4},{7,5},{8,10},{9,11},{10,... | collective-permute-start | bytes 56 | tf_op jit(solution)/shard_map/ppermute | solution.py:27
  79.9 1.5 %collective-permute-done.5 = f32[4]{0:T(128)S(1)} collective-permute-done((f32[4]{0:T(128)S(1)}, f32[4]{0:T(128)S(1)}, u32[]{:S(2)}, u32[]{:S(2)}) %collective-permute-start.5) | collective-permute-done | bytes 48 | tf_op jit(solution)/shard_map/ppermute | solution.py:27
  81.4 2.5 %fusion.68 = f32[4]{0:T(128)S(1)} fusion(f32[4]{0:T(128)S(1)} %collective-permute-done.5, f32[4]{0:T(128)S(1)} %collective-permute-done.4, f32[1]{0:T(128)} %bitcast.23, f32[1]{0:T(128)} %bitcast.22, f32[1]{0:T(128)} %bitcast.21, f32[1]{0:T(128)} %bitcast.16), kind=kLoop, calls=%fused_computation.128 | loop fusion | flops 20 | bytes 64 | tf_op jit(solution)/shard_map/add | solution.py:27
  83.9 2.1 %collective-permute-start.6 = (f32[4]{0:T(128)S(1)}, f32[4]{0:T(128)S(1)}, u32[]{:S(2)}, u32[]{:S(2)}) collective-permute-start(f32[4]{0:T(128)S(1)} %fusion.68), channel_id=1, source_target_pairs={{0,4},{1,5},{2,6},{3,7},{4,0},{5,1},{6,2},{7,3},{8,12},{9,13},{10,... | collective-permute-start | bytes 56 | tf_op jit(solution)/shard_map/ppermute | solution.py:27
  86.0 1.5 %collective-permute-done.6 = f32[4]{0:T(128)S(1)} collective-permute-done((f32[4]{0:T(128)S(1)}, f32[4]{0:T(128)S(1)}, u32[]{:S(2)}, u32[]{:S(2)}) %collective-permute-start.6) | collective-permute-done | bytes 48 | tf_op jit(solution)/shard_map/ppermute | solution.py:27
  87.5 3.0 %collective-permute-start.7 = (f32[4]{0:T(128)S(1)}, f32[4]{0:T(128)S(1)}, u32[]{:S(2)}, u32[]{:S(2)}) collective-permute-start(f32[4]{0:T(128)S(1)} %add.304), channel_id=1, source_target_pairs={{0,8},{1,9},{2,10},{3,11},{4,12},{5,13},{6,14},{7,15},{8,0},{9,1},... | collective-permute-start | bytes 56 | tf_op jit(solution)/shard_map/ppermute | solution.py:27
  90.6 1.5 %collective-permute-done.7 = f32[4]{0:T(128)S(1)} collective-permute-done((f32[4]{0:T(128)S(1)}, f32[4]{0:T(128)S(1)}, u32[]{:S(2)}, u32[]{:S(2)}) %collective-permute-start.7) | collective-permute-done | bytes 48 | tf_op jit(solution)/shard_map/ppermute | solution.py:27
  92.1 0.7 fusion.65
  97.8 5.0 %add_bitcast_fusion = (f32[16,32,1024]{2,0,1:T(8,128)S(1)}, f32[16,32,1024]{2,0,1:T(8,128)S(1)}) fusion(f32[32,16,1024]{2,1,0:T(8,128)} %get-tuple-element.8, f32[32,16,1024]{2,1,0:T(8,128)} %copy-done.5, f32[36,16,1024]{2,1,0:T(8,128)} %get-tuple-element.10, f32[]{:T(128)S(6)} %mul.279, f32[]{:T(128)S(6)} %add.308, ...), kind=kLoop, calls=%fused_computation.81 | loop fusion | flops 3670016 | bytes 14680072 | tf_op jit(solution)/shard_map/transpose | solution.py:112
  102.8 2.5 %copy.13 = f32[16,32,1024]{2,1,0:T(8,128)} copy(f32[16,32,1024]{2,0,1:T(8,128)S(1)} %get-tuple-element.57) | data formatting | bytes 4194304
  105.3 2.5 %copy.12 = f32[16,32,1024]{2,1,0:T(8,128)} copy(f32[16,32,1024]{2,0,1:T(8,128)S(1)} %get-tuple-element.58) | data formatting | bytes 4194304
  (63 shorter events, 0.8 us)
Async XLA Ops:
  0.6 9.4 %copy-start = (bf16[32,32,1024]{2,1,0:T(8,128)(2,1)S(1)}, bf16[32,32,1024]{2,1,0:T(8,128)(2,1)}, u32[]{:S(2)}) copy-start(bf16[32,32,1024]{2,1,0:T(8,128)(2,1)} %param.13) | copy-start | bytes 6291460
  2.5 4.1 %copy-start.12 = (f32[32,1024]{1,0:T(8,128)S(1)}, f32[32,1024]{1,0:T(8,128)}, u32[]{:S(2)}) copy-start(f32[32,1024]{1,0:T(8,128)} %param.12) | copy-start | bytes 393220
  5.4 1.5 %copy-start.2 = (f32[16,32,1024]{2,0,1:T(8,128)}, f32[16,32,1024]{2,0,1:T(8,128)S(1)}, u32[]{:S(2)}) copy-start(f32[16,32,1024]{2,0,1:T(8,128)S(1)} %copy.31) | copy-start | bytes 6291460
  5.5 12.2 %collective-permute-start = (f32[37,1024]{1,0:T(8,128)S(1)}, f32[37,1024]{1,0:T(8,128)S(1)}, u32[]{:S(2)}, u32[]{:S(2)}) collective-permute-start(f32[37,1024]{1,0:T(8,128)S(1)} %get-tuple-element.34), channel_id=1, source_target_pairs={{0,1},{1,0},{2,3},{3,2},{4,5},{5,4},{6,7},{7,6},{8,9},{9,8},{10,11... | collective-permute-start | bytes 454664 | tf_op jit(solution)/shard_map/ppermute | solution.py:16
  6.0 11.7 %collective-permute-start.1 = (f32[37,1024]{1,0:T(8,128)S(1)}, f32[37,1024]{1,0:T(8,128)S(1)}, u32[]{:S(2)}, u32[]{:S(2)}) collective-permute-start(f32[37,1024]{1,0:T(8,128)S(1)} %get-tuple-element.35), channel_id=1, source_target_pairs={{1,2},{2,1},{3,4},{4,3},{5,6},{6,5},{7,8},{8,7},{9,10},{10,9},{11,... | collective-permute-start | bytes 454664 | tf_op jit(solution)/shard_map/ppermute | solution.py:17
  6.9 2.4 %copy-start.14 = (f32[8]{0:T(128)S(1)}, f32[8]{0:T(128)}, u32[]{:S(2)}) copy-start(f32[8]{0:T(128)} %param.15) | copy-start | bytes 100
  6.9 3.1 %copy-start.15 = (bf16[32]{0:T(256)(128)(2,1)S(1)}, bf16[32]{0:T(256)(128)(2,1)}, u32[]{:S(2)}) copy-start(bf16[32]{0:T(256)(128)(2,1)} %param.14) | copy-start | bytes 196
  9.3 3.0 %copy-start.13 = (s32[32,1024]{1,0:T(8,128)S(1)}, s32[32,1024]{1,0:T(8,128)}, u32[]{:S(2)}) copy-start(s32[32,1024]{1,0:T(8,128)} %param.11) | copy-start | bytes 393220
  10.0 7.9 %copy-start.3 = (f32[16,32,1024]{2,0,1:T(8,128)S(1)}, f32[16,32,1024]{2,0,1:T(8,128)}, u32[]{:S(2)}) copy-start(f32[16,32,1024]{2,0,1:T(8,128)} %copy-done.2) | copy-start | bytes 6291460
  18.3 1.6 %copy-start.10 = (f32[32,15,1024]{2,1,0:T(8,128)S(1)}, f32[32,15,1024]{2,1,0:T(8,128)}, u32[]{:S(2)}) copy-start(f32[32,15,1024]{2,1,0:T(8,128)} %get-tuple-element.25) | copy-start | bytes 5898244
  18.3 2.2 %copy-start.11 = (s32[16,32,1024]{2,1,0:T(8,128)S(1)}, s32[16,32,1024]{2,1,0:T(8,128)}, u32[]{:S(2)}) copy-start(s32[16,32,1024]{2,1,0:T(8,128)} %param.9) | copy-start | bytes 6291460
  19.7 1.8 %copy-start.8 = (f32[16,32,1024]{2,1,0:T(8,128)S(1)}, f32[16,32,1024]{2,1,0:T(8,128)}, u32[]{:S(2)}) copy-start(f32[16,32,1024]{2,1,0:T(8,128)} %param.8) | copy-start | bytes 6291460
  19.7 2.4 %copy-start.9 = (f32[32,15,1024]{2,1,0:T(8,128)S(1)}, f32[32,15,1024]{2,1,0:T(8,128)}, u32[]{:S(2)}) copy-start(f32[32,15,1024]{2,1,0:T(8,128)} %get-tuple-element.24) | copy-start | bytes 5898244
  29.6 25.9 %copy-start.4 = (f32[32,16,1024]{2,1,0:T(8,128)}, f32[32,16,1024]{2,1,0:T(8,128)S(1)}, u32[]{:S(2)}) copy-start(f32[32,16,1024]{2,1,0:T(8,128)S(1)} %get-tuple-element.12) | copy-start | bytes 6291460
  29.6 25.9 %copy-start.5 = (f32[32,16,1024]{2,1,0:T(8,128)}, f32[32,16,1024]{2,1,0:T(8,128)S(1)}, u32[]{:S(2)}) copy-start(f32[32,16,1024]{2,1,0:T(8,128)S(1)} %get-tuple-element.13) | copy-start | bytes 6291460
  29.7 5.1 %collective-permute-start.2 = (f32[66,1024]{1,0:T(8,128)S(1)}, f32[66,1024]{1,0:T(8,128)S(1)}, u32[]{:S(2)}, u32[]{:S(2)}) collective-permute-start(f32[66,1024]{1,0:T(8,128)S(1)} %get-tuple-element.30), channel_id=1, source_target_pairs={{0,1},{1,0},{2,3},{3,2},{4,5},{5,4},{6,7},{7,6},{8,9},{9,8},{10,11... | collective-permute-start | bytes 811016 | tf_op jit(solution)/shard_map/ppermute | solution.py:16
  33.6 1.2 %collective-permute-start.3 = (f32[66,1024]{1,0:T(8,128)S(1)}, f32[66,1024]{1,0:T(8,128)S(1)}, u32[]{:S(2)}, u32[]{:S(2)}) collective-permute-start(f32[66,1024]{1,0:T(8,128)S(1)} %get-tuple-element.31), channel_id=1, source_target_pairs={{1,2},{2,1},{3,4},{4,3},{5,6},{6,5},{7,8},{8,7},{9,10},{10,9},{11,... | collective-permute-start | bytes 811016 | tf_op jit(solution)/shard_map/ppermute | solution.py:17
  53.7 1.7 %copy-start.7 = (f32[36,16,1024]{2,1,0:T(8,128)S(1)}, f32[36,16,1024]{2,1,0:T(8,128)}, u32[]{:S(2)}) copy-start(f32[36,16,1024]{2,1,0:T(8,128)} %get-tuple-element.11) | copy-start | bytes 7077892
  55.1 1.7 %copy-start.6 = (f32[36,16,1024]{2,1,0:T(8,128)S(1)}, f32[36,16,1024]{2,1,0:T(8,128)}, u32[]{:S(2)}) copy-start(f32[36,16,1024]{2,1,0:T(8,128)} %get-tuple-element.10) | copy-start | bytes 7077892
  64.7 10.0 %collective-permute-start.4 = (f32[4]{0:T(128)S(1)}, f32[4]{0:T(128)S(1)}, u32[]{:S(2)}, u32[]{:S(2)}) collective-permute-start(f32[4]{0:T(128)S(1)} %pad_maximum_fusion.9), channel_id=1, source_target_pairs={{0,1},{1,0},{2,3},{3,2},{4,5},{5,4},{6,7},{7,6},{8,9},{9,8},{10,11... | collective-permute-start | bytes 56 | tf_op jit(solution)/shard_map/ppermute | solution.py:27
  77.2 4.2 %collective-permute-start.5 = (f32[4]{0:T(128)S(1)}, f32[4]{0:T(128)S(1)}, u32[]{:S(2)}, u32[]{:S(2)}) collective-permute-start(f32[4]{0:T(128)S(1)} %fusion.67), channel_id=1, source_target_pairs={{0,2},{1,3},{2,0},{3,1},{4,6},{5,7},{6,4},{7,5},{8,10},{9,11},{10,... | collective-permute-start | bytes 56 | tf_op jit(solution)/shard_map/ppermute | solution.py:27
  83.9 3.6 %collective-permute-start.6 = (f32[4]{0:T(128)S(1)}, f32[4]{0:T(128)S(1)}, u32[]{:S(2)}, u32[]{:S(2)}) collective-permute-start(f32[4]{0:T(128)S(1)} %fusion.68), channel_id=1, source_target_pairs={{0,4},{1,5},{2,6},{3,7},{4,0},{5,1},{6,2},{7,3},{8,12},{9,13},{10,... | collective-permute-start | bytes 56 | tf_op jit(solution)/shard_map/ppermute | solution.py:27
  87.5 4.6 %collective-permute-start.7 = (f32[4]{0:T(128)S(1)}, f32[4]{0:T(128)S(1)}, u32[]{:S(2)}, u32[]{:S(2)}) collective-permute-start(f32[4]{0:T(128)S(1)} %add.304), channel_id=1, source_target_pairs={{0,8},{1,9},{2,10},{3,11},{4,12},{5,13},{6,14},{7,15},{8,0},{9,1},... | collective-permute-start | bytes 56 | tf_op jit(solution)/shard_map/ppermute | solution.py:27
  102.8 5.1 %copy-start.1 = (bf16[32,32,1024]{2,1,0:T(8,128)(2,1)S(1)}, bf16[32,32,1024]{2,1,0:T(8,128)(2,1)}, u32[]{:S(2)}) copy-start(bf16[32,32,1024]{2,1,0:T(8,128)(2,1)} %param.13) | copy-start | bytes 6291460

commit v2 on v1

v2 whole, which is shorter than its diff:
```python
import functools

import jax
import jax.numpy as jnp
from jax import lax
from jax.experimental import pallas as pl
from jax.experimental.pallas import tpu as pltpu
from jax.sharding import PartitionSpec as P

AX = "gx"
LANES = 128
prior_scale = 0.04
time_coupling = 0.5
F32 = jnp.float32
VMEM = pltpu.VMEM
MIB = 1 << 20


def swap_halos(head, tail):
    count = lax.axis_size(AX)
    odd = lax.axis_index(AX) % 2 == 1
    first = [(i, i ^ 1) for i in range(count) if (i ^ 1) < count]
    second = [(i, ((i + 1) ^ 1) - 1) for i in range(count) if 0 <= ((i + 1) ^ 1) - 1 < count]
    got_first = lax.ppermute(jnp.where(odd, head, tail), AX, first)
    got_second = lax.ppermute(jnp.where(odd, tail, head), AX, second)
    return jnp.where(odd, got_first, got_second), jnp.where(odd, got_second, got_first)


def all_sum(values):
    count = lax.axis_size(AX)
    if count & (count - 1):
        return lax.psum(values, AX)
    step = 1
    while step < count:
        values = values + lax.ppermute(values, AX, [(i, i ^ step) for i in range(count)])
        step *= 2
    return values


def row_of(ref, row):
    return [ref[row, :, c : c + LANES] for c in range(0, ref.shape[2], LANES)]


def put_row(ref, row, tiles):
    for j, tile in enumerate(tiles):
        ref[row, :, j * LANES : (j + 1) * LANES] = tile


def map_row(ref, row):
    return [ref[row, :, c : c + LANES] for c in range(0, ref.shape[2], LANES)]


def masks(weeks):
    lane = lax.broadcasted_iota(jnp.int32, (weeks, LANES), 1)
    week = lax.broadcasted_iota(jnp.int32, (weeks, LANES), 0)
    return lane == 0, lane == LANES - 1, week == 0, week == weeks - 1


def laplace_row(up, mid, down, kappa, mask):
    first, last = mask[0], mask[1]
    count = len(mid)
    to_right = [pltpu.roll(t, 1, 1) for t in mid]
    to_left = [pltpu.roll(t, LANES - 1, 1) for t in mid]
    out = []
    for j in range(count):
        west = jnp.where(first, to_right[j - 1] if j > 0 else 0.0, to_right[j])
        east = jnp.where(last, to_left[j + 1] if j + 1 < count else 0.0, to_left[j])
        out.append((kappa[j] + 4.0) * mid[j] - ((up[j] + down[j]) + (west + east)))
    return out


def temporal_tile(tile, mask):
    weeks = tile.shape[0]
    before = jnp.where(mask[2], tile, pltpu.roll(tile, 1, 0))
    after = jnp.where(mask[3], tile, pltpu.roll(tile, weeks - 1, 0))
    return (2.0 * tile - before) - after


def fold(tiles):
    parts = [t[h : h + 8] for t in tiles for h in range(0, t.shape[0], 8)]
    while len(parts) > 1:
        parts = [a + b for a, b in zip(parts[::2], parts[1::2])] + ([parts[-1]] if len(parts) % 2 else [])
    return parts[0]


def diag_base(kappa):
    return prior_scale * ((kappa + 4.0) * (kappa + 4.0) + 4.0) + 2.0 * time_coupling


def start_kernel(effects, intercepts, latent, counts, covariates, land, zones, kappa,
                 field, grad, weight, inv, search, image, eta,
                 tally, covs, field_sem, tally_sem, cov_sem):
    weeks, rows, cols = latent.shape
    num_covs = covariates.shape[0]
    mask = masks(weeks)

    def field_copy(r):
        return pltpu.make_async_copy(latent.at[:, r, :], field.at[r + 2], field_sem.at[r])

    def tally_copy(r):
        return pltpu.make_async_copy(counts.at[:, r, :], tally.at[r], tally_sem.at[r])

    cov_copy = pltpu.make_async_copy(covariates, covs, cov_sem)
    for r in range(rows):
        field_copy(r).start()
    cov_copy.start()
    for r in range(rows):
        tally_copy(r).start()
    field_copy(0).wait()
    field_copy(1).wait()

    @pl.loop(1, rows - 1)
    def _(r):
        field_copy(r + 1).wait()
        put_row(image, r + 1, laplace_row(
            row_of(field, r + 1), row_of(field, r + 2), row_of(field, r + 3), map_row(kappa, r), mask))

    cov_copy.wait()
    width = 2 * LANES
    for c in range(0, cols, width):
        total = jnp.zeros((rows, width), F32)
        ids = zones[:, c : c + width]
        for z in range(intercepts.shape[0]):
            total = jnp.where(ids == z, intercepts[z], total)
        for k in range(num_covs):
            total = total + effects[k] * covs[k, :, c : c + width].astype(F32)
        for r in range(rows):
            eta[r, :, c : c + width] = total[r : r + 1]

    def pointwise(r):
        tally_copy(r).wait()
        lat, eta_row, land_row, kap, count_row = (
            row_of(field, r + 2), map_row(eta, r), map_row(land, r), map_row(kappa, r), row_of(tally, r))
        out, heavy, inverse = [], [], []
        for j, tile in enumerate(lat):
            on = land_row[j]
            curve = jnp.tanh(0.5 * (tile + eta_row[j]))
            heavy.append(on * (1.0 - curve * curve))
            inverse.append(1.0 / (diag_base(kap[j]) + heavy[j]))
            out.append(on * (count_row[j].astype(F32) - 2.0 - 2.0 * curve) - time_coupling * temporal_tile(tile, mask))
        put_row(weight, r + 2, heavy)
        put_row(inv, r + 2, inverse)
        return out, inverse, kap

    @pl.loop(0, 4)
    def _(i):
        r = jnp.where(i < 2, i, rows - 4 + i)
        put_row(grad, r, pointwise(r)[0])

    @pl.loop(2, rows - 2)
    def _(r):
        out, inverse, kap = pointwise(r)
        outer = laplace_row(row_of(image, r), row_of(image, r + 1), row_of(image, r + 2), kap, mask)
        out = [a - prior_scale * b for a, b in zip(out, outer)]
        put_row(grad, r, out)
        put_row(search, r + 4, [a * b for a, b in zip(out, inverse)])


def scale_of(r, rows, inside):
    return jnp.where(r < 0, inside[0], jnp.where(r >= rows, inside[1], 1.0))


def put_halo(ref, row, packed, at, weeks):
    for c in range(0, packed.shape[1], LANES):
        ref[row, :, c : c + LANES] = packed[at : at + weeks, c : c + LANES]


def edge_kernel(inside, above, below, kappa, eta, inv, field_in, grad_in, search_in, image_in,
                field, grad, search, image, head, tail):
    weeks = field.shape[1]
    rows, _, cols = eta.shape
    mask = masks(weeks)
    for d in range(2):
        put_halo(field, d, above, d * weeks, weeks)
        put_halo(field, rows + 2 + d, below, d * weeks, weeks)

    @pl.loop(0, 4)
    def _(i):
        r = jnp.where(i < 2, i - 1, rows - 3 + i)
        keep = scale_of(r, rows, inside)
        out = laplace_row(row_of(field, r + 1), row_of(field, r + 2), row_of(field, r + 3), map_row(kappa, r + 3), mask)
        put_row(image, r + 1, [keep * t for t in out])

    @pl.loop(0, 4)
    def _(i):
        r = jnp.where(i < 2, i, rows - 4 + i)
        outer = laplace_row(row_of(image, r), row_of(image, r + 1), row_of(image, r + 2), map_row(kappa, r + 3), mask)
        out = [a - prior_scale * b for a, b in zip(row_of(grad, r), outer)]
        put_row(grad, r, out)
        put_row(search, r + 4, [a * b for a, b in zip(out, row_of(inv, r + 2))])

    for d in range(4):
        for c in range(0, cols, LANES):
            head[d * weeks : (d + 1) * weeks, c : c + LANES] = search[4 + d, :, c : c + LANES]
            tail[d * weeks : (d + 1) * weeks, c : c + LANES] = search[rows + d, :, c : c + LANES]
    for d in range(2):
        head[4 * weeks + d : 4 * weeks + d + 1, :] = eta[d]
        tail[4 * weeks + d : 4 * weeks + d + 1, :] = eta[rows - 2 + d]


def hessian_row(r, source, at, image, kappa, weight, mask):
    outer = laplace_row(image(r - 1), image(r), image(r + 1), map_row(kappa, r + 3), mask)
    mid = row_of(source, at)
    heavy = row_of(weight, r + 2)
    return mid, [
        prior_scale * o + (time_coupling * temporal_tile(m, mask) + h * m) for o, m, h in zip(outer, mid, heavy)
    ]


def inner_kernel(kappa, grad, weight, inv, search, first, image, second, second_image, last, sums):
    weeks = grad.shape[1]
    rows = grad.shape[0]
    mask = masks(weeks)

    @pl.loop(1, rows - 1)
    def _(r):
        put_row(first, r + 3, laplace_row(
            row_of(search, r + 3), row_of(search, r + 4), row_of(search, r + 5), map_row(kappa, r + 3), mask))

    zero = jnp.zeros((8, LANES), F32)

    def apply(r, carry):
        rz, pq, cross = carry
        mid, out = hessian_row(r, search, r + 4, lambda q: row_of(first, q + 3), kappa, weight, mask)
        other = [a * b for a, b in zip(out, row_of(inv, r + 2))]
        put_row(image, r, out)
        put_row(second, r + 2, other)
        return (
            rz + fold([a * b for a, b in zip(mid, row_of(grad, r))]),
            pq + fold([a * b for a, b in zip(mid, out)]),
            cross + fold([a * b for a, b in zip(other, out)]),
        )

    rz, pq, cross = lax.fori_loop(2, rows - 2, apply, (zero, zero, zero))

    @pl.loop(3, rows - 3)
    def _(r):
        put_row(second_image, r + 1, laplace_row(
            row_of(second, r + 1), row_of(second, r + 2), row_of(second, r + 3), map_row(kappa, r + 3), mask))

    def apply_second(r, total):
        mid, out = hessian_row(r, second, r + 2, lambda q: row_of(second_image, q + 1), kappa, weight, mask)
        put_row(last, r, out)
        return total + fold([a * b for a, b in zip(mid, out)])

    total = lax.fori_loop(4, rows - 4, apply_second, zero)
    for k, value in enumerate((rz, pq, cross, total)):
        sums[8 * k : 8 * k + 8, :] = value


def outer_kernel(inside, above, below, kappa, eta, land, field, grad, partial,
                 weight_in, inv_in, search_in, first_in, image_in, second_in, second_image_in, last_in,
                 weight, inv, search, first, image, second, second_image, last, sums):
    weeks = grad.shape[1]
    rows = grad.shape[0]
    mask = masks(weeks)
    for d in range(4):
        put_halo(search, d, above, d * weeks, weeks)
        put_halo(search, rows + 4 + d, below, d * weeks, weeks)

    @pl.loop(0, 4)
    def _(i):
        r = jnp.where(i < 2, i - 2, rows - 2 + i)
        eta_row, land_row, kap = map_row(eta, r + 2), map_row(land, r + 2), map_row(kappa, r + 3)
        heavy = []
        for j, tile in enumerate(row_of(field, r + 2)):
            curve = jnp.tanh(0.5 * (tile + eta_row[j]))
            heavy.append(land_row[j] * (1.0 - curve * curve))
        put_row(weight, r + 2, heavy)
        put_row(inv, r + 2, [1.0 / (diag_base(k) + h) for k, h in zip(kap, heavy)])

    @pl.loop(0, 8)
    def _(i):
        r = jnp.where(i < 4, i - 3, rows - 5 + i)
        keep = scale_of(r, rows, inside)
        out = laplace_row(
            row_of(search, r + 3), row_of(search, r + 4), row_of(search, r + 5), map_row(kappa, r + 3), mask)
        put_row(first, r + 3, [keep * t for t in out])

    def apply(i, carry):
        rz, pq, cross = carry
        r = jnp.where(i < 4, i - 2, rows - 6 + i)
        keep = scale_of(r, rows, inside)
        mine = jnp.where((r >= 0) & (r < rows), 1.0, 0.0)
        own = jnp.clip(r, 0, rows - 1)
        mid, out = hessian_row(r, search, r + 4, lambda q: row_of(first, q + 3), kappa, weight, mask)
        other = [keep * (a * b) for a, b in zip(out, row_of(inv, r + 2))]
        put_row(second, r + 2, other)

        @pl.when((r >= 0) & (r < rows))
        def _():
            put_row(image, own, out)

        return (
            rz + mine * fold([a * b for a, b in zip(mid, row_of(grad, own))]),
            pq + mine * fold([a * b for a, b in zip(mid, out)]),
            cross + mine * fold([a * b for a, b in zip(other, out)]),
        )

    rz, pq, cross = lax.fori_loop(0, 8, apply, tuple(partial[8 * k : 8 * k + 8, :] for k in range(3)))

    @pl.loop(0, 8)
    def _(i):
        r = jnp.where(i < 4, i - 1, rows - 7 + i)
        keep = scale_of(r, rows, inside)
        out = laplace_row(
            row_of(second, r + 1), row_of(second, r + 2), row_of(second, r + 3), map_row(kappa, r + 3), mask)
        put_row(second_image, r + 1, [keep * t for t in out])

    def apply_second(i, total):
        r = jnp.where(i < 4, i, rows - 8 + i)
        mid, out = hessian_row(r, second, r + 2, lambda q: row_of(second_image, q + 1), kappa, weight, mask)
        put_row(last, r, out)
        return total + fold([a * b for a, b in zip(mid, out)])

    total = lax.fori_loop(0, 8, apply_second, partial[24:32, :])
    sums[...] = jnp.zeros_like(sums)
    for k, value in enumerate((rz, pq, cross, total)):
        sums[k : k + 1, :] = jnp.sum(value, axis=0, keepdims=True)


def final_kernel(sums, grad, search, image, second, last, newton_out, residual_out, newton, residual, newton_sem, residual_sem):
    rows, weeks, cols = grad.shape
    rz, pq, cross, total = (jnp.sum(sums[k : k + 1, :], axis=1, keepdims=True) for k in range(4))
    first_step = rz / pq
    rz_next = first_step * first_step * cross - rz
    turn = 1.0 + rz_next / rz
    second_step = rz_next / (turn * (turn * pq - 2.0 * first_step * cross) + first_step * first_step * total)
    along = jnp.broadcast_to(first_step + second_step * turn, (weeks, LANES))
    across = jnp.broadcast_to(second_step * first_step, (weeks, LANES))

    def copies(r):
        return (
            pltpu.make_async_copy(newton.at[r], newton_out.at[:, r, :], newton_sem.at[r]),
            pltpu.make_async_copy(residual.at[r], residual_out.at[:, r, :], residual_sem.at[r]),
        )

    @pl.loop(0, rows)
    def _(r):
        put_row(newton, r, [along * p - across * y for p, y in zip(row_of(search, r + 4), row_of(second, r + 2))])
        put_row(residual, r, [
            g - along * w + across * h for g, w, h in zip(row_of(grad, r), row_of(image, r), row_of(last, r))])
        for copy in copies(r):
            copy.start()

    @pl.loop(0, rows)
    def _(r):
        for copy in copies(r):
            copy.wait()


def call(kernel, outs, ins, scratch=(), aliases=None, limit=2, flops=0, moved=0):
    shapes = tuple(VMEM(shape, F32) if space is VMEM else jax.ShapeDtypeStruct(shape, F32) for shape, space in outs)
    return pl.pallas_call(
        kernel,
        out_shape=shapes,
        in_specs=[pl.BlockSpec(memory_space=space) for _, space in ins],
        out_specs=tuple(pl.BlockSpec(memory_space=space) for _, space in outs),
        scratch_shapes=list(scratch),
        input_output_aliases=aliases or {},
        compiler_params=pltpu.CompilerParams(vmem_limit_bytes=limit * MIB),
        cost_estimate=pl.CostEstimate(flops=flops, bytes_accessed=moved, transcendentals=0),
    )(*[array for array, _ in ins])


def shards(latent, counts, land_mask, region_ids, kappa_sq, covariates, effects, intercepts):
    weeks, rows, cols = latent.shape
    me = lax.axis_index(AX)
    land_own = land_mask.astype(F32)
    inside = jnp.stack([me > 0, me < lax.axis_size(AX) - 1]).astype(F32)

    def pack(wide, flat):
        return jnp.concatenate([jnp.transpose(wide, (1, 0, 2)).reshape(-1, cols)] + flat, axis=0)

    head = pack(latent[:, :2], [kappa_sq[:3], land_own[:2]])
    tail = pack(latent[:, -2:], [kappa_sq[-3:], land_own[-2:]])
    above, below = swap_halos(head, tail)
    cut = 2 * weeks

    def ext(depth):
        return ((rows + 2 * depth, weeks, cols), VMEM)

    def as_map(flat):
        return flat.reshape(-1, 1, cols)

    cells = weeks * rows * cols
    SMEM, ANY = pltpu.SMEM, pl.ANY
    field, grad, weight, inv, search, image, eta = call(
        start_kernel,
        [ext(2), ext(0), ext(2), ext(2), ext(4), ext(1), ((rows, 1, cols), VMEM)],
        [(effects.astype(F32), SMEM), (intercepts, SMEM), (latent, ANY), (counts, ANY), (covariates, ANY),
         (as_map(land_own), VMEM), (region_ids, VMEM), (as_map(kappa_sq), VMEM)],
        scratch=[pltpu.VMEM((rows, weeks, cols), jnp.int32), pltpu.VMEM(covariates.shape, covariates.dtype),
                 pltpu.SemaphoreType.DMA((rows,)), pltpu.SemaphoreType.DMA((rows,)), pltpu.SemaphoreType.DMA],
        flops=80 * cells, moved=12 * cells, limit=8,
    )
    kappa = as_map(jnp.concatenate([above[cut : cut + 3], kappa_sq, below[cut : cut + 3]]))
    land = as_map(jnp.concatenate([above[cut + 3 :], land_own, below[cut + 3 :]]))
    packed = ((4 * weeks + 8, cols), VMEM)
    field, grad, search, image, head, tail = call(
        edge_kernel,
        [ext(2), ext(0), ext(4), ext(1), packed, packed],
        [(inside, SMEM), (above, VMEM), (below, VMEM), (kappa, VMEM), (eta, VMEM), (inv, VMEM),
         (field, VMEM), (grad, VMEM), (search, VMEM), (image, VMEM)],
        aliases={6: 0, 7: 1, 8: 2, 9: 3},
        flops=10 * cells, moved=cells,
    )
    above, below = swap_halos(head, tail)
    first, image, second, second_image, last, partial = call(
        inner_kernel,
        [ext(3), ext(0), ext(2), ext(1), ext(0), ((32, LANES), VMEM)],
        [(kappa, VMEM), (grad, VMEM), (weight, VMEM), (inv, VMEM), (search, VMEM)],
        flops=80 * cells, moved=12 * cells,
    )
    cut = 4 * weeks
    eta = jnp.concatenate([as_map(above[cut : cut + 2]), eta, as_map(below[cut : cut + 2])])
    weight, inv, search, first, image, second, second_image, last, sums = call(
        outer_kernel,
        [ext(2), ext(2), ext(4), ext(3), ext(0), ext(2), ext(1), ext(0), ((8, LANES), VMEM)],
        [(inside, SMEM), (above, VMEM), (below, VMEM), (kappa, VMEM), (eta, VMEM), (land, VMEM), (field, VMEM),
         (grad, VMEM), (partial, VMEM), (weight, VMEM), (inv, VMEM), (search, VMEM), (first, VMEM), (image, VMEM),
         (second, VMEM), (second_image, VMEM), (last, VMEM)],
        aliases={9 + k: k for k in range(8)},
        flops=20 * cells, moved=cells,
    )
    return call(
        final_kernel,
        [(latent.shape, ANY), (latent.shape, ANY)],
        [(all_sum(sums), VMEM), (grad, VMEM), (search, VMEM), (image, VMEM), (second, VMEM), (last, VMEM)],
        scratch=[pltpu.VMEM((rows, weeks, cols), F32), pltpu.VMEM((rows, weeks, cols), F32),
                 pltpu.SemaphoreType.DMA((rows,)), pltpu.SemaphoreType.DMA((rows,))],
        flops=8 * cells, moved=8 * cells, limit=6,
    )


def solution(mesh):
    placed = (
        P(None, "gx", "region"),
        P(None, "gx", "region"),
        P("gx", "region"),
        P("gx", "region"),
        P("gx", "region"),
        P(None, "gx", "region"),
        P("region"),
        P("region"),
    )
    return jax.shard_map(
        shards,
        mesh=mesh,
        in_specs=placed,
        out_specs=(P(None, "gx", "region"), P(None, "gx", "region")),
        check_vma=False,
    )
```

time: 108 us -> 62.5 us (0.58)
  other arithmetic: 48.2 us -> 1.34 us
  Pallas kernels: 0 us -> 32.3 us
  local copies, waits for them, and re-layouts: 22.5 us -> 6.02 us
  starting transfers between devices: 22.9 us -> 14.4 us
  between operations: 6.25 us -> 0.96 us
  matrix products: 2.33 us -> 0 us
  waiting for transfers between devices: 5.66 us -> 7.21 us
    pallas_call x0 -> x5, Pallas kernels: none -> 32.3 us  [call(): pl.pallas_call(kernel, out_shape=shapes, in_specs=[pl.BlockSpec(memory_sp...]
    mul x4 -> x0, other arithmetic: 15.9 us -> none  [the longest x1 11.6 us: shards(): other = inside(2) * (image / (diag_base[1:-1, None] + weight))]
    ppermute x4, starting transfers between devices: 17 us -> 5.75 us  [all_sum(): lax.ppermute(values, AX, [(i, i ^ step) for i in range(count)])]
    slice x29 -> x7, local copies, waits for them, and re-layouts: 10.2 us -> 0.97 us  [the longest x2 0.94 us: shards(): head = pack(latent[:, :2], [kappa_sq[:3], land_own[:2]])]
    unnamed x35 -> x14, local copies, waits for them, and re-layouts: 11.7 us -> 3.2 us
    div x1 -> x0, other arithmetic: 7.48 us -> none  [shards(): search = gradient / (diag_base[3:-3, None] + weight)]
    add x5 -> x0, other arithmetic: 5.39 us -> none  [the longest x1 5.28 us: shards(): eta = cov_term + offset]
    reduce_sum x1 -> x0, other arithmetic: 5.26 us -> none  [shards(): jnp.sum(search * own_image)]
  transfers between devices with their start and end apart: 8 -> 8, of which waited for: 5 -> 4; matrix products, arithmetic and copies ran while one was open for 10% -> 1% of each run, Pallas kernels for 0% -> 38%
where the time goes in v2:
time: 62.5 us; the launch traced here: 62.3 us
  Pallas kernels  32.3 us (52%)
  starting transfers between devices  14.4 us (23%)
  waiting for transfers between devices  7.21 us (12%)
  local copies, waits for them, and re-layouts  6.02 us (10%)
  other arithmetic  1.34 us (2%)
  between operations  0.96 us (2%)
    pallas_call x5, Pallas kernels, call(): pl.pallas_call(kernel, out_shape=shapes, in_specs=[pl.BlockSpec(memory_sp...  32.3 us
    ppermute x2, starting transfers between devices, swap_halos(): got_first = lax.ppermute(jnp.where(odd, head, tail), AX, first)  7.31 us
    ppermute x4, waiting for transfers between devices, all_sum(): lax.ppermute(values, AX, [(i, i ^ step) for i in range(count)])  7.2 us
    ppermute x4, starting transfers between devices, all_sum(): lax.ppermute(values, AX, [(i, i ^ step) for i in range(count)])  5.75 us
    unnamed x14, local copies, waits for them, and re-layouts  3.2 us
    transpose x3, local copies, waits for them, and re-layouts, pack(): jnp.transpose(wide, (1, 0, 2)).reshape(-1, cols)  1.39 us
    ppermute x2, starting transfers between devices, swap_halos(): got_second = lax.ppermute(jnp.where(odd, tail, head), AX, second)  1.35 us
  transfers between devices with their start and end apart: 8, of which 4 were waited for; matrix products, arithmetic and copies ran while one was open for 1% of the time, Pallas kernels for 38%

profile of v2, /device:TPU:0, one launch (start us, length us, event | category | flops | bytes accessed | tf_op | source)
XLA Modules:
  0.0 62.3 jit_solution(2266279369854091902)
XLA Ops:
  0.6 0.0 copy-start.5
  0.6 0.0 copy-start
  0.7 0.0 copy-start.6
  0.7 0.0 copy-start.4
  0.7 0.0 copy-start.3
  0.7 0.9 %fusion.2 = (f32[3,1024]{1,0:T(4,128)S(1)}, f32[3,1024]{1,0:T(4,128)S(1)}) fusion(f32[32,1024]{1,0:T(8,128)} %param.12), kind=kLoop, calls=%fused_computation.18 | loop fusion | bytes 49152 | tf_op jit(solution)/shard_map/slice | solution.py:375
  1.6 0.9 %convert_bitcast_fusion = (f32[32,1,1024]{2,0,1:T(8,128)S(1)}, f32[32,1024]{1,0:T(8,128)S(1)}) fusion(s32[32,1024]{1,0:T(8,128)} %param.10), kind=kLoop, calls=%fused_computation.17 | loop fusion | flops 32768 | bytes 393216 | tf_op jit(solution)/shard_map/reshape | solution.py:384
  2.6 1.3 %slice_bitcast_fusion.1 = (f32[2,16,1024]{2,0,1:T(2,128)S(1)}, f32[2,16,1024]{2,0,1:T(2,128)S(1)}) fusion(f32[16,32,1024]{2,1,0:T(8,128)} %latent.1), kind=kLoop, calls=%fused_computation.10 | loop fusion | bytes 524288 | tf_op jit(solution)/shard_map/transpose | solution.py:373
  4.0 0.7 %collective-permute-start.1 = (f32[37,1024]{1,0:T(8,128)S(1)}, f32[37,1024]{1,0:T(8,128)S(1)}, u32[]{:S(2)}, u32[]{:S(2)}) collective-permute-start(f32[37,1024]{1,0:T(8,128)S(1)} %get-tuple-element.56), channel_id=1, source_target_pairs={{1,2},{2,1},{3,4},{4,3},{5,6},{6,5},{7,8},{8,7},{9,10},{10,9},{11,... | collective-permute-start | bytes 454664 | tf_op jit(solution)/shard_map/ppermute | solution.py:25
  4.7 4.4 %collective-permute-start = (f32[37,1024]{1,0:T(8,128)S(1)}, f32[37,1024]{1,0:T(8,128)S(1)}, u32[]{:S(2)}, u32[]{:S(2)}) collective-permute-start(f32[37,1024]{1,0:T(8,128)S(1)} %get-tuple-element.57), channel_id=1, source_target_pairs={{0,1},{1,0},{2,3},{3,2},{4,5},{5,4},{6,7},{7,6},{8,9},{9,8},{10,11... | collective-permute-start | bytes 454664 | tf_op jit(solution)/shard_map/ppermute | solution.py:24
  9.1 0.0 copy-done.5
  9.1 0.1 reshape.32.kappa
  9.2 0.0 copy-done.6
  9.2 0.1 copy.24.land
  9.3 0.0 copy-done
  9.3 0.0 copy-done.4
  9.3 0.0 copy-done.3
  9.4 0.0 copy-start.1
  9.4 1.6 %copy-done.1 = s32[16,32,1024]{2,1,0:T(8,128)S(1)} copy-done((s32[16,32,1024]{2,1,0:T(8,128)S(1)}, s32[16,32,1024]{2,1,0:T(8,128)}, u32[]{:S(2)}) %copy-start.1) | copy-done | bytes 2097176
  10.9 0.0 copy-start.2
  11.0 1.6 %copy-done.2 = bf16[32,32,1024]{2,1,0:T(8,128)(2,1)S(1)} copy-done((bf16[32,32,1024]{2,1,0:T(8,128)(2,1)S(1)}, bf16[32,32,1024]{2,1,0:T(8,128)(2,1)}, u32[]{:S(2)}) %copy-start.2) | copy-done | bytes 2097176
  12.5 11.4 %shard_map.95 = (f32[36,16,1024]{2,1,0:T(8,128)S(1)}, f32[32,16,1024]{2,1,0:T(8,128)S(1)}, f32[36,16,1024]{2,1,0:T(8,128)S(1)}, f32[36,16,1024]{2,1,0:T(8,128)S(...) custom-call(f32[32]{0:T(128)S(1)} %convert_element_type.11.effects, ...), custom_call_target="tpu_custom_call" | custom-call | flops 41943040 | bytes 6291456 | tf_op jit(solution)/shard_map/pallas_call | solution.py:354
  23.9 0.1 add_convert_fusion.inside
  24.0 0.0 collective-permute-done.1
  24.0 0.0 collective-permute-done
  24.1 0.1 reshape.30.kappa
  24.2 1.5 %shard_map.96 = (f32[36,16,1024]{2,1,0:T(8,128)S(1)}, f32[32,16,1024]{2,1,0:T(8,128)S(1)}, f32[40,16,1024]{2,1,0:T(8,128)S(1)}, f32[34,16,1024]{2,1,0:T(8,128)S(...) custom-call(f32[2]{0:T(128)S(1)} %add_convert_fusion.inside, ...), custom_call_target="tpu_custom_call", output_to_operand_aliasing={{0}: (6, {}), {1}: (7, {}), {2}: (8, {}), {3}: (9, {})} | custom-call | flops 5242880 | bytes 524288 | tf_op jit(solution)/shard_map/pallas_call | solution.py:354
  25.7 0.7 %collective-permute-start.3 = (f32[72,1024]{1,0:T(8,128)S(1)}, f32[72,1024]{1,0:T(8,128)S(1)}, u32[]{:S(2)}, u32[]{:S(2)}) collective-permute-start(f32[72,1024]{1,0:T(8,128)S(1)} %get-tuple-element.52), channel_id=1, source_target_pairs={{1,2},{2,1},{3,4},{4,3},{5,6},{6,5},{7,8},{8,7},{9,10},{10,9},{11,... | collective-permute-start | bytes 884744 | tf_op jit(solution)/shard_map/ppermute | solution.py:25
  26.4 3.0 %collective-permute-start.2 = (f32[72,1024]{1,0:T(8,128)S(1)}, f32[72,1024]{1,0:T(8,128)S(1)}, u32[]{:S(2)}, u32[]{:S(2)}) collective-permute-start(f32[72,1024]{1,0:T(8,128)S(1)} %get-tuple-element.53), channel_id=1, source_target_pairs={{0,1},{1,0},{2,3},{3,2},{4,5},{5,4},{6,7},{7,6},{8,9},{9,8},{10,11... | collective-permute-start | bytes 884744 | tf_op jit(solution)/shard_map/ppermute | solution.py:24
  29.4 0.1 reshape.35.land
  29.6 12.3 %shard_map.97 = (f32[38,16,1024]{2,1,0:T(8,128)S(1)}, f32[32,16,1024]{2,1,0:T(8,128)S(1)}, f32[36,16,1024]{2,1,0:T(8,128)S(1)}, f32[34,16,1024]{2,1,0:T(8,128)S(...) custom-call(f32[38,1,1024]{2,1,0:T(1,128)S(1)} %reshape.30.kappa, f32[32,16,1024]{2,1,0:T(8,128)S(1)} %get-tuple-element.34.grad, ...), custom_call_target="tpu_custom_call" | custom-call | flops 41943040 | bytes 6291456 | tf_op jit(solution)/shard_map/pallas_call | solution.py:354
  41.9 0.0 collective-permute-done.3
  41.9 0.0 collective-permute-done.2
  42.0 0.1 pad_maximum_fusion.4.eta
  42.2 4.5 %shard_map.98 = (f32[36,16,1024]{2,1,0:T(8,128)S(1)}, f32[36,16,1024]{2,1,0:T(8,128)S(1)}, f32[40,16,1024]{2,1,0:T(8,128)S(1)}, f32[38,16,1024]{2,1,0:T(8,128)S(...) custom-call(f32[2]{0:T(128)S(1)} %add_convert_fusion.inside, ...), custom_call_target="tpu_custom_call", output_to_operand_aliasing={{0}: (9, {}), {1}: (10, {}), {2}: (11, {}), {3}: (12, {}), ... | custom-call | flops 10485760 | bytes 524288 | tf_op jit(solution)/shard_map/pallas_call | solution.py:354
  46.7 0.1 collective-permute-start.4
  46.7 1.1 %collective-permute-done.4 = f32[8,128]{1,0:T(8,128)S(1)} collective-permute-done((f32[8,128]{1,0:T(8,128)S(1)}, f32[8,128]{1,0:T(8,128)S(1)}, u32[]{:S(2)}, u32[]{:S(2)}) %collective-permute-start.4) | collective-permute-done | bytes 4128 | tf_op jit(solution)/shard_map/ppermute | solution.py:35
  47.9 1.5 %collective-permute-start.5 = (f32[8,128]{1,0:T(8,128)S(1)}, f32[8,128]{1,0:T(8,128)S(1)}, u32[]{:S(2)}, u32[]{:S(2)}) collective-permute-start(f32[8,128]{1,0:T(8,128)S(1)} %add.18), channel_id=1, source_target_pairs={{0,2},{1,3},{2,0},{3,1},{4,6},{5,7},{6,4},{7,5},{8,10},{9,11},{10,... | collective-permute-start | bytes 12296 | tf_op jit(solution)/shard_map/ppermute | solution.py:35
  49.4 2.1 %collective-permute-done.5 = f32[8,128]{1,0:T(8,128)S(1)} collective-permute-done((f32[8,128]{1,0:T(8,128)S(1)}, f32[8,128]{1,0:T(8,128)S(1)}, u32[]{:S(2)}, u32[]{:S(2)}) %collective-permute-start.5) | collective-permute-done | bytes 4128 | tf_op jit(solution)/shard_map/ppermute | solution.py:35
  51.5 1.6 %collective-permute-start.6 = (f32[8,128]{1,0:T(8,128)S(1)}, f32[8,128]{1,0:T(8,128)S(1)}, u32[]{:S(2)}, u32[]{:S(2)}) collective-permute-start(f32[8,128]{1,0:T(8,128)S(1)} %add.19), channel_id=1, source_target_pairs={{0,4},{1,5},{2,6},{3,7},{4,0},{5,1},{6,2},{7,3},{8,12},{9,13},{10,... | collective-permute-start | bytes 12296 | tf_op jit(solution)/shard_map/ppermute | solution.py:35
  53.1 2.0 %collective-permute-done.6 = f32[8,128]{1,0:T(8,128)S(1)} collective-permute-done((f32[8,128]{1,0:T(8,128)S(1)}, f32[8,128]{1,0:T(8,128)S(1)}, u32[]{:S(2)}, u32[]{:S(2)}) %collective-permute-start.6) | collective-permute-done | bytes 4128 | tf_op jit(solution)/shard_map/ppermute | solution.py:35
  55.1 2.6 %collective-permute-start.7 = (f32[8,128]{1,0:T(8,128)S(1)}, f32[8,128]{1,0:T(8,128)S(1)}, u32[]{:S(2)}, u32[]{:S(2)}) collective-permute-start(f32[8,128]{1,0:T(8,128)S(1)} %add.20), channel_id=1, source_target_pairs={{0,8},{1,9},{2,10},{3,11},{4,12},{5,13},{6,14},{7,15},{8,0},{9,1},... | collective-permute-start | bytes 12296 | tf_op jit(solution)/shard_map/ppermute | solution.py:35
  57.7 1.9 %collective-permute-done.7 = f32[8,128]{1,0:T(8,128)S(1)} collective-permute-done((f32[8,128]{1,0:T(8,128)S(1)}, f32[8,128]{1,0:T(8,128)S(1)}, u32[]{:S(2)}, u32[]{:S(2)}) %collective-permute-start.7) | collective-permute-done | bytes 4128 | tf_op jit(solution)/shard_map/ppermute | solution.py:35
  59.6 2.7 %shard_map.99 = (f32[16,32,1024]{2,1,0:T(8,128)}, f32[16,32,1024]{2,1,0:T(8,128)}) custom-call(f32[8,128]{1,0:T(8,128)S(1)} %add.21.sums, f32[32,16,1024]{2,1,0:T(8,128)S(1)} %get-tuple-element.34.grad, f32[40,16,1024]{2,1,0:T(8,128)S(1)} %get-tuple-element.44.search, f32[32,16,1024]{2,1,0:T(8,128)S(1)} %get-tuple-element.45.image, ...), custom_call_target="tpu_custom_call" | custom-call | flops 4194304 | bytes 4194304 | tf_op jit(solution)/shard_map/pallas_call | solution.py:354
  (22 shorter events, 0.4 us)
Async XLA Ops:
  0.6 8.4 %copy-start.5 = (f32[32,1024]{1,0:T(8,128)S(1)}, f32[32,1024]{1,0:T(8,128)}, u32[]{:S(2)}) copy-start(f32[32,1024]{1,0:T(8,128)} %param.12) | copy-start | bytes 393220
  0.6 8.7 %copy-start = (f32[16,32,1024]{2,1,0:T(8,128)S(1)}, f32[16,32,1024]{2,1,0:T(8,128)}, u32[]{:S(2)}) copy-start(f32[16,32,1024]{2,1,0:T(8,128)} %latent.1) | copy-start | bytes 6291460
  0.7 8.5 %copy-start.6 = (bf16[32]{0:T(256)(128)(2,1)S(1)}, bf16[32]{0:T(256)(128)(2,1)}, u32[]{:S(2)}) copy-start(bf16[32]{0:T(256)(128)(2,1)} %param.14) | copy-start | bytes 196
  0.7 8.7 %copy-start.4 = (f32[8]{0:T(128)S(1)}, f32[8]{0:T(128)}, u32[]{:S(2)}) copy-start(f32[8]{0:T(128)} %intercepts.1) | copy-start | bytes 100
  0.7 8.7 %copy-start.3 = (s32[32,1024]{1,0:T(8,128)S(1)}, s32[32,1024]{1,0:T(8,128)}, u32[]{:S(2)}) copy-start(s32[32,1024]{1,0:T(8,128)} %zones.1) | copy-start | bytes 393220
  4.0 20.0 %collective-permute-start.1 = (f32[37,1024]{1,0:T(8,128)S(1)}, f32[37,1024]{1,0:T(8,128)S(1)}, u32[]{:S(2)}, u32[]{:S(2)}) collective-permute-start(f32[37,1024]{1,0:T(8,128)S(1)} %get-tuple-element.56), channel_id=1, source_target_pairs={{1,2},{2,1},{3,4},{4,3},{5,6},{6,5},{7,8},{8,7},{9,10},{10,9},{11,... | collective-permute-start | bytes 454664 | tf_op jit(solution)/shard_map/ppermute | solution.py:25
  4.7 19.3 %collective-permute-start = (f32[37,1024]{1,0:T(8,128)S(1)}, f32[37,1024]{1,0:T(8,128)S(1)}, u32[]{:S(2)}, u32[]{:S(2)}) collective-permute-start(f32[37,1024]{1,0:T(8,128)S(1)} %get-tuple-element.57), channel_id=1, source_target_pairs={{0,1},{1,0},{2,3},{3,2},{4,5},{5,4},{6,7},{7,6},{8,9},{9,8},{10,11... | collective-permute-start | bytes 454664 | tf_op jit(solution)/shard_map/ppermute | solution.py:24
  9.4 1.6 %copy-start.1 = (s32[16,32,1024]{2,1,0:T(8,128)S(1)}, s32[16,32,1024]{2,1,0:T(8,128)}, u32[]{:S(2)}) copy-start(s32[16,32,1024]{2,1,0:T(8,128)} %counts.1) | copy-start | bytes 6291460
  10.9 1.6 %copy-start.2 = (bf16[32,32,1024]{2,1,0:T(8,128)(2,1)S(1)}, bf16[32,32,1024]{2,1,0:T(8,128)(2,1)}, u32[]{:S(2)}) copy-start(bf16[32,32,1024]{2,1,0:T(8,128)(2,1)} %covariates.1) | copy-start | bytes 6291460
  25.7 16.2 %collective-permute-start.3 = (f32[72,1024]{1,0:T(8,128)S(1)}, f32[72,1024]{1,0:T(8,128)S(1)}, u32[]{:S(2)}, u32[]{:S(2)}) collective-permute-start(f32[72,1024]{1,0:T(8,128)S(1)} %get-tuple-element.52), channel_id=1, source_target_pairs={{1,2},{2,1},{3,4},{4,3},{5,6},{6,5},{7,8},{8,7},{9,10},{10,9},{11,... | collective-permute-start | bytes 884744 | tf_op jit(solution)/shard_map/ppermute | solution.py:25
  26.4 15.5 %collective-permute-start.2 = (f32[72,1024]{1,0:T(8,128)S(1)}, f32[72,1024]{1,0:T(8,128)S(1)}, u32[]{:S(2)}, u32[]{:S(2)}) collective-permute-start(f32[72,1024]{1,0:T(8,128)S(1)} %get-tuple-element.53), channel_id=1, source_target_pairs={{0,1},{1,0},{2,3},{3,2},{4,5},{5,4},{6,7},{7,6},{8,9},{9,8},{10,11... | collective-permute-start | bytes 884744 | tf_op jit(solution)/shard_map/ppermute | solution.py:24
  46.7 1.2 %collective-permute-start.4 = (f32[8,128]{1,0:T(8,128)S(1)}, f32[8,128]{1,0:T(8,128)S(1)}, u32[]{:S(2)}, u32[]{:S(2)}) collective-permute-start(f32[8,128]{1,0:T(8,128)S(1)} %get-tuple-element.43), channel_id=1, source_target_pairs={{0,1},{1,0},{2,3},{3,2},{4,5},{5,4},{6,7},{7,6},{8,9},{9,8},{10,11... | collective-permute-start | bytes 12296 | tf_op jit(solution)/shard_map/ppermute | solution.py:35
  47.9 3.6 %collective-permute-start.5 = (f32[8,128]{1,0:T(8,128)S(1)}, f32[8,128]{1,0:T(8,128)S(1)}, u32[]{:S(2)}, u32[]{:S(2)}) collective-permute-start(f32[8,128]{1,0:T(8,128)S(1)} %add.18), channel_id=1, source_target_pairs={{0,2},{1,3},{2,0},{3,1},{4,6},{5,7},{6,4},{7,5},{8,10},{9,11},{10,... | collective-permute-start | bytes 12296 | tf_op jit(solution)/shard_map/ppermute | solution.py:35
  51.5 3.6 %collective-permute-start.6 = (f32[8,128]{1,0:T(8,128)S(1)}, f32[8,128]{1,0:T(8,128)S(1)}, u32[]{:S(2)}, u32[]{:S(2)}) collective-permute-start(f32[8,128]{1,0:T(8,128)S(1)} %add.19), channel_id=1, source_target_pairs={{0,4},{1,5},{2,6},{3,7},{4,0},{5,1},{6,2},{7,3},{8,12},{9,13},{10,... | collective-permute-start | bytes 12296 | tf_op jit(solution)/shard_map/ppermute | solution.py:35
  55.1 4.5 %collective-permute-start.7 = (f32[8,128]{1,0:T(8,128)S(1)}, f32[8,128]{1,0:T(8,128)S(1)}, u32[]{:S(2)}, u32[]{:S(2)}) collective-permute-start(f32[8,128]{1,0:T(8,128)S(1)} %add.20), channel_id=1, source_target_pairs={{0,8},{1,9},{2,10},{3,11},{4,12},{5,13},{6,14},{7,15},{8,0},{9,1},... | collective-permute-start | bytes 12296 | tf_op jit(solution)/shard_map/ppermute | solution.py:35

commit v3 on v2

v3 whole, which is shorter than its diff:
```python
import functools

import jax
import jax.numpy as jnp
from jax import lax
from jax.experimental import pallas as pl
from jax.experimental.pallas import tpu as pltpu
from jax.sharding import PartitionSpec as P

AX = "gx"
LANES = 128
prior_scale = 0.04
time_coupling = 0.5
F32 = jnp.float32
VMEM = pltpu.VMEM
MIB = 1 << 20


def pair_maps(count):
    first = [(i, i ^ 1) for i in range(count) if (i ^ 1) < count]
    second = [(i, ((i + 1) ^ 1) - 1) for i in range(count) if 0 <= ((i + 1) ^ 1) - 1 < count]
    return first, second


def all_sum(values):
    count = lax.axis_size(AX)
    if count & (count - 1):
        return lax.psum(values, AX)
    step = 1
    while step < count:
        values = values + lax.ppermute(values, AX, [(i, i ^ step) for i in range(count)])
        step *= 2
    return values


def row_of(ref, row):
    return [ref[row, :, c : c + LANES] for c in range(0, ref.shape[2], LANES)]


def put_row(ref, row, tiles):
    for j, tile in enumerate(tiles):
        ref[row, :, j * LANES : (j + 1) * LANES] = tile


def map_row(ref, row):
    return [ref[row, :, c : c + LANES] for c in range(0, ref.shape[2], LANES)]


def masks(weeks):
    lane = lax.broadcasted_iota(jnp.int32, (weeks, LANES), 1)
    week = lax.broadcasted_iota(jnp.int32, (weeks, LANES), 0)
    return lane == 0, lane == LANES - 1, week == 0, week == weeks - 1


def laplace_row(up, mid, down, kappa, mask):
    first, last = mask[0], mask[1]
    count = len(mid)
    to_right = [pltpu.roll(t, 1, 1) for t in mid]
    to_left = [pltpu.roll(t, LANES - 1, 1) for t in mid]
    out = []
    for j in range(count):
        west = jnp.where(first, to_right[j - 1] if j > 0 else 0.0, to_right[j])
        east = jnp.where(last, to_left[j + 1] if j + 1 < count else 0.0, to_left[j])
        out.append((kappa[j] + 4.0) * mid[j] - ((up[j] + down[j]) + (west + east)))
    return out


def temporal_tile(tile, mask):
    weeks = tile.shape[0]
    before = jnp.where(mask[2], tile, pltpu.roll(tile, 1, 0))
    after = jnp.where(mask[3], tile, pltpu.roll(tile, weeks - 1, 0))
    return (2.0 * tile - before) - after


def fold(tiles):
    parts = [t[h : h + 8] for t in tiles for h in range(0, t.shape[0], 8)]
    while len(parts) > 1:
        parts = [a + b for a, b in zip(parts[::2], parts[1::2])] + ([parts[-1]] if len(parts) % 2 else [])
    return parts[0]


def diag_base(kappa):
    return prior_scale * ((kappa + 4.0) * (kappa + 4.0) + 4.0) + 2.0 * time_coupling


def is_odd():
    return lax.axis_index(AX) % 2 == 1


def row_loop(low, high, body, carry=None, most=14):
    count = high - low
    step = max(k for k in range(1, most + 1) if count % k == 0)

    def chunk(i, value):
        for k in range(step):
            value = body(low + i * step + k, value)
        return value

    if step == count:
        return chunk(0, carry)
    if carry is None:
        lax.fori_loop(0, count // step, lambda i, z: (chunk(i, None), z)[1], 0)
        return None
    return lax.fori_loop(0, count // step, chunk, carry)


def pack_kernel(latent, kappa, land, first, second, kappa_out, land_out, sems):
    weeks, rows, cols = latent.shape
    odd = is_odd()
    copies = []
    for k, (out, base) in enumerate(((first, jnp.where(odd, 0, rows - 2)), (second, jnp.where(odd, rows - 2, 0)))):
        for d in range(2):
            copies.append(pltpu.make_async_copy(
                latent.at[:, base + d, :], out.at[d * weeks : (d + 1) * weeks, :], sems.at[2 * k + d]))
    for copy in copies:
        copy.start()
    for r in range(rows):
        kappa_out[r + 3] = kappa[r : r + 1, :]
        land_out[r] = land[r : r + 1, :].astype(F32)
    at = 2 * weeks
    for d in range(3):
        top, bottom = kappa[d : d + 1, :], kappa[rows - 3 + d : rows - 2 + d, :]
        first[at + d : at + d + 1, :] = jnp.where(odd, top, bottom)
        second[at + d : at + d + 1, :] = jnp.where(odd, bottom, top)
    for d in range(2):
        top, bottom = (land[q : q + 1, :].astype(F32) for q in (d, rows - 2 + d))
        first[at + 3 + d : at + 4 + d, :] = jnp.where(odd, top, bottom)
        second[at + 3 + d : at + 4 + d, :] = jnp.where(odd, bottom, top)
    first[at + 5 :, :] = jnp.zeros((3, cols), F32)
    second[at + 5 :, :] = jnp.zeros((3, cols), F32)
    for copy in copies:
        copy.wait()


def start_kernel(effects, intercepts, latent, counts, covariates, land, zones, kappa,
                 field, grad, weight, inv, search, image, eta,
                 tally, covs, field_sem, tally_sem, cov_sem):
    weeks, rows, cols = latent.shape
    num_covs = covariates.shape[0]
    mask = masks(weeks)

    def field_copy(r):
        return pltpu.make_async_copy(latent.at[:, r, :], field.at[r + 2], field_sem.at[r])

    def tally_copy(r):
        return pltpu.make_async_copy(counts.at[:, r, :], tally.at[r], tally_sem.at[r])

    cov_copy = pltpu.make_async_copy(covariates, covs, cov_sem)
    for r in range(rows):
        field_copy(r).start()
    cov_copy.start()
    for r in range(rows):
        tally_copy(r).start()
    field_copy(0).wait()
    field_copy(1).wait()

    def inner_image(r, _):
        field_copy(r + 1).wait()
        put_row(image, r + 1, laplace_row(
            row_of(field, r + 1), row_of(field, r + 2), row_of(field, r + 3), map_row(kappa, r + 3), mask))

    row_loop(1, rows - 1, inner_image)
    cov_copy.wait()
    width = 2 * LANES
    for c in range(0, cols, width):
        total = jnp.zeros((rows, width), F32)
        ids = zones[:, c : c + width]
        for z in range(intercepts.shape[0]):
            total = jnp.where(ids == z, intercepts[z], total)
        for k in range(num_covs):
            total = total + effects[k] * covs[k, :, c : c + width].astype(F32)
        for r in range(rows):
            eta[r, :, c : c + width] = total[r : r + 1]

    def pointwise(r):
        tally_copy(r).wait()
        lat, eta_row, land_row, kap, count_row = (
            row_of(field, r + 2), map_row(eta, r), map_row(land, r), map_row(kappa, r + 3), row_of(tally, r))
        out, heavy, inverse = [], [], []
        for j, tile in enumerate(lat):
            on = land_row[j]
            curve = jnp.tanh(0.5 * (tile + eta_row[j]))
            heavy.append(on * (1.0 - curve * curve))
            inverse.append(1.0 / (diag_base(kap[j]) + heavy[j]))
            out.append(on * (count_row[j].astype(F32) - 2.0 - 2.0 * curve) - time_coupling * temporal_tile(tile, mask))
        put_row(weight, r + 2, heavy)
        put_row(inv, r + 2, inverse)
        return out, inverse, kap

    for r in (0, 1, rows - 2, rows - 1):
        put_row(grad, r, pointwise(r)[0])

    def gradient(r, _):
        out, inverse, kap = pointwise(r)
        outer = laplace_row(row_of(image, r), row_of(image, r + 1), row_of(image, r + 2), kap, mask)
        out = [a - prior_scale * b for a, b in zip(out, outer)]
        put_row(grad, r, out)
        put_row(search, r + 4, [a * b for a, b in zip(out, inverse)])

    row_loop(2, rows - 2, gradient, most=7)


def keep_inside(r, rows, tiles):
    if 0 <= r < rows:
        return tiles
    place, count = lax.axis_index(AX), lax.axis_size(AX)
    keep = jnp.where(place > 0 if r < 0 else place < count - 1, 1.0, 0.0)
    return [keep * t for t in tiles]


def halo_row(r, rows, depth, height, first, second):
    odd = is_odd()
    at = (r + depth if r < 0 else r - rows) * height
    a, b = (first, second) if r < 0 else (second, first)
    return [jnp.where(odd, a[at : at + height, c : c + LANES], b[at : at + height, c : c + LANES])
            for c in range(0, first.shape[1], LANES)]


def halo_line(above, line, first, second):
    odd = is_odd()
    a, b = (first, second) if above else (second, first)
    return [jnp.where(odd, a[line : line + 1, c : c + LANES], b[line : line + 1, c : c + LANES])
            for c in range(0, first.shape[1], LANES)]


def edge_kernel(got_first, got_second, eta, inv, kappa_in, field_in, grad_in, search_in, image_in,
                kappa, field, grad, search, image, first, second):
    weeks = field.shape[1]
    rows, _, cols = eta.shape
    mask = masks(weeks)
    odd = is_odd()
    for d in range(2):
        put_row(field, d, halo_row(d - 2, rows, 2, weeks, got_first, got_second))
        put_row(field, rows + 2 + d, halo_row(rows + d, rows, 2, weeks, got_first, got_second))
    for d in range(3):
        put_row(kappa, d, halo_line(True, 2 * weeks + d, got_first, got_second))
        put_row(kappa, rows + 3 + d, halo_line(False, 2 * weeks + d, got_first, got_second))
    for r in (-1, 0, rows - 1, rows):
        put_row(image, r + 1, keep_inside(r, rows, laplace_row(
            row_of(field, r + 1), row_of(field, r + 2), row_of(field, r + 3), map_row(kappa, r + 3), mask)))
    for r in (0, 1, rows - 2, rows - 1):
        outer = laplace_row(row_of(image, r), row_of(image, r + 1), row_of(image, r + 2), map_row(kappa, r + 3), mask)
        out = [a - prior_scale * b for a, b in zip(row_of(grad, r), outer)]
        put_row(grad, r, out)
        put_row(search, r + 4, [a * b for a, b in zip(out, row_of(inv, r + 2))])
    at = 4 * weeks
    for c in range(0, cols, LANES):
        part = slice(c, c + LANES)
        for d in range(4):
            top, bottom = search[4 + d, :, part], search[rows + d, :, part]
            first[d * weeks : (d + 1) * weeks, part] = jnp.where(odd, top, bottom)
            second[d * weeks : (d + 1) * weeks, part] = jnp.where(odd, bottom, top)
        for d in range(2):
            top, bottom = eta[d, :, part], eta[rows - 2 + d, :, part]
            first[at + d : at + d + 1, part] = jnp.where(odd, top, bottom)
            second[at + d : at + d + 1, part] = jnp.where(odd, bottom, top)
        first[at + 2 :, part] = jnp.zeros((6, LANES), F32)
        second[at + 2 :, part] = jnp.zeros((6, LANES), F32)


def hessian_row(r, source, at, image, offset, kappa, weight, mask):
    outer = laplace_row(row_of(image, r + offset - 1), row_of(image, r + offset), row_of(image, r + offset + 1),
                        map_row(kappa, r + 3), mask)
    mid = row_of(source, at)
    heavy = row_of(weight, r + 2)
    return mid, [
        prior_scale * o + (time_coupling * temporal_tile(m, mask) + h * m) for o, m, h in zip(outer, mid, heavy)
    ]


def dot_rows(a, b):
    return fold([x * y for x, y in zip(a, b)])


def inner_kernel(kappa, grad, weight, inv, search, first, image, second, second_image, last, sums):
    weeks = grad.shape[1]
    rows = grad.shape[0]
    mask = masks(weeks)

    def inner_image(r, _):
        put_row(first, r + 3, laplace_row(
            row_of(search, r + 3), row_of(search, r + 4), row_of(search, r + 5), map_row(kappa, r + 3), mask))

    row_loop(1, rows - 1, inner_image)
    zero = jnp.zeros((8, LANES), F32)

    def apply(r, carry):
        rz, pq, cross = carry
        mid, out = hessian_row(r, search, r + 4, first, 3, kappa, weight, mask)
        other = [a * b for a, b in zip(out, row_of(inv, r + 2))]
        put_row(image, r, out)
        put_row(second, r + 2, other)
        return rz + dot_rows(mid, row_of(grad, r)), pq + dot_rows(mid, out), cross + dot_rows(other, out)

    rz, pq, cross = row_loop(2, rows - 2, apply, (zero, zero, zero), most=7)

    def second_inner(r, _):
        put_row(second_image, r + 1, laplace_row(
            row_of(second, r + 1), row_of(second, r + 2), row_of(second, r + 3), map_row(kappa, r + 3), mask))

    row_loop(3, rows - 3, second_inner)

    def apply_second(r, total):
        mid, out = hessian_row(r, second, r + 2, second_image, 1, kappa, weight, mask)
        put_row(last, r, out)
        return total + dot_rows(mid, out)

    total = row_loop(4, rows - 4, apply_second, zero, most=8)
    for k, value in enumerate((rz, pq, cross, total)):
        sums[8 * k : 8 * k + 8, :] = value


def outer_kernel(old_first, old_second, got_first, got_second, kappa, field, grad, partial,
                 weight_in, inv_in, search_in, first_in, image_in, second_in, second_image_in, last_in,
                 weight, inv, search, first, image, second, second_image, last, sums):
    weeks = grad.shape[1]
    rows = grad.shape[0]
    mask = masks(weeks)
    for d in range(4):
        put_row(search, d, halo_row(d - 4, rows, 4, weeks, got_first, got_second))
        put_row(search, rows + 4 + d, halo_row(rows + d, rows, 4, weeks, got_first, got_second))
    for above in (True, False):
        for d in range(2):
            r = d - 2 if above else rows + d
            eta_row = halo_line(above, 4 * weeks + d, got_first, got_second)
            land_row = halo_line(above, 2 * weeks + 3 + d, old_first, old_second)
            heavy = []
            for j, tile in enumerate(row_of(field, r + 2)):
                curve = jnp.tanh(0.5 * (tile + eta_row[j]))
                heavy.append(land_row[j] * (1.0 - curve * curve))
            put_row(weight, r + 2, heavy)
            put_row(inv, r + 2, [1.0 / (diag_base(k) + h) for k, h in zip(map_row(kappa, r + 3), heavy)])

    for r in (-3, -2, -1, 0, rows - 1, rows, rows + 1, rows + 2):
        put_row(first, r + 3, keep_inside(r, rows, laplace_row(
            row_of(search, r + 3), row_of(search, r + 4), row_of(search, r + 5), map_row(kappa, r + 3), mask)))
    rz, pq, cross, total = (partial[8 * k : 8 * k + 8, :] for k in range(4))
    for r in (-2, -1, 0, 1, rows - 2, rows - 1, rows, rows + 1):
        mid, out = hessian_row(r, search, r + 4, first, 3, kappa, weight, mask)
        other = keep_inside(r, rows, [a * b for a, b in zip(out, row_of(inv, r + 2))])
        put_row(second, r + 2, other)
        if 0 <= r < rows:
            put_row(image, r, out)
            rz, pq, cross = rz + dot_rows(mid, row_of(grad, r)), pq + dot_rows(mid, out), cross + dot_rows(other, out)
    for r in (-1, 0, 1, 2, rows - 3, rows - 2, rows - 1, rows):
        put_row(second_image, r + 1, keep_inside(r, rows, laplace_row(
            row_of(second, r + 1), row_of(second, r + 2), row_of(second, r + 3), map_row(kappa, r + 3), mask)))
    for r in (0, 1, 2, 3, rows - 4, rows - 3, rows - 2, rows - 1):
        mid, out = hessian_row(r, second, r + 2, second_image, 1, kappa, weight, mask)
        put_row(last, r, out)
        total = total + dot_rows(mid, out)
    sums[...] = jnp.zeros_like(sums)
    for k, value in enumerate((rz, pq, cross, total)):
        sums[k : k + 1, :] = jnp.sum(value, axis=0, keepdims=True)


def final_kernel(sums, grad, search, image, second, last, newton_out, residual_out, newton, residual, newton_sem, residual_sem):
    rows, weeks, cols = grad.shape
    rz, pq, cross, total = (jnp.sum(sums[k : k + 1, :], axis=1, keepdims=True) for k in range(4))
    first_step = rz / pq
    rz_next = first_step * first_step * cross - rz
    turn = 1.0 + rz_next / rz
    second_step = rz_next / (turn * (turn * pq - 2.0 * first_step * cross) + first_step * first_step * total)
    along = jnp.broadcast_to(first_step + second_step * turn, (weeks, LANES))
    across = jnp.broadcast_to(second_step * first_step, (weeks, LANES))

    def copies(r):
        return (
            pltpu.make_async_copy(newton.at[r], newton_out.at[:, r, :], newton_sem.at[r]),
            pltpu.make_async_copy(residual.at[r], residual_out.at[:, r, :], residual_sem.at[r]),
        )

    def combine(r, _):
        put_row(newton, r, [along * p - across * y for p, y in zip(row_of(search, r + 4), row_of(second, r + 2))])
        put_row(residual, r, [
            g - along * w + across * h for g, w, h in zip(row_of(grad, r), row_of(image, r), row_of(last, r))])
        for copy in copies(r):
            copy.start()

    row_loop(0, rows, combine, most=8)
    for r in range(rows):
        for copy in copies(r):
            copy.wait()


def call(kernel, outs, ins, scratch=(), aliases=None, limit=2, flops=0, moved=0):
    shapes = tuple(VMEM(shape, F32) if space is VMEM else jax.ShapeDtypeStruct(shape, F32) for shape, space in outs)
    return pl.pallas_call(
        kernel,
        out_shape=shapes,
        in_specs=[pl.BlockSpec(memory_space=space) for _, space in ins],
        out_specs=tuple(pl.BlockSpec(memory_space=space) for _, space in outs),
        scratch_shapes=list(scratch),
        input_output_aliases=aliases or {},
        compiler_params=pltpu.CompilerParams(vmem_limit_bytes=limit * MIB),
        cost_estimate=pl.CostEstimate(flops=flops, bytes_accessed=moved, transcendentals=0),
    )(*[pltpu.with_memory_space_constraint(array, space) if space is pltpu.HBM else array for array, space in ins])


def shards(latent, counts, land_mask, region_ids, kappa_sq, covariates, effects, intercepts):
    weeks, rows, cols = latent.shape
    swap, cross = pair_maps(lax.axis_size(AX))

    def ext(depth):
        return ((rows + 2 * depth, weeks, cols), VMEM)

    def maps(depth):
        return ((rows + 2 * depth, 1, cols), VMEM)

    cells = weeks * rows * cols
    SMEM, ANY, HBM, DMA = pltpu.SMEM, pl.ANY, pltpu.HBM, pltpu.SemaphoreType.DMA
    packed = ((2 * weeks + 8, cols), VMEM)
    near, far, kappa, land = call(
        pack_kernel,
        [packed, packed, maps(3), maps(0)],
        [(latent, HBM), (kappa_sq, VMEM), (land_mask, VMEM)],
        scratch=[DMA((4,))],
        flops=cells // 16, moved=cells,
    )
    old_near, old_far = lax.ppermute(near, AX, swap), lax.ppermute(far, AX, cross)
    field, grad, weight, inv, search, image, eta = call(
        start_kernel,
        [ext(2), ext(0), ext(2), ext(2), ext(4), ext(1), maps(0)],
        [(effects.astype(F32), SMEM), (intercepts, SMEM), (latent, ANY), (counts, HBM), (covariates, HBM),
         (land, VMEM), (region_ids, VMEM), (kappa, VMEM)],
        scratch=[pltpu.VMEM((rows, weeks, cols), jnp.int32), pltpu.VMEM(covariates.shape, covariates.dtype),
                 DMA((rows,)), DMA((rows,)), DMA],
        flops=80 * cells, moved=12 * cells, limit=8,
    )
    packed = ((4 * weeks + 8, cols), VMEM)
    kappa, field, grad, search, image, near, far = call(
        edge_kernel,
        [maps(3), ext(2), ext(0), ext(4), ext(1), packed, packed],
        [(old_near, VMEM), (old_far, VMEM), (eta, VMEM), (inv, VMEM),
         (kappa, VMEM), (field, VMEM), (grad, VMEM), (search, VMEM), (image, VMEM)],
        aliases={4 + k: k for k in range(5)},
        flops=10 * cells, moved=cells,
    )
    near, far = lax.ppermute(near, AX, swap), lax.ppermute(far, AX, cross)
    first, image, second, second_image, last, partial = call(
        inner_kernel,
        [ext(3), ext(0), ext(2), ext(1), ext(0), ((32, LANES), VMEM)],
        [(kappa, VMEM), (grad, VMEM), (weight, VMEM), (inv, VMEM), (search, VMEM)],
        flops=80 * cells, moved=12 * cells,
    )
    weight, inv, search, first, image, second, second_image, last, sums = call(
        outer_kernel,
        [ext(2), ext(2), ext(4), ext(3), ext(0), ext(2), ext(1), ext(0), ((8, LANES), VMEM)],
        [(old_near, VMEM), (old_far, VMEM), (near, VMEM), (far, VMEM), (kappa, VMEM), (field, VMEM),
         (grad, VMEM), (partial, VMEM), (weight, VMEM), (inv, VMEM), (search, VMEM), (first, VMEM), (image, VMEM),
         (second, VMEM), (second_image, VMEM), (last, VMEM)],
        aliases={8 + k: k for k in range(8)},
        flops=20 * cells, moved=cells,
    )
    return call(
        final_kernel,
        [(latent.shape, ANY), (latent.shape, ANY)],
        [(all_sum(sums), VMEM), (grad, VMEM), (search, VMEM), (image, VMEM), (second, VMEM), (last, VMEM)],
        scratch=[pltpu.VMEM((rows, weeks, cols), F32), pltpu.VMEM((rows, weeks, cols), F32), DMA((rows,)), DMA((rows,))],
        flops=8 * cells, moved=8 * cells, limit=6,
    )


def solution(mesh):
    placed = (
        P(None, "gx", "region"),
        P(None, "gx", "region"),
        P("gx", "region"),
        P("gx", "region"),
        P("gx", "region"),
        P(None, "gx", "region"),
        P("region"),
        P("region"),
    )
    return jax.shard_map(
        shards,
        mesh=mesh,
        in_specs=placed,
        out_specs=(P(None, "gx", "region"), P(None, "gx", "region")),
        check_vma=False,
    )
```

time: 62.5 us -> 47.6 us (0.76)
  Pallas kernels: 32.3 us -> 21.5 us
  local copies, waits for them, and re-layouts: 6.02 us -> 1.96 us
  starting transfers between devices: 14.4 us -> 17.6 us
  waiting for transfers between devices: 7.21 us -> 5.59 us
  other arithmetic: 1.34 us -> 0.02 us
    pallas_call x5 -> x6, Pallas kernels: 32.3 us -> 21.5 us  [call(): pl.pallas_call(kernel, out_shape=shapes, in_specs=[pl.BlockSpec(memory_sp...]
    ppermute x4, starting transfers between devices: 5.75 us -> 11.8 us  [all_sum(): lax.ppermute(values, AX, [(i, i ^ step) for i in range(count)])]
    ppermute x4, starting transfers between devices: 8.66 us -> 5.77 us  [the longest x2 4.6 us: shards(): near, far = (lax.ppermute(near, AX, swap), lax.ppermute(far, AX, cross))]
    ppermute x4, waiting for transfers between devices: 7.2 us -> 5.58 us  [all_sum(): lax.ppermute(values, AX, [(i, i ^ step) for i in range(count)])]
    transpose x3 -> x0, local copies, waits for them, and re-layouts: 1.39 us -> none  [pack(): jnp.transpose(wide, (1, 0, 2)).reshape(-1, cols)]
    unnamed x14 -> x12, local copies, waits for them, and re-layouts: 3.2 us -> 1.96 us
    slice x7 -> x0, local copies, waits for them, and re-layouts: 0.97 us -> none  [the longest x2 0.94 us: shards(): head = pack(latent[:, :2], [kappa_sq[:3], land_own[:2]])]
    reshape x1 -> x0, other arithmetic: 0.92 us -> none  [as_map(): return flat.reshape(-1, 1, cols)]
  transfers between devices with their start and end apart: 8 -> 8, of which waited for: 4 -> 4; matrix products, arithmetic and copies ran while one was open for 1% -> 0% of each run, Pallas kernels for 38% -> 33%
where the time goes in v3:
time: 47.6 us; the launch traced here: 47.4 us
  Pallas kernels  21.5 us (45%)
  starting transfers between devices  17.6 us (37%)
  waiting for transfers between devices  5.59 us (12%)
  local copies, waits for them, and re-layouts  1.96 us (4%)
  between operations  0.78 us (2%)
    pallas_call x6, Pallas kernels, call(): pl.pallas_call(kernel, out_shape=shapes, in_specs=[pl.BlockSpec(memory_sp...  21.5 us
    ppermute x4, starting transfers between devices, all_sum(): lax.ppermute(values, AX, [(i, i ^ step) for i in range(count)])  11.8 us
    ppermute x4, waiting for transfers between devices, all_sum(): lax.ppermute(values, AX, [(i, i ^ step) for i in range(count)])  5.58 us
    ppermute x2, starting transfers between devices, shards(): near, far = (lax.ppermute(near, AX, swap), lax.ppermute(far, AX, cross))  4.6 us
    unnamed x12, local copies, waits for them, and re-layouts  1.96 us
  transfers between devices with their start and end apart: 8, of which 4 were waited for; matrix products, arithmetic and copies ran while one was open for 0% of the time, Pallas kernels for 33%

profile of v3, /device:TPU:0, one launch (start us, length us, event | category | flops | bytes accessed | tf_op | source)
XLA Modules:
  0.0 47.4 jit_solution(15480299608514864761)
XLA Ops:
  0.6 0.0 copy-start
  0.6 0.0 copy-start.1
  0.7 1.0 %copy-done.1 = f32[32,1024]{1,0:T(8,128)S(1)} copy-done((f32[32,1024]{1,0:T(8,128)S(1)}, f32[32,1024]{1,0:T(8,128)}, u32[]{:S(2)}) %copy-start.1) | copy-done | bytes 131096
  1.7 0.0 copy-start.2
  1.7 0.9 %copy-done.2 = s32[32,1024]{1,0:T(8,128)S(1)} copy-done((s32[32,1024]{1,0:T(8,128)S(1)}, s32[32,1024]{1,0:T(8,128)}, u32[]{:S(2)}) %copy-start.2) | copy-done | bytes 131096
  2.6 0.0 copy-start.5
  2.6 0.0 copy-start.3
  2.6 0.0 copy-start.4
  2.6 1.0 %shard_map.95 = (f32[40,1024]{1,0:T(8,128)S(1)}, f32[40,1024]{1,0:T(8,128)S(1)}, f32[38,1,1024]{2,1,0:T(1,128)S(1)}, f32[32,1,1024]{2,1,0:T(1,128)S(1)}) custom-call(f32[16,32,1024]{2,1,0:T(8,128)} %latent.3, f32[32,1024]{1,0:T(8,128)S(1)} %copy-done.1, s32[32,1024]{1,0:T(8,128)S(1)} %copy-done.2), custom_call_target="tpu_custom_call" | custom-call | flops 32768 | bytes 524288 | tf_op jit(solution)/shard_map/pallas_call | solution.py:388
  3.7 0.5 %collective-permute-start = (f32[40,1024]{1,0:T(8,128)S(1)}, f32[40,1024]{1,0:T(8,128)S(1)}, u32[]{:S(2)}, u32[]{:S(2)}) collective-permute-start(f32[40,1024]{1,0:T(8,128)S(1)} %get-tuple-element.30), channel_id=1, source_target_pairs={{0,1},{1,0},{2,3},{3,2},{4,5},{5,4},{6,7},{7,6},{8,9},{9,8},{10,11... | collective-permute-start | bytes 491528 | tf_op jit(solution)/shard_map/ppermute | solution.py:420
  4.2 0.7 %collective-permute-start.1 = (f32[40,1024]{1,0:T(8,128)S(1)}, f32[40,1024]{1,0:T(8,128)S(1)}, u32[]{:S(2)}, u32[]{:S(2)}) collective-permute-start(f32[40,1024]{1,0:T(8,128)S(1)} %get-tuple-element.31), channel_id=1, source_target_pairs={{1,2},{2,1},{3,4},{4,3},{5,6},{6,5},{7,8},{8,7},{9,10},{10,9},{11,... | collective-permute-start | bytes 491528 | tf_op jit(solution)/shard_map/ppermute | solution.py:420
  4.8 0.0 copy-done.5
  4.9 0.0 copy-done
  4.9 0.0 copy-done.3
  4.9 0.0 copy-done.4
  4.9 10.0 %shard_map.96 = (f32[36,16,1024]{2,1,0:T(8,128)S(1)}, f32[32,16,1024]{2,1,0:T(8,128)S(1)}, f32[36,16,1024]{2,1,0:T(8,128)S(1)}, f32[36,16,1024]{2,1,0:T(8,128)S(...) custom-call(f32[32]{0:T(128)S(1)} %convert_element_type.3.effects, ...), custom_call_target="tpu_custom_call" | custom-call | flops 41943040 | bytes 6291456 | tf_op jit(solution)/shard_map/pallas_call | solution.py:388
  14.9 0.0 collective-permute-done.got_first.old_first
  14.9 0.0 collective-permute-done.1.got_second.old_second
  14.9 0.4 shard_map.97
  15.3 3.9 %collective-permute-start.2 = (f32[72,1024]{1,0:T(8,128)S(1)}, f32[72,1024]{1,0:T(8,128)S(1)}, u32[]{:S(2)}, u32[]{:S(2)}) collective-permute-start(f32[72,1024]{1,0:T(8,128)S(1)} %get-tuple-element.40), channel_id=1, source_target_pairs={{0,1},{1,0},{2,3},{3,2},{4,5},{5,4},{6,7},{7,6},{8,9},{9,8},{10,11... | collective-permute-start | bytes 884744 | tf_op jit(solution)/shard_map/ppermute | solution.py:439
  19.3 0.7 %collective-permute-start.3 = (f32[72,1024]{1,0:T(8,128)S(1)}, f32[72,1024]{1,0:T(8,128)S(1)}, u32[]{:S(2)}, u32[]{:S(2)}) collective-permute-start(f32[72,1024]{1,0:T(8,128)S(1)} %get-tuple-element.41), channel_id=1, source_target_pairs={{1,2},{2,1},{3,4},{4,3},{5,6},{6,5},{7,8},{8,7},{9,10},{10,9},{11,... | collective-permute-start | bytes 884744 | tf_op jit(solution)/shard_map/ppermute | solution.py:439
  19.9 5.7 %shard_map.98 = (f32[38,16,1024]{2,1,0:T(8,128)S(1)}, f32[32,16,1024]{2,1,0:T(8,128)S(1)}, f32[36,16,1024]{2,1,0:T(8,128)S(1)}, f32[34,16,1024]{2,1,0:T(8,128)S(...) custom-call(f32[38,1,1024]{2,1,0:T(1,128)S(1)} %get-tuple-element.42.kappa, ...), custom_call_target="tpu_custom_call" | custom-call | flops 41943040 | bytes 6291456 | tf_op jit(solution)/shard_map/pallas_call | solution.py:388
  25.7 0.0 collective-permute-done.2.got_first
  25.7 0.0 collective-permute-done.3.got_second
  25.7 1.7 %shard_map.99 = (f32[36,16,1024]{2,1,0:T(8,128)S(1)}, f32[36,16,1024]{2,1,0:T(8,128)S(1)}, f32[40,16,1024]{2,1,0:T(8,128)S(1)}, f32[38,16,1024]{2,1,0:T(8,128)S(...) custom-call(f32[40,1024]{1,0:T(8,128)S(1)} %collective-permute-done., ...), custom_call_target="tpu_custom_call", output_to_operand_aliasing={{0}: (8, {}), {1}: (9, {}), {2}: (10, {}), {3}: (11, {}), {... | custom-call | flops 10485760 | bytes 524288 | tf_op jit(solution)/shard_map/pallas_call | solution.py:388
  27.4 4.0 %collective-permute-start.4 = (f32[8,128]{1,0:T(8,128)S(1)}, f32[8,128]{1,0:T(8,128)S(1)}, u32[]{:S(2)}, u32[]{:S(2)}) collective-permute-start(f32[8,128]{1,0:T(8,128)S(1)} %get-tuple-element.53), channel_id=1, source_target_pairs={{0,1},{1,0},{2,3},{3,2},{4,5},{5,4},{6,7},{7,6},{8,9},{9,8},{10,11... | collective-permute-start | bytes 12296 | tf_op jit(solution)/shard_map/ppermute | solution.py:31
  31.4 0.8 %collective-permute-done.4 = f32[8,128]{1,0:T(8,128)S(1)} collective-permute-done((f32[8,128]{1,0:T(8,128)S(1)}, f32[8,128]{1,0:T(8,128)S(1)}, u32[]{:S(2)}, u32[]{:S(2)}) %collective-permute-start.4) | collective-permute-done | bytes 4128 | tf_op jit(solution)/shard_map/ppermute | solution.py:31
  32.2 2.7 %collective-permute-start.5 = (f32[8,128]{1,0:T(8,128)S(1)}, f32[8,128]{1,0:T(8,128)S(1)}, u32[]{:S(2)}, u32[]{:S(2)}) collective-permute-start(f32[8,128]{1,0:T(8,128)S(1)} %add.12), channel_id=1, source_target_pairs={{0,2},{1,3},{2,0},{3,1},{4,6},{5,7},{6,4},{7,5},{8,10},{9,11},{10,... | collective-permute-start | bytes 12296 | tf_op jit(solution)/shard_map/ppermute | solution.py:31
  34.9 1.6 %collective-permute-done.5 = f32[8,128]{1,0:T(8,128)S(1)} collective-permute-done((f32[8,128]{1,0:T(8,128)S(1)}, f32[8,128]{1,0:T(8,128)S(1)}, u32[]{:S(2)}, u32[]{:S(2)}) %collective-permute-start.5) | collective-permute-done | bytes 4128 | tf_op jit(solution)/shard_map/ppermute | solution.py:31
  36.5 2.1 %collective-permute-start.6 = (f32[8,128]{1,0:T(8,128)S(1)}, f32[8,128]{1,0:T(8,128)S(1)}, u32[]{:S(2)}, u32[]{:S(2)}) collective-permute-start(f32[8,128]{1,0:T(8,128)S(1)} %add.13), channel_id=1, source_target_pairs={{0,4},{1,5},{2,6},{3,7},{4,0},{5,1},{6,2},{7,3},{8,12},{9,13},{10,... | collective-permute-start | bytes 12296 | tf_op jit(solution)/shard_map/ppermute | solution.py:31
  38.6 1.6 %collective-permute-done.6 = f32[8,128]{1,0:T(8,128)S(1)} collective-permute-done((f32[8,128]{1,0:T(8,128)S(1)}, f32[8,128]{1,0:T(8,128)S(1)}, u32[]{:S(2)}, u32[]{:S(2)}) %collective-permute-start.6) | collective-permute-done | bytes 4128 | tf_op jit(solution)/shard_map/ppermute | solution.py:31
  40.2 3.0 %collective-permute-start.7 = (f32[8,128]{1,0:T(8,128)S(1)}, f32[8,128]{1,0:T(8,128)S(1)}, u32[]{:S(2)}, u32[]{:S(2)}) collective-permute-start(f32[8,128]{1,0:T(8,128)S(1)} %add.14), channel_id=1, source_target_pairs={{0,8},{1,9},{2,10},{3,11},{4,12},{5,13},{6,14},{7,15},{8,0},{9,1},... | collective-permute-start | bytes 12296 | tf_op jit(solution)/shard_map/ppermute | solution.py:31
  43.2 1.6 %collective-permute-done.7 = f32[8,128]{1,0:T(8,128)S(1)} collective-permute-done((f32[8,128]{1,0:T(8,128)S(1)}, f32[8,128]{1,0:T(8,128)S(1)}, u32[]{:S(2)}, u32[]{:S(2)}) %collective-permute-start.7) | collective-permute-done | bytes 4128 | tf_op jit(solution)/shard_map/ppermute | solution.py:31
  44.8 2.7 %shard_map.100 = (f32[16,32,1024]{2,1,0:T(8,128)}, f32[16,32,1024]{2,1,0:T(8,128)}) custom-call(f32[8,128]{1,0:T(8,128)S(1)} %add.15.sums, f32[32,16,1024]{2,1,0:T(8,128)S(1)} %get-tuple-element.44.grad, f32[40,16,1024]{2,1,0:T(8,128)S(1)} %get-tuple-element.54.search, f32[32,16,1024]{2,1,0:T(8,128)S(1)} %get-tuple-element.55.image, ...), custom_call_target="tpu_custom_call" | custom-call | flops 4194304 | bytes 4194304 | tf_op jit(solution)/shard_map/pallas_call | solution.py:388
  (5 shorter events, 0.0 us)
Async XLA Ops:
  0.6 4.2 %copy-start = (f32[16,32,1024]{2,1,0:T(8,128)S(1)}, f32[16,32,1024]{2,1,0:T(8,128)}, u32[]{:S(2)}) copy-start(f32[16,32,1024]{2,1,0:T(8,128)} %latent.3) | copy-start | bytes 6291460
  0.6 1.1 %copy-start.1 = (f32[32,1024]{1,0:T(8,128)S(1)}, f32[32,1024]{1,0:T(8,128)}, u32[]{:S(2)}) copy-start(f32[32,1024]{1,0:T(8,128)} %kappa.1) | copy-start | bytes 393220
  1.7 0.9 %copy-start.2 = (s32[32,1024]{1,0:T(8,128)S(1)}, s32[32,1024]{1,0:T(8,128)}, u32[]{:S(2)}) copy-start(s32[32,1024]{1,0:T(8,128)} %land.1) | copy-start | bytes 393220
  2.6 2.2 %copy-start.5 = (bf16[32]{0:T(256)(128)(2,1)S(1)}, bf16[32]{0:T(256)(128)(2,1)}, u32[]{:S(2)}) copy-start(bf16[32]{0:T(256)(128)(2,1)} %param.14) | copy-start | bytes 196
  2.6 2.3 %copy-start.3 = (s32[32,1024]{1,0:T(8,128)S(1)}, s32[32,1024]{1,0:T(8,128)}, u32[]{:S(2)}) copy-start(s32[32,1024]{1,0:T(8,128)} %zones.1) | copy-start | bytes 393220
  2.6 2.3 %copy-start.4 = (f32[8]{0:T(128)S(1)}, f32[8]{0:T(128)}, u32[]{:S(2)}) copy-start(f32[8]{0:T(128)} %intercepts.1) | copy-start | bytes 100
  3.7 11.2 %collective-permute-start = (f32[40,1024]{1,0:T(8,128)S(1)}, f32[40,1024]{1,0:T(8,128)S(1)}, u32[]{:S(2)}, u32[]{:S(2)}) collective-permute-start(f32[40,1024]{1,0:T(8,128)S(1)} %get-tuple-element.30), channel_id=1, source_target_pairs={{0,1},{1,0},{2,3},{3,2},{4,5},{5,4},{6,7},{7,6},{8,9},{9,8},{10,11... | collective-permute-start | bytes 491528 | tf_op jit(solution)/shard_map/ppermute | solution.py:420
  4.2 10.7 %collective-permute-start.1 = (f32[40,1024]{1,0:T(8,128)S(1)}, f32[40,1024]{1,0:T(8,128)S(1)}, u32[]{:S(2)}, u32[]{:S(2)}) collective-permute-start(f32[40,1024]{1,0:T(8,128)S(1)} %get-tuple-element.31), channel_id=1, source_target_pairs={{1,2},{2,1},{3,4},{4,3},{5,6},{6,5},{7,8},{8,7},{9,10},{10,9},{11,... | collective-permute-start | bytes 491528 | tf_op jit(solution)/shard_map/ppermute | solution.py:420
  15.3 10.3 %collective-permute-start.2 = (f32[72,1024]{1,0:T(8,128)S(1)}, f32[72,1024]{1,0:T(8,128)S(1)}, u32[]{:S(2)}, u32[]{:S(2)}) collective-permute-start(f32[72,1024]{1,0:T(8,128)S(1)} %get-tuple-element.40), channel_id=1, source_target_pairs={{0,1},{1,0},{2,3},{3,2},{4,5},{5,4},{6,7},{7,6},{8,9},{9,8},{10,11... | collective-permute-start | bytes 884744 | tf_op jit(solution)/shard_map/ppermute | solution.py:439
  19.3 6.4 %collective-permute-start.3 = (f32[72,1024]{1,0:T(8,128)S(1)}, f32[72,1024]{1,0:T(8,128)S(1)}, u32[]{:S(2)}, u32[]{:S(2)}) collective-permute-start(f32[72,1024]{1,0:T(8,128)S(1)} %get-tuple-element.41), channel_id=1, source_target_pairs={{1,2},{2,1},{3,4},{4,3},{5,6},{6,5},{7,8},{8,7},{9,10},{10,9},{11,... | collective-permute-start | bytes 884744 | tf_op jit(solution)/shard_map/ppermute | solution.py:439
  27.4 4.8 %collective-permute-start.4 = (f32[8,128]{1,0:T(8,128)S(1)}, f32[8,128]{1,0:T(8,128)S(1)}, u32[]{:S(2)}, u32[]{:S(2)}) collective-permute-start(f32[8,128]{1,0:T(8,128)S(1)} %get-tuple-element.53), channel_id=1, source_target_pairs={{0,1},{1,0},{2,3},{3,2},{4,5},{5,4},{6,7},{7,6},{8,9},{9,8},{10,11... | collective-permute-start | bytes 12296 | tf_op jit(solution)/shard_map/ppermute | solution.py:31
  32.2 4.3 %collective-permute-start.5 = (f32[8,128]{1,0:T(8,128)S(1)}, f32[8,128]{1,0:T(8,128)S(1)}, u32[]{:S(2)}, u32[]{:S(2)}) collective-permute-start(f32[8,128]{1,0:T(8,128)S(1)} %add.12), channel_id=1, source_target_pairs={{0,2},{1,3},{2,0},{3,1},{4,6},{5,7},{6,4},{7,5},{8,10},{9,11},{10,... | collective-permute-start | bytes 12296 | tf_op jit(solution)/shard_map/ppermute | solution.py:31
  36.5 3.7 %collective-permute-start.6 = (f32[8,128]{1,0:T(8,128)S(1)}, f32[8,128]{1,0:T(8,128)S(1)}, u32[]{:S(2)}, u32[]{:S(2)}) collective-permute-start(f32[8,128]{1,0:T(8,128)S(1)} %add.13), channel_id=1, source_target_pairs={{0,4},{1,5},{2,6},{3,7},{4,0},{5,1},{6,2},{7,3},{8,12},{9,13},{10,... | collective-permute-start | bytes 12296 | tf_op jit(solution)/shard_map/ppermute | solution.py:31
  40.2 4.6 %collective-permute-start.7 = (f32[8,128]{1,0:T(8,128)S(1)}, f32[8,128]{1,0:T(8,128)S(1)}, u32[]{:S(2)}, u32[]{:S(2)}) collective-permute-start(f32[8,128]{1,0:T(8,128)S(1)} %add.14), channel_id=1, source_target_pairs={{0,8},{1,9},{2,10},{3,11},{4,12},{5,13},{6,14},{7,15},{8,0},{9,1},... | collective-permute-start | bytes 12296 | tf_op jit(solution)/shard_map/ppermute | solution.py:31

commit v4 on v3

--- a/solution.py
+++ b/solution.py
@@ -104,16 +104,19 @@
     return lax.fori_loop(0, count // step, chunk, carry)
 
 
-def pack_kernel(latent, kappa, land, first, second, kappa_out, land_out, sems):
+def pack_kernel(latent, kappa_hbm, land_hbm, first, second, kappa_out, land_out, kappa, land, sems):
     weeks, rows, cols = latent.shape
     odd = is_odd()
+    map_copies = [pltpu.make_async_copy(kappa_hbm, kappa, sems.at[4]), pltpu.make_async_copy(land_hbm, land, sems.at[5])]
     copies = []
     for k, (out, base) in enumerate(((first, jnp.where(odd, 0, rows - 2)), (second, jnp.where(odd, rows - 2, 0)))):
         for d in range(2):
             copies.append(pltpu.make_async_copy(
                 latent.at[:, base + d, :], out.at[d * weeks : (d + 1) * weeks, :], sems.at[2 * k + d]))
-    for copy in copies:
+    for copy in map_copies + copies:
         copy.start()
+    for copy in map_copies:
+        copy.wait()
     for r in range(rows):
         kappa_out[r + 3] = kappa[r : r + 1, :]
         land_out[r] = land[r : r + 1, :].astype(F32)
@@ -132,30 +135,25 @@
         copy.wait()
 
 
-def start_kernel(effects, intercepts, latent, counts, covariates, land, zones, kappa,
-                 field, grad, weight, inv, search, image, eta,
-                 tally, covs, field_sem, tally_sem, cov_sem):
+def rows_first(source, target, shift):
+    weeks, rows, cols = source.shape
+    for r in range(0, rows, 8):
+        for c in range(0, cols, LANES):
+            block = source[:, r : r + 8, c : c + LANES].astype(F32)
+            target[r + shift : r + shift + 8, :, c : c + LANES] = jnp.swapaxes(block, 0, 1)
+
+
+def front_kernel(effects, intercepts, latent, covariates, zones, kappa, counts,
+                 field, image, eta, tally, covs, raw, cov_sem, sem):
     weeks, rows, cols = latent.shape
-    num_covs = covariates.shape[0]
     mask = masks(weeks)
-
-    def field_copy(r):
-        return pltpu.make_async_copy(latent.at[:, r, :], field.at[r + 2], field_sem.at[r])
-
-    def tally_copy(r):
-        return pltpu.make_async_copy(counts.at[:, r, :], tally.at[r], tally_sem.at[r])
-
+    copy = pltpu.make_async_copy(counts, raw, sem)
     cov_copy = pltpu.make_async_copy(covariates, covs, cov_sem)
-    for r in range(rows):
-        field_copy(r).start()
     cov_copy.start()
-    for r in range(rows):
-        tally_copy(r).start()
-    field_copy(0).wait()
-    field_copy(1).wait()
+    copy.start()
+    rows_first(latent, field, 2)
 
     def inner_image(r, _):
-        field_copy(r + 1).wait()
         put_row(image, r + 1, laplace_row(
             row_of(field, r + 1), row_of(field, r + 2), row_of(field, r + 3), map_row(kappa, r + 3), mask))
 
@@ -167,37 +165,29 @@
         ids = zones[:, c : c + width]
         for z in range(intercepts.shape[0]):
             total = jnp.where(ids == z, intercepts[z], total)
-        for k in range(num_covs):
+        for k in range(covs.shape[0]):
             total = total + effects[k] * covs[k, :, c : c + width].astype(F32)
         for r in range(rows):
             eta[r, :, c : c + width] = total[r : r + 1]
-
-    def pointwise(r):
-        tally_copy(r).wait()
-        lat, eta_row, land_row, kap, count_row = (
-            row_of(field, r + 2), map_row(eta, r), map_row(land, r), map_row(kappa, r + 3), row_of(tally, r))
-        out, heavy, inverse = [], [], []
-        for j, tile in enumerate(lat):
-            on = land_row[j]
-            curve = jnp.tanh(0.5 * (tile + eta_row[j]))
-            heavy.append(on * (1.0 - curve * curve))
-            inverse.append(1.0 / (diag_base(kap[j]) + heavy[j]))
-            out.append(on * (count_row[j].astype(F32) - 2.0 - 2.0 * curve) - time_coupling * temporal_tile(tile, mask))
-        put_row(weight, r + 2, heavy)
-        put_row(inv, r + 2, inverse)
-        return out, inverse, kap
-
-    for r in (0, 1, rows - 2, rows - 1):
-        put_row(grad, r, pointwise(r)[0])
-
-    def gradient(r, _):
-        out, inverse, kap = pointwise(r)
-        outer = laplace_row(row_of(image, r), row_of(image, r + 1), row_of(image, r + 2), kap, mask)
-        out = [a - prior_scale * b for a, b in zip(out, outer)]
-        put_row(grad, r, out)
-        put_row(search, r + 4, [a * b for a, b in zip(out, inverse)])
-
-    row_loop(2, rows - 2, gradient, most=7)
+    copy.wait()
+    rows_first(raw, tally, 0)
+
+
+def gradient_row(r, field, tally, eta, land, kappa, image, grad, weight, inv, search, mask):
+    outer = laplace_row(row_of(image, r), row_of(image, r + 1), row_of(image, r + 2), map_row(kappa, r + 3), mask)
+    eta_row, land_row, kap, count_row = map_row(eta, r), map_row(land, r), map_row(kappa, r + 3), row_of(tally, r)
+    for j, tile in enumerate(row_of(field, r + 2)):
+        on = land_row[j]
+        curve = jnp.tanh(0.5 * (tile + eta_row[j]))
+        heavy = on * (1.0 - curve * curve)
+        inverse = 1.0 / (diag_base(kap[j]) + heavy)
+        out = on * (count_row[j] - 2.0 - 2.0 * curve) - time_coupling * temporal_tile(tile, mask)
+        out = out - prior_scale * outer[j]
+        part = slice(j * LANES, (j + 1) * LANES)
+        weight[r + 2, :, part] = heavy
+        inv[r + 2, :, part] = inverse
+        grad[r, :, part] = out
+        search[r + 4, :, part] = out * inverse
 
 
 def keep_inside(r, rows, tiles):
@@ -223,8 +213,8 @@
             for c in range(0, first.shape[1], LANES)]
 
 
-def edge_kernel(got_first, got_second, eta, inv, kappa_in, field_in, grad_in, search_in, image_in,
-                kappa, field, grad, search, image, first, second):
+def edge_kernel(got_first, got_second, eta, land, tally, kappa_in, field_in, image_in,
+                kappa, field, image, grad, weight, inv, search, first, second):
     weeks = field.shape[1]
     rows, _, cols = eta.shape
     mask = masks(weeks)
@@ -238,11 +228,8 @@
     for r in (-1, 0, rows - 1, rows):
         put_row(image, r + 1, keep_inside(r, rows, laplace_row(
             row_of(field, r + 1), row_of(field, r + 2), row_of(field, r + 3), map_row(kappa, r + 3), mask)))
-    for r in (0, 1, rows - 2, rows - 1):
-        outer = laplace_row(row_of(image, r), row_of(image, r + 1), row_of(image, r + 2), map_row(kappa, r + 3), mask)
-        out = [a - prior_scale * b for a, b in zip(row_of(grad, r), outer)]
-        put_row(grad, r, out)
-        put_row(search, r + 4, [a * b for a, b in zip(out, row_of(inv, r + 2))])
+    for r in (0, 1, 2, 3, rows - 4, rows - 3, rows - 2, rows - 1):
+        gradient_row(r, field, tally, eta, land, kappa, image, grad, weight, inv, search, mask)
     at = 4 * weeks
     for c in range(0, cols, LANES):
         part = slice(c, c + LANES)
@@ -272,10 +259,16 @@
     return fold([x * y for x, y in zip(a, b)])
 
 
-def inner_kernel(kappa, grad, weight, inv, search, first, image, second, second_image, last, sums):
+def inner_kernel(kappa, eta, land, tally, field, start_image, grad_in, weight_in, inv_in, search_in,
+                 grad, weight, inv, search, first, image, second, second_image, last, sums):
     weeks = grad.shape[1]
     rows = grad.shape[0]
     mask = masks(weeks)
+
+    def gradient(r, _):
+        gradient_row(r, field, tally, eta, land, kappa, start_image, grad, weight, inv, search, mask)
+
+    row_loop(4, rows - 4, gradient, most=8)
 
     def inner_image(r, _):
         put_row(first, r + 3, laplace_row(
@@ -413,35 +406,36 @@
     near, far, kappa, land = call(
         pack_kernel,
         [packed, packed, maps(3), maps(0)],
-        [(latent, HBM), (kappa_sq, VMEM), (land_mask, VMEM)],
-        scratch=[DMA((4,))],
+        [(latent, HBM), (kappa_sq, HBM), (land_mask, HBM)],
+        scratch=[pltpu.VMEM((rows, cols), F32), pltpu.VMEM((rows, cols), jnp.int32), DMA((6,))],
         flops=cells // 16, moved=cells,
     )
     old_near, old_far = lax.ppermute(near, AX, swap), lax.ppermute(far, AX, cross)
-    field, grad, weight, inv, search, image, eta = call(
-        start_kernel,
-        [ext(2), ext(0), ext(2), ext(2), ext(4), ext(1), maps(0)],
-        [(effects.astype(F32), SMEM), (intercepts, SMEM), (latent, ANY), (counts, HBM), (covariates, HBM),
-         (land, VMEM), (region_ids, VMEM), (kappa, VMEM)],
-        scratch=[pltpu.VMEM((rows, weeks, cols), jnp.int32), pltpu.VMEM(covariates.shape, covariates.dtype),
-                 DMA((rows,)), DMA((rows,)), DMA],
-        flops=80 * cells, moved=12 * cells, limit=8,
+    field, image, eta, tally = call(
+        front_kernel,
+        [ext(2), ext(1), maps(0), ext(0)],
+        [(effects.astype(F32), SMEM), (intercepts, SMEM), (latent, VMEM), (covariates, HBM),
+         (region_ids, VMEM), (kappa, VMEM), (counts, HBM)],
+        scratch=[pltpu.VMEM(covariates.shape, covariates.dtype), pltpu.VMEM(counts.shape, jnp.int32), DMA, DMA],
+        flops=40 * cells, moved=12 * cells, limit=8,
     )
     packed = ((4 * weeks + 8, cols), VMEM)
-    kappa, field, grad, search, image, near, far = call(
+    kappa, field, image, grad, weight, inv, search, near, far = call(
         edge_kernel,
-        [maps(3), ext(2), ext(0), ext(4), ext(1), packed, packed],
-        [(old_near, VMEM), (old_far, VMEM), (eta, VMEM), (inv, VMEM),
-         (kappa, VMEM), (field, VMEM), (grad, VMEM), (search, VMEM), (image, VMEM)],
-        aliases={4 + k: k for k in range(5)},
+        [maps(3), ext(2), ext(1), ext(0), ext(2), ext(2), ext(4), packed, packed],
+        [(old_near, VMEM), (old_far, VMEM), (eta, VMEM), (land, VMEM), (tally, VMEM),
+         (kappa, VMEM), (field, VMEM), (image, VMEM)],
+        aliases={5 + k: k for k in range(3)},
         flops=10 * cells, moved=cells,
     )
     near, far = lax.ppermute(near, AX, swap), lax.ppermute(far, AX, cross)
-    first, image, second, second_image, last, partial = call(
+    grad, weight, inv, search, first, image, second, second_image, last, partial = call(
         inner_kernel,
-        [ext(3), ext(0), ext(2), ext(1), ext(0), ((32, LANES), VMEM)],
-        [(kappa, VMEM), (grad, VMEM), (weight, VMEM), (inv, VMEM), (search, VMEM)],
-        flops=80 * cells, moved=12 * cells,
+        [ext(0), ext(2), ext(2), ext(4), ext(3), ext(0), ext(2), ext(1), ext(0), ((32, LANES), VMEM)],
+        [(kappa, VMEM), (eta, VMEM), (land, VMEM), (tally, VMEM), (field, VMEM), (image, VMEM),
+         (grad, VMEM), (weight, VMEM), (inv, VMEM), (search, VMEM)],
+        aliases={6 + k: k for k in range(4)},
+        flops=120 * cells, moved=12 * cells,
     )
     weight, inv, search, first, image, second, second_image, last, sums = call(
         outer_kernel,

time: 47.6 us -> 41.2 us (0.87)
  Pallas kernels: 21.5 us -> 17.1 us
  local copies, waits for them, and re-layouts: 1.96 us -> 0.02 us
    pallas_call x6, Pallas kernels: 21.5 us -> 17.1 us  [call(): pl.pallas_call(kernel, out_shape=shapes, in_specs=[pl.BlockSpec(memory_sp...]
    unnamed x12 -> x8, local copies, waits for them, and re-layouts: 1.96 us -> 0.02 us
  transfers between devices with their start and end apart: 8 -> 8, of which waited for: 4 -> 4; matrix products, arithmetic and copies ran while one was open for 0% -> 0% of each run, Pallas kernels for 33% -> 26%
where the time goes in v4:
time: 41.2 us; the launch traced here: 41.1 us
  starting transfers between devices  17.5 us (42%)
  Pallas kernels  17.1 us (42%)
  waiting for transfers between devices  5.6 us (14%)
  between operations  0.79 us (2%)
    pallas_call x6, Pallas kernels, call(): pl.pallas_call(kernel, out_shape=shapes, in_specs=[pl.BlockSpec(memory_sp...  17.1 us
    ppermute x4, starting transfers between devices, all_sum(): lax.ppermute(values, AX, [(i, i ^ step) for i in range(count)])  11.7 us
    ppermute x4, waiting for transfers between devices, all_sum(): lax.ppermute(values, AX, [(i, i ^ step) for i in range(count)])  5.59 us
    ppermute x2, starting transfers between devices, shards(): near, far = (lax.ppermute(near, AX, swap), lax.ppermute(far, AX, cross))  4.6 us
  transfers between devices with their start and end apart: 8, of which 4 were waited for; matrix products, arithmetic and copies ran while one was open for 0% of the time, Pallas kernels for 26%

profile of v4, /device:TPU:0, one launch (start us, length us, event | category | flops | bytes accessed | tf_op | source)
XLA Modules:
  0.0 41.1 jit_solution(6256921053523301528)
XLA Ops:
  0.6 0.0 copy-start
  0.6 0.0 copy-start.3
  0.7 0.0 copy-start.2
  0.7 0.0 copy-start.1
  0.7 1.3 %shard_map.95 = (f32[40,1024]{1,0:T(8,128)S(1)}, f32[40,1024]{1,0:T(8,128)S(1)}, f32[38,1,1024]{2,1,0:T(1,128)S(1)}, f32[32,1,1024]{2,1,0:T(1,128)S(1)}) custom-call(f32[16,32,1024]{2,1,0:T(8,128)} %latent.3, f32[32,1024]{1,0:T(8,128)} %kappa_hbm.1, s32[32,1024]{1,0:T(8,128)} %land_hbm.1), custom_call_target="tpu_custom_call" | custom-call | flops 32768 | bytes 524288 | tf_op jit(solution)/shard_map/pallas_call | solution.py:381
  2.0 0.5 %collective-permute-start = (f32[40,1024]{1,0:T(8,128)S(1)}, f32[40,1024]{1,0:T(8,128)S(1)}, u32[]{:S(2)}, u32[]{:S(2)}) collective-permute-start(f32[40,1024]{1,0:T(8,128)S(1)} %get-tuple-element.34), channel_id=1, source_target_pairs={{0,1},{1,0},{2,3},{3,2},{4,5},{5,4},{6,7},{7,6},{8,9},{9,8},{10,11... | collective-permute-start | bytes 491528 | tf_op jit(solution)/shard_map/ppermute | solution.py:413
  2.5 0.7 %collective-permute-start.1 = (f32[40,1024]{1,0:T(8,128)S(1)}, f32[40,1024]{1,0:T(8,128)S(1)}, u32[]{:S(2)}, u32[]{:S(2)}) collective-permute-start(f32[40,1024]{1,0:T(8,128)S(1)} %get-tuple-element.35), channel_id=1, source_target_pairs={{1,2},{2,1},{3,4},{4,3},{5,6},{6,5},{7,8},{8,7},{9,10},{10,9},{11,... | collective-permute-start | bytes 491528 | tf_op jit(solution)/shard_map/ppermute | solution.py:413
  3.2 0.0 copy-done.3
  3.2 0.0 copy-done
  3.2 0.0 copy-done.2
  3.2 0.0 copy-done.1
  3.2 3.2 %shard_map.96 = (f32[36,16,1024]{2,1,0:T(8,128)S(1)}, f32[34,16,1024]{2,1,0:T(8,128)S(1)}, f32[32,1,1024]{2,1,0:T(1,128)S(1)}, f32[32,16,1024]{2,1,0:T(8,128)S(1)}) custom-call(f32[32]{0:T(128)S(1)} %convert_element_type.3.effects, f32[8]{0:T(128)S(1)} %copy-done.2, f32[16,32,1024]{2,1,0:T(8,128)S(1)} %copy-done, bf16[32,32,1024]{2,1,0:T(8,128)(2,1)} %covariates.1, ...), custom_call_target="tpu_custom_call" | custom-call | flops 20971520 | bytes 6291456 | tf_op jit(solution)/shard_map/pallas_call | solution.py:381
  6.4 0.0 collective-permute-done.got_first.old_first
  6.4 0.0 collective-permute-done.1.got_second.old_second
  6.4 0.9 %shard_map.97 = (f32[38,1,1024]{2,1,0:T(1,128)S(1)}, f32[36,16,1024]{2,1,0:T(8,128)S(1)}, f32[34,16,1024]{2,1,0:T(8,128)S(1)}, f32[32,16,1024]{2,1,0:T(8,128)S(1...) custom-call(f32[40,1024]{1,0:T(8,128)S(1)} %collective-permute-done., ...), custom_call_target="tpu_custom_call", output_to_operand_aliasing={{0}: (5, {}), {1}: (6, {}), {2}: (7, {})} | custom-call | flops 5242880 | bytes 524288 | tf_op jit(solution)/shard_map/pallas_call | solution.py:381
  7.3 3.9 %collective-permute-start.2 = (f32[72,1024]{1,0:T(8,128)S(1)}, f32[72,1024]{1,0:T(8,128)S(1)}, u32[]{:S(2)}, u32[]{:S(2)}) collective-permute-start(f32[72,1024]{1,0:T(8,128)S(1)} %get-tuple-element.42), channel_id=1, source_target_pairs={{0,1},{1,0},{2,3},{3,2},{4,5},{5,4},{6,7},{7,6},{8,9},{9,8},{10,11... | collective-permute-start | bytes 884744 | tf_op jit(solution)/shard_map/ppermute | solution.py:431
  11.2 0.7 %collective-permute-start.3 = (f32[72,1024]{1,0:T(8,128)S(1)}, f32[72,1024]{1,0:T(8,128)S(1)}, u32[]{:S(2)}, u32[]{:S(2)}) collective-permute-start(f32[72,1024]{1,0:T(8,128)S(1)} %get-tuple-element.43), channel_id=1, source_target_pairs={{1,2},{2,1},{3,4},{4,3},{5,6},{6,5},{7,8},{8,7},{9,10},{10,9},{11,... | collective-permute-start | bytes 884744 | tf_op jit(solution)/shard_map/ppermute | solution.py:431
  11.9 7.5 %shard_map.98 = (f32[32,16,1024]{2,1,0:T(8,128)S(1)}, f32[36,16,1024]{2,1,0:T(8,128)S(1)}, f32[36,16,1024]{2,1,0:T(8,128)S(1)}, f32[40,16,1024]{2,1,0:T(8,128)S(...) custom-call(f32[38,1,1024]{2,1,0:T(1,128)S(1)} %get-tuple-element.44, ...), custom_call_target="tpu_custom_call", output_to_operand_aliasing={{0}: (6, {}), {1}: (7, {}), {2}: (8, {}), {3}: (9, {})} | custom-call | flops 62914560 | bytes 6291456 | tf_op jit(solution)/shard_map/pallas_call | solution.py:381
  19.4 0.0 collective-permute-done.2.got_first
  19.5 0.0 collective-permute-done.3.got_second
  19.5 1.6 %shard_map.99 = (f32[36,16,1024]{2,1,0:T(8,128)S(1)}, f32[36,16,1024]{2,1,0:T(8,128)S(1)}, f32[40,16,1024]{2,1,0:T(8,128)S(1)}, f32[38,16,1024]{2,1,0:T(8,128)S(...) custom-call(f32[40,1024]{1,0:T(8,128)S(1)} %collective-permute-done., ...), custom_call_target="tpu_custom_call", output_to_operand_aliasing={{0}: (8, {}), {1}: (9, {}), {2}: (10, {}), {3}: (11, {}), {... | custom-call | flops 10485760 | bytes 524288 | tf_op jit(solution)/shard_map/pallas_call | solution.py:381
  21.1 4.5 %collective-permute-start.4 = (f32[8,128]{1,0:T(8,128)S(1)}, f32[8,128]{1,0:T(8,128)S(1)}, u32[]{:S(2)}, u32[]{:S(2)}) collective-permute-start(f32[8,128]{1,0:T(8,128)S(1)} %get-tuple-element.61), channel_id=1, source_target_pairs={{0,1},{1,0},{2,3},{3,2},{4,5},{5,4},{6,7},{7,6},{8,9},{9,8},{10,11... | collective-permute-start | bytes 12296 | tf_op jit(solution)/shard_map/ppermute | solution.py:31
  25.6 0.8 %collective-permute-done.4 = f32[8,128]{1,0:T(8,128)S(1)} collective-permute-done((f32[8,128]{1,0:T(8,128)S(1)}, f32[8,128]{1,0:T(8,128)S(1)}, u32[]{:S(2)}, u32[]{:S(2)}) %collective-permute-start.4) | collective-permute-done | bytes 4128 | tf_op jit(solution)/shard_map/ppermute | solution.py:31
  26.4 2.0 %collective-permute-start.5 = (f32[8,128]{1,0:T(8,128)S(1)}, f32[8,128]{1,0:T(8,128)S(1)}, u32[]{:S(2)}, u32[]{:S(2)}) collective-permute-start(f32[8,128]{1,0:T(8,128)S(1)} %add.12), channel_id=1, source_target_pairs={{0,2},{1,3},{2,0},{3,1},{4,6},{5,7},{6,4},{7,5},{8,10},{9,11},{10,... | collective-permute-start | bytes 12296 | tf_op jit(solution)/shard_map/ppermute | solution.py:31
  28.4 1.6 %collective-permute-done.5 = f32[8,128]{1,0:T(8,128)S(1)} collective-permute-done((f32[8,128]{1,0:T(8,128)S(1)}, f32[8,128]{1,0:T(8,128)S(1)}, u32[]{:S(2)}, u32[]{:S(2)}) %collective-permute-start.5) | collective-permute-done | bytes 4128 | tf_op jit(solution)/shard_map/ppermute | solution.py:31
  30.0 2.2 %collective-permute-start.6 = (f32[8,128]{1,0:T(8,128)S(1)}, f32[8,128]{1,0:T(8,128)S(1)}, u32[]{:S(2)}, u32[]{:S(2)}) collective-permute-start(f32[8,128]{1,0:T(8,128)S(1)} %add.13), channel_id=1, source_target_pairs={{0,4},{1,5},{2,6},{3,7},{4,0},{5,1},{6,2},{7,3},{8,12},{9,13},{10,... | collective-permute-start | bytes 12296 | tf_op jit(solution)/shard_map/ppermute | solution.py:31
  32.2 1.6 %collective-permute-done.6 = f32[8,128]{1,0:T(8,128)S(1)} collective-permute-done((f32[8,128]{1,0:T(8,128)S(1)}, f32[8,128]{1,0:T(8,128)S(1)}, u32[]{:S(2)}, u32[]{:S(2)}) %collective-permute-start.6) | collective-permute-done | bytes 4128 | tf_op jit(solution)/shard_map/ppermute | solution.py:31
  33.8 3.0 %collective-permute-start.7 = (f32[8,128]{1,0:T(8,128)S(1)}, f32[8,128]{1,0:T(8,128)S(1)}, u32[]{:S(2)}, u32[]{:S(2)}) collective-permute-start(f32[8,128]{1,0:T(8,128)S(1)} %add.14), channel_id=1, source_target_pairs={{0,8},{1,9},{2,10},{3,11},{4,12},{5,13},{6,14},{7,15},{8,0},{9,1},... | collective-permute-start | bytes 12296 | tf_op jit(solution)/shard_map/ppermute | solution.py:31
  36.8 1.6 %collective-permute-done.7 = f32[8,128]{1,0:T(8,128)S(1)} collective-permute-done((f32[8,128]{1,0:T(8,128)S(1)}, f32[8,128]{1,0:T(8,128)S(1)}, u32[]{:S(2)}, u32[]{:S(2)}) %collective-permute-start.7) | collective-permute-done | bytes 4128 | tf_op jit(solution)/shard_map/ppermute | solution.py:31
  38.4 2.7 %shard_map.100 = (f32[16,32,1024]{2,1,0:T(8,128)}, f32[16,32,1024]{2,1,0:T(8,128)}) custom-call(f32[8,128]{1,0:T(8,128)S(1)} %add.15.sums, f32[32,16,1024]{2,1,0:T(8,128)S(1)} %get-tuple-element.51.grad, f32[40,16,1024]{2,1,0:T(8,128)S(1)} %get-tuple-element.62.search, f32[32,16,1024]{2,1,0:T(8,128)S(1)} %get-tuple-element.63.image, ...), custom_call_target="tpu_custom_call" | custom-call | flops 4194304 | bytes 4194304 | tf_op jit(solution)/shard_map/pallas_call | solution.py:381
  (5 shorter events, 0.0 us)
Async XLA Ops:
  0.6 2.6 %copy-start = (f32[16,32,1024]{2,1,0:T(8,128)S(1)}, f32[16,32,1024]{2,1,0:T(8,128)}, u32[]{:S(2)}) copy-start(f32[16,32,1024]{2,1,0:T(8,128)} %latent.3) | copy-start | bytes 6291460
  0.6 2.5 %copy-start.3 = (bf16[32]{0:T(256)(128)(2,1)S(1)}, bf16[32]{0:T(256)(128)(2,1)}, u32[]{:S(2)}) copy-start(bf16[32]{0:T(256)(128)(2,1)} %param.14) | copy-start | bytes 196
  0.7 2.6 %copy-start.2 = (f32[8]{0:T(128)S(1)}, f32[8]{0:T(128)}, u32[]{:S(2)}) copy-start(f32[8]{0:T(128)} %intercepts.1) | copy-start | bytes 100
  0.7 2.6 %copy-start.1 = (s32[32,1024]{1,0:T(8,128)S(1)}, s32[32,1024]{1,0:T(8,128)}, u32[]{:S(2)}) copy-start(s32[32,1024]{1,0:T(8,128)} %zones.1) | copy-start | bytes 393220
  2.0 4.4 %collective-permute-start = (f32[40,1024]{1,0:T(8,128)S(1)}, f32[40,1024]{1,0:T(8,128)S(1)}, u32[]{:S(2)}, u32[]{:S(2)}) collective-permute-start(f32[40,1024]{1,0:T(8,128)S(1)} %get-tuple-element.34), channel_id=1, source_target_pairs={{0,1},{1,0},{2,3},{3,2},{4,5},{5,4},{6,7},{7,6},{8,9},{9,8},{10,11... | collective-permute-start | bytes 491528 | tf_op jit(solution)/shard_map/ppermute | solution.py:413
  2.5 3.9 %collective-permute-start.1 = (f32[40,1024]{1,0:T(8,128)S(1)}, f32[40,1024]{1,0:T(8,128)S(1)}, u32[]{:S(2)}, u32[]{:S(2)}) collective-permute-start(f32[40,1024]{1,0:T(8,128)S(1)} %get-tuple-element.35), channel_id=1, source_target_pairs={{1,2},{2,1},{3,4},{4,3},{5,6},{6,5},{7,8},{8,7},{9,10},{10,9},{11,... | collective-permute-start | bytes 491528 | tf_op jit(solution)/shard_map/ppermute | solution.py:413
  7.3 12.1 %collective-permute-start.2 = (f32[72,1024]{1,0:T(8,128)S(1)}, f32[72,1024]{1,0:T(8,128)S(1)}, u32[]{:S(2)}, u32[]{:S(2)}) collective-permute-start(f32[72,1024]{1,0:T(8,128)S(1)} %get-tuple-element.42), channel_id=1, source_target_pairs={{0,1},{1,0},{2,3},{3,2},{4,5},{5,4},{6,7},{7,6},{8,9},{9,8},{10,11... | collective-permute-start | bytes 884744 | tf_op jit(solution)/shard_map/ppermute | solution.py:431
  11.2 8.2 %collective-permute-start.3 = (f32[72,1024]{1,0:T(8,128)S(1)}, f32[72,1024]{1,0:T(8,128)S(1)}, u32[]{:S(2)}, u32[]{:S(2)}) collective-permute-start(f32[72,1024]{1,0:T(8,128)S(1)} %get-tuple-element.43), channel_id=1, source_target_pairs={{1,2},{2,1},{3,4},{4,3},{5,6},{6,5},{7,8},{8,7},{9,10},{10,9},{11,... | collective-permute-start | bytes 884744 | tf_op jit(solution)/shard_map/ppermute | solution.py:431
  21.1 5.3 %collective-permute-start.4 = (f32[8,128]{1,0:T(8,128)S(1)}, f32[8,128]{1,0:T(8,128)S(1)}, u32[]{:S(2)}, u32[]{:S(2)}) collective-permute-start(f32[8,128]{1,0:T(8,128)S(1)} %get-tuple-element.61), channel_id=1, source_target_pairs={{0,1},{1,0},{2,3},{3,2},{4,5},{5,4},{6,7},{7,6},{8,9},{9,8},{10,11... | collective-permute-start | bytes 12296 | tf_op jit(solution)/shard_map/ppermute | solution.py:31
  26.4 3.6 %collective-permute-start.5 = (f32[8,128]{1,0:T(8,128)S(1)}, f32[8,128]{1,0:T(8,128)S(1)}, u32[]{:S(2)}, u32[]{:S(2)}) collective-permute-start(f32[8,128]{1,0:T(8,128)S(1)} %add.12), channel_id=1, source_target_pairs={{0,2},{1,3},{2,0},{3,1},{4,6},{5,7},{6,4},{7,5},{8,10},{9,11},{10,... | collective-permute-start | bytes 12296 | tf_op jit(solution)/shard_map/ppermute | solution.py:31
  30.0 3.8 %collective-permute-start.6 = (f32[8,128]{1,0:T(8,128)S(1)}, f32[8,128]{1,0:T(8,128)S(1)}, u32[]{:S(2)}, u32[]{:S(2)}) collective-permute-start(f32[8,128]{1,0:T(8,128)S(1)} %add.13), channel_id=1, source_target_pairs={{0,4},{1,5},{2,6},{3,7},{4,0},{5,1},{6,2},{7,3},{8,12},{9,13},{10,... | collective-permute-start | bytes 12296 | tf_op jit(solution)/shard_map/ppermute | solution.py:31
  33.8 4.6 %collective-permute-start.7 = (f32[8,128]{1,0:T(8,128)S(1)}, f32[8,128]{1,0:T(8,128)S(1)}, u32[]{:S(2)}, u32[]{:S(2)}) collective-permute-start(f32[8,128]{1,0:T(8,128)S(1)} %add.14), channel_id=1, source_target_pairs={{0,8},{1,9},{2,10},{3,11},{4,12},{5,13},{6,14},{7,15},{8,0},{9,1},... | collective-permute-start | bytes 12296 | tf_op jit(solution)/shard_map/ppermute | solution.py:31

commit v5 on v4

--- a/solution.py
+++ b/solution.py
@@ -22,15 +22,29 @@
     return first, second
 
 
-def all_sum(values):
+def swap_rows(near, far):
+    swap, cross = pair_maps(lax.axis_size(AX))
+    far = lax.ppermute(far, AX, cross)
+    return lax.ppermute(near, AX, swap), far
+
+
+def all_sum(values, works):
     count = lax.axis_size(AX)
+    results = []
     if count & (count - 1):
-        return lax.psum(values, AX)
+        return lax.psum(values, AX), [work(values) for work in works]
     step = 1
     while step < count:
-        values = values + lax.ppermute(values, AX, [(i, i ^ step) for i in range(count)])
+        got = lax.ppermute(values, AX, [(i, i ^ step) for i in range(count)])
+        if step > 1 and len(results) < len(works):
+            piece = works[len(results)](values)
+            got, piece = lax.optimization_barrier((got, piece))
+            results.append(piece)
+        values = values + got
         step *= 2
-    return values
+    while len(results) < len(works):
+        results.append(works[len(results)](values))
+    return values, results
 
 
 def row_of(ref, row):
@@ -129,8 +143,6 @@
         top, bottom = (land[q : q + 1, :].astype(F32) for q in (d, rows - 2 + d))
         first[at + 3 + d : at + 4 + d, :] = jnp.where(odd, top, bottom)
         second[at + 3 + d : at + 4 + d, :] = jnp.where(odd, bottom, top)
-    first[at + 5 :, :] = jnp.zeros((3, cols), F32)
-    second[at + 5 :, :] = jnp.zeros((3, cols), F32)
     for copy in copies:
         copy.wait()
 
@@ -241,18 +253,18 @@
             top, bottom = eta[d, :, part], eta[rows - 2 + d, :, part]
             first[at + d : at + d + 1, part] = jnp.where(odd, top, bottom)
             second[at + d : at + d + 1, part] = jnp.where(odd, bottom, top)
-        first[at + 2 :, part] = jnp.zeros((6, LANES), F32)
-        second[at + 2 :, part] = jnp.zeros((6, LANES), F32)
+
+
+def mass_row(r, source, at, weight, mask):
+    mid = row_of(source, at)
+    return mid, [time_coupling * temporal_tile(m, mask) + h * m for m, h in zip(mid, row_of(weight, r + 2))]
 
 
 def hessian_row(r, source, at, image, offset, kappa, weight, mask):
     outer = laplace_row(row_of(image, r + offset - 1), row_of(image, r + offset), row_of(image, r + offset + 1),
                         map_row(kappa, r + 3), mask)
-    mid = row_of(source, at)
-    heavy = row_of(weight, r + 2)
-    return mid, [
-        prior_scale * o + (time_coupling * temporal_tile(m, mask) + h * m) for o, m, h in zip(outer, mid, heavy)
-    ]
+    mid, mass = mass_row(r, source, at, weight, mask)
+    return mid, [prior_scale * o + m for o, m in zip(outer, mass)]
 
 
 def dot_rows(a, b):
@@ -260,7 +272,7 @@
 
 
 def inner_kernel(kappa, eta, land, tally, field, start_image, grad_in, weight_in, inv_in, search_in,
-                 grad, weight, inv, search, first, image, second, second_image, last, sums):
+                 grad, weight, inv, search, first, image, second, second_image, sums):
     weeks = grad.shape[1]
     rows = grad.shape[0]
     mask = masks(weeks)
@@ -278,34 +290,31 @@
     zero = jnp.zeros((8, LANES), F32)
 
     def apply(r, carry):
-        rz, pq, cross = carry
+        rz, pq, cross, total = carry
         mid, out = hessian_row(r, search, r + 4, first, 3, kappa, weight, mask)
         other = [a * b for a, b in zip(out, row_of(inv, r + 2))]
+        mass = [time_coupling * temporal_tile(y, mask) + h * y for y, h in zip(other, row_of(weight, r + 2))]
         put_row(image, r, out)
         put_row(second, r + 2, other)
-        return rz + dot_rows(mid, row_of(grad, r)), pq + dot_rows(mid, out), cross + dot_rows(other, out)
-
-    rz, pq, cross = row_loop(2, rows - 2, apply, (zero, zero, zero), most=7)
-
-    def second_inner(r, _):
-        put_row(second_image, r + 1, laplace_row(
-            row_of(second, r + 1), row_of(second, r + 2), row_of(second, r + 3), map_row(kappa, r + 3), mask))
-
-    row_loop(3, rows - 3, second_inner)
-
-    def apply_second(r, total):
-        mid, out = hessian_row(r, second, r + 2, second_image, 1, kappa, weight, mask)
-        put_row(last, r, out)
-        return total + dot_rows(mid, out)
-
-    total = row_loop(4, rows - 4, apply_second, zero, most=8)
-    for k, value in enumerate((rz, pq, cross, total)):
+        return (rz + dot_rows(mid, row_of(grad, r)), pq + dot_rows(mid, out), cross + dot_rows(other, out),
+                total + dot_rows(other, mass))
+
+    rz, pq, cross, total = row_loop(2, rows - 2, apply, (zero, zero, zero, zero), most=7)
+
+    def second_inner(r, square):
+        out = laplace_row(
+            row_of(second, r + 1), row_of(second, r + 2), row_of(second, r + 3), map_row(kappa, r + 3), mask)
+        put_row(second_image, r + 1, out)
+        return square + dot_rows(out, out)
+
+    square = row_loop(3, rows - 3, second_inner, zero)
+    for k, value in enumerate((rz, pq, cross, total + prior_scale * square)):
         sums[8 * k : 8 * k + 8, :] = value
 
 
 def outer_kernel(old_first, old_second, got_first, got_second, kappa, field, grad, partial,
-                 weight_in, inv_in, search_in, first_in, image_in, second_in, second_image_in, last_in,
-                 weight, inv, search, first, image, second, second_image, last, sums):
+                 weight_in, inv_in, search_in, first_in, image_in, second_in, second_image_in,
+                 weight, inv, search, first, image, second, second_image, sums):
     weeks = grad.shape[1]
     rows = grad.shape[0]
     mask = masks(weeks)
@@ -334,20 +343,30 @@
         put_row(second, r + 2, other)
         if 0 <= r < rows:
             put_row(image, r, out)
+            mass = [time_coupling * temporal_tile(y, mask) + h * y for y, h in zip(other, row_of(weight, r + 2))]
             rz, pq, cross = rz + dot_rows(mid, row_of(grad, r)), pq + dot_rows(mid, out), cross + dot_rows(other, out)
+            total = total + dot_rows(other, mass)
     for r in (-1, 0, 1, 2, rows - 3, rows - 2, rows - 1, rows):
-        put_row(second_image, r + 1, keep_inside(r, rows, laplace_row(
-            row_of(second, r + 1), row_of(second, r + 2), row_of(second, r + 3), map_row(kappa, r + 3), mask)))
-    for r in (0, 1, 2, 3, rows - 4, rows - 3, rows - 2, rows - 1):
-        mid, out = hessian_row(r, second, r + 2, second_image, 1, kappa, weight, mask)
-        put_row(last, r, out)
-        total = total + dot_rows(mid, out)
+        out = keep_inside(r, rows, laplace_row(
+            row_of(second, r + 1), row_of(second, r + 2), row_of(second, r + 3), map_row(kappa, r + 3), mask))
+        put_row(second_image, r + 1, out)
+        if 0 <= r < rows:
+            total = total + prior_scale * dot_rows(out, out)
     sums[...] = jnp.zeros_like(sums)
     for k, value in enumerate((rz, pq, cross, total)):
         sums[k : k + 1, :] = jnp.sum(value, axis=0, keepdims=True)
 
 
-def final_kernel(sums, grad, search, image, second, last, newton_out, residual_out, newton, residual, newton_sem, residual_sem):
+def last_kernel(low, gate, kappa, weight, second, second_image, last):
+    mask = masks(last.shape[1])
+
+    def apply(r, _):
+        put_row(last, r, hessian_row(r + low, second, r + low + 2, second_image, 1, kappa, weight, mask)[1])
+
+    row_loop(0, last.shape[0], apply, most=8)
+
+
+def final_kernel(sums, grad, search, image, second, upper, lower, newton_out, residual_out, newton, residual, newton_sem, residual_sem):
     rows, weeks, cols = grad.shape
     rz, pq, cross, total = (jnp.sum(sums[k : k + 1, :], axis=1, keepdims=True) for k in range(4))
     first_step = rz / pq
@@ -363,14 +382,17 @@
             pltpu.make_async_copy(residual.at[r], residual_out.at[:, r, :], residual_sem.at[r]),
         )
 
-    def combine(r, _):
+    half = upper.shape[0]
+
+    def combine(r, last, at):
         put_row(newton, r, [along * p - across * y for p, y in zip(row_of(search, r + 4), row_of(second, r + 2))])
         put_row(residual, r, [
-            g - along * w + across * h for g, w, h in zip(row_of(grad, r), row_of(image, r), row_of(last, r))])
+            g - along * w + across * h for g, w, h in zip(row_of(grad, r), row_of(image, r), row_of(last, r - at))])
         for copy in copies(r):
             copy.start()
 
-    row_loop(0, rows, combine, most=8)
+    row_loop(0, half, lambda r, _: combine(r, upper, 0), most=8)
+    row_loop(half, rows, lambda r, _: combine(r, lower, half), most=8)
     for r in range(rows):
         for copy in copies(r):
             copy.wait()
@@ -392,7 +414,6 @@
 
 def shards(latent, counts, land_mask, region_ids, kappa_sq, covariates, effects, intercepts):
     weeks, rows, cols = latent.shape
-    swap, cross = pair_maps(lax.axis_size(AX))
 
     def ext(depth):
         return ((rows + 2 * depth, weeks, cols), VMEM)
@@ -402,7 +423,7 @@
 
     cells = weeks * rows * cols
     SMEM, ANY, HBM, DMA = pltpu.SMEM, pl.ANY, pltpu.HBM, pltpu.SemaphoreType.DMA
-    packed = ((2 * weeks + 8, cols), VMEM)
+    packed = ((2 * weeks + 5, cols), VMEM)
     near, far, kappa, land = call(
         pack_kernel,
         [packed, packed, maps(3), maps(0)],
@@ -410,7 +431,7 @@
         scratch=[pltpu.VMEM((rows, cols), F32), pltpu.VMEM((rows, cols), jnp.int32), DMA((6,))],
         flops=cells // 16, moved=cells,
     )
-    old_near, old_far = lax.ppermute(near, AX, swap), lax.ppermute(far, AX, cross)
+    old_near, old_far = swap_rows(near, far)
     field, image, eta, tally = call(
         front_kernel,
         [ext(2), ext(1), maps(0), ext(0)],
@@ -419,7 +440,7 @@
         scratch=[pltpu.VMEM(covariates.shape, covariates.dtype), pltpu.VMEM(counts.shape, jnp.int32), DMA, DMA],
         flops=40 * cells, moved=12 * cells, limit=8,
     )
-    packed = ((4 * weeks + 8, cols), VMEM)
+    packed = ((4 * weeks + 2, cols), VMEM)
     kappa, field, image, grad, weight, inv, search, near, far = call(
         edge_kernel,
         [maps(3), ext(2), ext(1), ext(0), ext(2), ext(2), ext(4), packed, packed],
@@ -428,28 +449,39 @@
         aliases={5 + k: k for k in range(3)},
         flops=10 * cells, moved=cells,
     )
-    near, far = lax.ppermute(near, AX, swap), lax.ppermute(far, AX, cross)
-    grad, weight, inv, search, first, image, second, second_image, last, partial = call(
+    near, far = swap_rows(near, far)
+    grad, weight, inv, search, first, image, second, second_image, partial = call(
         inner_kernel,
-        [ext(0), ext(2), ext(2), ext(4), ext(3), ext(0), ext(2), ext(1), ext(0), ((32, LANES), VMEM)],
+        [ext(0), ext(2), ext(2), ext(4), ext(3), ext(0), ext(2), ext(1), ((32, LANES), VMEM)],
         [(kappa, VMEM), (eta, VMEM), (land, VMEM), (tally, VMEM), (field, VMEM), (image, VMEM),
          (grad, VMEM), (weight, VMEM), (inv, VMEM), (search, VMEM)],
         aliases={6 + k: k for k in range(4)},
         flops=120 * cells, moved=12 * cells,
     )
-    weight, inv, search, first, image, second, second_image, last, sums = call(
+    weight, inv, search, first, image, second, second_image, sums = call(
         outer_kernel,
-        [ext(2), ext(2), ext(4), ext(3), ext(0), ext(2), ext(1), ext(0), ((8, LANES), VMEM)],
+        [ext(2), ext(2), ext(4), ext(3), ext(0), ext(2), ext(1), ((8, LANES), VMEM)],
         [(old_near, VMEM), (old_far, VMEM), (near, VMEM), (far, VMEM), (kappa, VMEM), (field, VMEM),
          (grad, VMEM), (partial, VMEM), (weight, VMEM), (inv, VMEM), (search, VMEM), (first, VMEM), (image, VMEM),
-         (second, VMEM), (second_image, VMEM), (last, VMEM)],
-        aliases={8 + k: k for k in range(8)},
+         (second, VMEM), (second_image, VMEM)],
+        aliases={8 + k: k for k in range(7)},
         flops=20 * cells, moved=cells,
     )
+    half = rows // 2
+
+    def last_rows(low, count):
+        return lambda gate: call(
+            functools.partial(last_kernel, low),
+            [((count, weeks, cols), VMEM)],
+            [(gate, VMEM), (kappa, VMEM), (weight, VMEM), (second, VMEM), (second_image, VMEM)],
+            flops=4 * cells, moved=cells,
+        )[0]
+
+    sums, (upper, lower) = all_sum(sums, [last_rows(0, half), last_rows(half, rows - half)])
     return call(
         final_kernel,
         [(latent.shape, ANY), (latent.shape, ANY)],
-        [(all_sum(sums), VMEM), (grad, VMEM), (search, VMEM), (image, VMEM), (second, VMEM), (last, VMEM)],
+        [(sums, VMEM), (grad, VMEM), (search, VMEM), (image, VMEM), (second, VMEM), (upper, VMEM), (lower, VMEM)],
         scratch=[pltpu.VMEM((rows, weeks, cols), F32), pltpu.VMEM((rows, weeks, cols), F32), DMA((rows,)), DMA((rows,))],
         flops=8 * cells, moved=8 * cells, limit=6,
     )

time: 41.2 us -> 40.9 us (level)
  waiting for transfers between devices: 5.6 us -> 3.86 us
  Pallas kernels: 17.1 us -> 18 us
  starting transfers between devices: 17.5 us -> 18 us
    ppermute x8, waiting for transfers between devices: 5.6 us -> 3.86 us  [the longest x4 3.85 us: all_sum(): got = lax.ppermute(values, AX, [(i, i ^ step) for i in range(count)])]
    pallas_call x6 -> x8, Pallas kernels: 17.1 us -> 18 us  [call(): pl.pallas_call(kernel, out_shape=shapes, in_specs=[pl.BlockSpec(memory_sp...]
    ppermute x8, starting transfers between devices: 17.5 us -> 18 us  [the longest x4 12.3 us: all_sum(): got = lax.ppermute(values, AX, [(i, i ^ step) for i in range(count)])]
  transfers between devices with their start and end apart: 8 -> 8, of which waited for: 4 -> 4; matrix products, arithmetic and copies ran while one was open for 0% -> 0% of each run, Pallas kernels for 26% -> 29%
where the time goes in v5:
time: 40.9 us; the launch traced here: 40.7 us
  Pallas kernels  18 us (44%)
  starting transfers between devices  18 us (44%)
  waiting for transfers between devices  3.86 us (9%)
  between operations  0.8 us (2%)
    pallas_call x8, Pallas kernels, call(): pl.pallas_call(kernel, out_shape=shapes, in_specs=[pl.BlockSpec(memory_sp...  18 us
    ppermute x4, starting transfers between devices, all_sum(): got = lax.ppermute(values, AX, [(i, i ^ step) for i in range(count)])  12.3 us
    ppermute x2, starting transfers between devices, swap_rows(): return (lax.ppermute(near, AX, swap), far)  4.45 us
    ppermute x4, waiting for transfers between devices, all_sum(): got = lax.ppermute(values, AX, [(i, i ^ step) for i in range(count)])  3.85 us
    ppermute x2, starting transfers between devices, swap_rows(): far = lax.ppermute(far, AX, cross)  1.33 us
  transfers between devices with their start and end apart: 8, of which 4 were waited for; matrix products, arithmetic and copies ran while one was open for 0% of the time, Pallas kernels for 29%

profile of v5, /device:TPU:0, one launch (start us, length us, event | category | flops | bytes accessed | tf_op | source)
XLA Modules:
  0.0 40.7 jit_solution(10904928096763382681)
XLA Ops:
  0.6 0.0 copy-start
  0.6 0.0 copy-start.3
  0.7 0.0 copy-start.2
  0.7 0.0 copy-start.1
  0.7 1.3 %shard_map.95 = (f32[37,1024]{1,0:T(8,128)S(1)}, f32[37,1024]{1,0:T(8,128)S(1)}, f32[38,1,1024]{2,1,0:T(1,128)S(1)}, f32[32,1,1024]{2,1,0:T(1,128)S(1)}) custom-call(f32[16,32,1024]{2,1,0:T(8,128)} %latent.3, f32[32,1024]{1,0:T(8,128)} %kappa_hbm.1, s32[32,1024]{1,0:T(8,128)} %land_hbm.1), custom_call_target="tpu_custom_call" | custom-call | flops 32768 | bytes 524288 | tf_op jit(solution)/shard_map/pallas_call | solution.py:403
  2.0 0.5 %collective-permute-start = (f32[37,1024]{1,0:T(8,128)S(1)}, f32[37,1024]{1,0:T(8,128)S(1)}, u32[]{:S(2)}, u32[]{:S(2)}) collective-permute-start(f32[37,1024]{1,0:T(8,128)S(1)} %get-tuple-element.38), channel_id=1, source_target_pairs={{0,1},{1,0},{2,3},{3,2},{4,5},{5,4},{6,7},{7,6},{8,9},{9,8},{10,11... | collective-permute-start | bytes 454664 | tf_op jit(solution)/shard_map/ppermute | solution.py:28
  2.5 0.7 %collective-permute-start.1 = (f32[37,1024]{1,0:T(8,128)S(1)}, f32[37,1024]{1,0:T(8,128)S(1)}, u32[]{:S(2)}, u32[]{:S(2)}) collective-permute-start(f32[37,1024]{1,0:T(8,128)S(1)} %get-tuple-element.39), channel_id=1, source_target_pairs={{1,2},{2,1},{3,4},{4,3},{5,6},{6,5},{7,8},{8,7},{9,10},{10,9},{11,... | collective-permute-start | bytes 454664 | tf_op jit(solution)/shard_map/ppermute | solution.py:27
  3.2 0.0 copy-done.3
  3.2 0.0 copy-done
  3.2 0.0 copy-done.2
  3.2 0.0 copy-done.1
  3.2 3.2 %shard_map.96 = (f32[36,16,1024]{2,1,0:T(8,128)S(1)}, f32[34,16,1024]{2,1,0:T(8,128)S(1)}, f32[32,1,1024]{2,1,0:T(1,128)S(1)}, f32[32,16,1024]{2,1,0:T(8,128)S(1)}) custom-call(f32[32]{0:T(128)S(1)} %convert_element_type.3.effects, f32[8]{0:T(128)S(1)} %copy-done.2, f32[16,32,1024]{2,1,0:T(8,128)S(1)} %copy-done, bf16[32,32,1024]{2,1,0:T(8,128)(2,1)} %covariates.1, ...), custom_call_target="tpu_custom_call" | custom-call | flops 20971520 | bytes 6291456 | tf_op jit(solution)/shard_map/pallas_call | solution.py:403
  6.4 0.0 collective-permute-done.got_first.old_first
  6.4 0.0 collective-permute-done.1.got_second.old_second
  6.4 0.8 %shard_map.97 = (f32[38,1,1024]{2,1,0:T(1,128)S(1)}, f32[36,16,1024]{2,1,0:T(8,128)S(1)}, f32[34,16,1024]{2,1,0:T(8,128)S(1)}, f32[32,16,1024]{2,1,0:T(8,128)S(1...) custom-call(f32[37,1024]{1,0:T(8,128)S(1)} %collective-permute-done., ...), custom_call_target="tpu_custom_call", output_to_operand_aliasing={{0}: (5, {}), {1}: (6, {}), {2}: (7, {})} | custom-call | flops 5242880 | bytes 524288 | tf_op jit(solution)/shard_map/pallas_call | solution.py:403
  7.3 3.9 %collective-permute-start.2 = (f32[66,1024]{1,0:T(8,128)S(1)}, f32[66,1024]{1,0:T(8,128)S(1)}, u32[]{:S(2)}, u32[]{:S(2)}) collective-permute-start(f32[66,1024]{1,0:T(8,128)S(1)} %get-tuple-element.46), channel_id=1, source_target_pairs={{0,1},{1,0},{2,3},{3,2},{4,5},{5,4},{6,7},{7,6},{8,9},{9,8},{10,11... | collective-permute-start | bytes 811016 | tf_op jit(solution)/shard_map/ppermute | solution.py:28
  11.2 0.7 %collective-permute-start.3 = (f32[66,1024]{1,0:T(8,128)S(1)}, f32[66,1024]{1,0:T(8,128)S(1)}, u32[]{:S(2)}, u32[]{:S(2)}) collective-permute-start(f32[66,1024]{1,0:T(8,128)S(1)} %get-tuple-element.47), channel_id=1, source_target_pairs={{1,2},{2,1},{3,4},{4,3},{5,6},{6,5},{7,8},{8,7},{9,10},{10,9},{11,... | collective-permute-start | bytes 811016 | tf_op jit(solution)/shard_map/ppermute | solution.py:27
  11.9 7.0 %shard_map.98 = (f32[32,16,1024]{2,1,0:T(8,128)S(1)}, f32[36,16,1024]{2,1,0:T(8,128)S(1)}, f32[36,16,1024]{2,1,0:T(8,128)S(1)}, f32[40,16,1024]{2,1,0:T(8,128)S(...) custom-call(f32[38,1,1024]{2,1,0:T(1,128)S(1)} %get-tuple-element.48, ...), custom_call_target="tpu_custom_call", output_to_operand_aliasing={{0}: (6, {}), {1}: (7, {}), {2}: (8, {}), {3}: (9, {})} | custom-call | flops 62914560 | bytes 6291456 | tf_op jit(solution)/shard_map/pallas_call | solution.py:403
  18.9 0.0 collective-permute-done.2.got_first
  18.9 0.0 collective-permute-done.3.got_second
  18.9 1.3 %shard_map.99 = (f32[36,16,1024]{2,1,0:T(8,128)S(1)}, f32[36,16,1024]{2,1,0:T(8,128)S(1)}, f32[40,16,1024]{2,1,0:T(8,128)S(1)}, f32[38,16,1024]{2,1,0:T(8,128)S(...) custom-call(f32[37,1024]{1,0:T(8,128)S(1)} %collective-permute-done., ...), custom_call_target="tpu_custom_call", output_to_operand_aliasing={{0}: (8, {}), {1}: (9, {}), {2}: (10, {}), {3}: (11, {}), {... | custom-call | flops 10485760 | bytes 524288 | tf_op jit(solution)/shard_map/pallas_call | solution.py:403
  20.2 4.5 %collective-permute-start.4 = (f32[8,128]{1,0:T(8,128)S(1)}, f32[8,128]{1,0:T(8,128)S(1)}, u32[]{:S(2)}, u32[]{:S(2)}) collective-permute-start(f32[8,128]{1,0:T(8,128)S(1)} %get-tuple-element.64), channel_id=1, source_target_pairs={{0,1},{1,0},{2,3},{3,2},{4,5},{5,4},{6,7},{7,6},{8,9},{9,8},{10,11... | collective-permute-start | bytes 12296 | tf_op jit(solution)/shard_map/ppermute | solution.py:38
  24.7 0.8 %collective-permute-done.4 = f32[8,128]{1,0:T(8,128)S(1)} collective-permute-done((f32[8,128]{1,0:T(8,128)S(1)}, f32[8,128]{1,0:T(8,128)S(1)}, u32[]{:S(2)}, u32[]{:S(2)}) %collective-permute-start.4) | collective-permute-done | bytes 4128 | tf_op jit(solution)/shard_map/ppermute | solution.py:38
  25.6 2.5 %collective-permute-start.5 = (f32[8,128]{1,0:T(8,128)S(1)}, f32[8,128]{1,0:T(8,128)S(1)}, u32[]{:S(2)}, u32[]{:S(2)}) collective-permute-start(f32[8,128]{1,0:T(8,128)S(1)} %add.12.gate), channel_id=1, source_target_pairs={{0,2},{1,3},{2,0},{3,1},{4,6},{5,7},{6,4},{7,5},{8,10},{9,11},{10,... | collective-permute-start | bytes 12296 | tf_op jit(solution)/shard_map/ppermute | solution.py:38
  28.0 0.9 %shard_map.100.upper = f32[16,16,1024]{2,1,0:T(8,128)S(1)} custom-call(f32[8,128]{1,0:T(8,128)S(1)} %add.12.gate, f32[38,1,1024]{2,1,0:T(1,128)S(1)} %get-tuple-element.48.kappa, f32[36,16,1024]{2,1,0:T(8,128)S(1)} %get-tuple-element.65.weight, f32[36,16,1024]{2,1,0:T(8,128)S(1)} %get-tuple-element.66.second, f32[34,16,1024]{2,1,0:T(8,128)S(1)} %get-tuple-element.67.second_image), custom_call_target="tpu_custom_call" | custom-call | flops 2097152 | bytes 524288 | tf_op jit(solution)/shard_map/pallas_call | solution.py:403
  28.9 0.7 %collective-permute-done.5 = f32[8,128]{1,0:T(8,128)S(1)} collective-permute-done((f32[8,128]{1,0:T(8,128)S(1)}, f32[8,128]{1,0:T(8,128)S(1)}, u32[]{:S(2)}, u32[]{:S(2)}) %collective-permute-start.5) | collective-permute-done | bytes 4128 | tf_op jit(solution)/shard_map/ppermute | solution.py:38
  29.6 2.2 %collective-permute-start.6 = (f32[8,128]{1,0:T(8,128)S(1)}, f32[8,128]{1,0:T(8,128)S(1)}, u32[]{:S(2)}, u32[]{:S(2)}) collective-permute-start(f32[8,128]{1,0:T(8,128)S(1)} %add.13.gate), channel_id=1, source_target_pairs={{0,4},{1,5},{2,6},{3,7},{4,0},{5,1},{6,2},{7,3},{8,12},{9,13},{10,... | collective-permute-start | bytes 12296 | tf_op jit(solution)/shard_map/ppermute | solution.py:38
  31.9 0.9 %shard_map.101.lower = f32[16,16,1024]{2,1,0:T(8,128)S(1)} custom-call(f32[8,128]{1,0:T(8,128)S(1)} %add.13.gate, f32[38,1,1024]{2,1,0:T(1,128)S(1)} %get-tuple-element.48.kappa, f32[36,16,1024]{2,1,0:T(8,128)S(1)} %get-tuple-element.65.weight, f32[36,16,1024]{2,1,0:T(8,128)S(1)} %get-tuple-element.66.second, f32[34,16,1024]{2,1,0:T(8,128)S(1)} %get-tuple-element.67.second_image), custom_call_target="tpu_custom_call" | custom-call | flops 2097152 | bytes 524288 | tf_op jit(solution)/shard_map/pallas_call | solution.py:403
  32.7 0.7 %collective-permute-done.6 = f32[8,128]{1,0:T(8,128)S(1)} collective-permute-done((f32[8,128]{1,0:T(8,128)S(1)}, f32[8,128]{1,0:T(8,128)S(1)}, u32[]{:S(2)}, u32[]{:S(2)}) %collective-permute-start.6) | collective-permute-done | bytes 4128 | tf_op jit(solution)/shard_map/ppermute | solution.py:38
  33.4 3.0 %collective-permute-start.7 = (f32[8,128]{1,0:T(8,128)S(1)}, f32[8,128]{1,0:T(8,128)S(1)}, u32[]{:S(2)}, u32[]{:S(2)}) collective-permute-start(f32[8,128]{1,0:T(8,128)S(1)} %add.14), channel_id=1, source_target_pairs={{0,8},{1,9},{2,10},{3,11},{4,12},{5,13},{6,14},{7,15},{8,0},{9,1},... | collective-permute-start | bytes 12296 | tf_op jit(solution)/shard_map/ppermute | solution.py:38
  36.5 1.6 %collective-permute-done.7 = f32[8,128]{1,0:T(8,128)S(1)} collective-permute-done((f32[8,128]{1,0:T(8,128)S(1)}, f32[8,128]{1,0:T(8,128)S(1)}, u32[]{:S(2)}, u32[]{:S(2)}) %collective-permute-start.7) | collective-permute-done | bytes 4128 | tf_op jit(solution)/shard_map/ppermute | solution.py:38
  38.1 2.7 %shard_map.102 = (f32[16,32,1024]{2,1,0:T(8,128)}, f32[16,32,1024]{2,1,0:T(8,128)}) custom-call(f32[8,128]{1,0:T(8,128)S(1)} %add.15.sums, f32[32,16,1024]{2,1,0:T(8,128)S(1)} %get-tuple-element.55.grad, f32[40,16,1024]{2,1,0:T(8,128)S(1)} %get-tuple-element.70.search, f32[32,16,1024]{2,1,0:T(8,128)S(1)} %get-tuple-element.71.image, ...), custom_call_target="tpu_custom_call" | custom-call | flops 4194304 | bytes 4194304 | tf_op jit(solution)/shard_map/pallas_call | solution.py:403
  (5 shorter events, 0.0 us)
Async XLA Ops:
  0.6 2.6 %copy-start = (f32[16,32,1024]{2,1,0:T(8,128)S(1)}, f32[16,32,1024]{2,1,0:T(8,128)}, u32[]{:S(2)}) copy-start(f32[16,32,1024]{2,1,0:T(8,128)} %latent.3) | copy-start | bytes 6291460
  0.6 2.5 %copy-start.3 = (bf16[32]{0:T(256)(128)(2,1)S(1)}, bf16[32]{0:T(256)(128)(2,1)}, u32[]{:S(2)}) copy-start(bf16[32]{0:T(256)(128)(2,1)} %param.14) | copy-start | bytes 196
  0.7 2.6 %copy-start.2 = (f32[8]{0:T(128)S(1)}, f32[8]{0:T(128)}, u32[]{:S(2)}) copy-start(f32[8]{0:T(128)} %intercepts.1) | copy-start | bytes 100
  0.7 2.6 %copy-start.1 = (s32[32,1024]{1,0:T(8,128)S(1)}, s32[32,1024]{1,0:T(8,128)}, u32[]{:S(2)}) copy-start(s32[32,1024]{1,0:T(8,128)} %zones.1) | copy-start | bytes 393220
  2.0 4.4 %collective-permute-start = (f32[37,1024]{1,0:T(8,128)S(1)}, f32[37,1024]{1,0:T(8,128)S(1)}, u32[]{:S(2)}, u32[]{:S(2)}) collective-permute-start(f32[37,1024]{1,0:T(8,128)S(1)} %get-tuple-element.38), channel_id=1, source_target_pairs={{0,1},{1,0},{2,3},{3,2},{4,5},{5,4},{6,7},{7,6},{8,9},{9,8},{10,11... | collective-permute-start | bytes 454664 | tf_op jit(solution)/shard_map/ppermute | solution.py:28
  2.5 3.9 %collective-permute-start.1 = (f32[37,1024]{1,0:T(8,128)S(1)}, f32[37,1024]{1,0:T(8,128)S(1)}, u32[]{:S(2)}, u32[]{:S(2)}) collective-permute-start(f32[37,1024]{1,0:T(8,128)S(1)} %get-tuple-element.39), channel_id=1, source_target_pairs={{1,2},{2,1},{3,4},{4,3},{5,6},{6,5},{7,8},{8,7},{9,10},{10,9},{11,... | collective-permute-start | bytes 454664 | tf_op jit(solution)/shard_map/ppermute | solution.py:27
  7.3 11.6 %collective-permute-start.2 = (f32[66,1024]{1,0:T(8,128)S(1)}, f32[66,1024]{1,0:T(8,128)S(1)}, u32[]{:S(2)}, u32[]{:S(2)}) collective-permute-start(f32[66,1024]{1,0:T(8,128)S(1)} %get-tuple-element.46), channel_id=1, source_target_pairs={{0,1},{1,0},{2,3},{3,2},{4,5},{5,4},{6,7},{7,6},{8,9},{9,8},{10,11... | collective-permute-start | bytes 811016 | tf_op jit(solution)/shard_map/ppermute | solution.py:28
  11.2 7.7 %collective-permute-start.3 = (f32[66,1024]{1,0:T(8,128)S(1)}, f32[66,1024]{1,0:T(8,128)S(1)}, u32[]{:S(2)}, u32[]{:S(2)}) collective-permute-start(f32[66,1024]{1,0:T(8,128)S(1)} %get-tuple-element.47), channel_id=1, source_target_pairs={{1,2},{2,1},{3,4},{4,3},{5,6},{6,5},{7,8},{8,7},{9,10},{10,9},{11,... | collective-permute-start | bytes 811016 | tf_op jit(solution)/shard_map/ppermute | solution.py:27
  20.2 5.3 %collective-permute-start.4 = (f32[8,128]{1,0:T(8,128)S(1)}, f32[8,128]{1,0:T(8,128)S(1)}, u32[]{:S(2)}, u32[]{:S(2)}) collective-permute-start(f32[8,128]{1,0:T(8,128)S(1)} %get-tuple-element.64), channel_id=1, source_target_pairs={{0,1},{1,0},{2,3},{3,2},{4,5},{5,4},{6,7},{7,6},{8,9},{9,8},{10,11... | collective-permute-start | bytes 12296 | tf_op jit(solution)/shard_map/ppermute | solution.py:38
  25.6 4.1 %collective-permute-start.5 = (f32[8,128]{1,0:T(8,128)S(1)}, f32[8,128]{1,0:T(8,128)S(1)}, u32[]{:S(2)}, u32[]{:S(2)}) collective-permute-start(f32[8,128]{1,0:T(8,128)S(1)} %add.12.gate), channel_id=1, source_target_pairs={{0,2},{1,3},{2,0},{3,1},{4,6},{5,7},{6,4},{7,5},{8,10},{9,11},{10,... | collective-permute-start | bytes 12296 | tf_op jit(solution)/shard_map/ppermute | solution.py:38
  29.6 3.8 %collective-permute-start.6 = (f32[8,128]{1,0:T(8,128)S(1)}, f32[8,128]{1,0:T(8,128)S(1)}, u32[]{:S(2)}, u32[]{:S(2)}) collective-permute-start(f32[8,128]{1,0:T(8,128)S(1)} %add.13.gate), channel_id=1, source_target_pairs={{0,4},{1,5},{2,6},{3,7},{4,0},{5,1},{6,2},{7,3},{8,12},{9,13},{10,... | collective-permute-start | bytes 12296 | tf_op jit(solution)/shard_map/ppermute | solution.py:38
  33.4 4.6 %collective-permute-start.7 = (f32[8,128]{1,0:T(8,128)S(1)}, f32[8,128]{1,0:T(8,128)S(1)}, u32[]{:S(2)}, u32[]{:S(2)}) collective-permute-start(f32[8,128]{1,0:T(8,128)S(1)} %add.14), channel_id=1, source_target_pairs={{0,8},{1,9},{2,10},{3,11},{4,12},{5,13},{6,14},{7,15},{8,0},{9,1},... | collective-permute-start | bytes 12296 | tf_op jit(solution)/shard_map/ppermute | solution.py:38

commit v6 on v5

--- a/solution.py
+++ b/solution.py
@@ -118,29 +118,30 @@
     return lax.fori_loop(0, count // step, chunk, carry)
 
 
-def pack_kernel(latent, kappa_hbm, land_hbm, first, second, kappa_out, land_out, kappa, land, sems):
+def pack_kernel(latent, kappa_hbm, land_hbm, first, second, kappa, land, sems):
     weeks, rows, cols = latent.shape
     odd = is_odd()
-    map_copies = [pltpu.make_async_copy(kappa_hbm, kappa, sems.at[4]), pltpu.make_async_copy(land_hbm, land, sems.at[5])]
     copies = []
     for k, (out, base) in enumerate(((first, jnp.where(odd, 0, rows - 2)), (second, jnp.where(odd, rows - 2, 0)))):
         for d in range(2):
             copies.append(pltpu.make_async_copy(
                 latent.at[:, base + d, :], out.at[d * weeks : (d + 1) * weeks, :], sems.at[2 * k + d]))
-    for copy in map_copies + copies:
+    map_copies = []
+    for k, (source, target) in enumerate(((kappa_hbm, kappa), (land_hbm, land))):
+        for d, at in enumerate((0, rows - 8)):
+            map_copies.append(pltpu.make_async_copy(
+                source.at[at : at + 8, :], target.at[8 * d : 8 * d + 8, :], sems.at[4 + 2 * k + d]))
+    for copy in copies + map_copies:
         copy.start()
     for copy in map_copies:
         copy.wait()
-    for r in range(rows):
-        kappa_out[r + 3] = kappa[r : r + 1, :]
-        land_out[r] = land[r : r + 1, :].astype(F32)
     at = 2 * weeks
     for d in range(3):
-        top, bottom = kappa[d : d + 1, :], kappa[rows - 3 + d : rows - 2 + d, :]
+        top, bottom = kappa[d : d + 1, :], kappa[13 + d : 14 + d, :]
         first[at + d : at + d + 1, :] = jnp.where(odd, top, bottom)
         second[at + d : at + d + 1, :] = jnp.where(odd, bottom, top)
     for d in range(2):
-        top, bottom = (land[q : q + 1, :].astype(F32) for q in (d, rows - 2 + d))
+        top, bottom = (land[q : q + 1, :].astype(F32) for q in (d, 14 + d))
         first[at + 3 + d : at + 4 + d, :] = jnp.where(odd, top, bottom)
         second[at + 3 + d : at + 4 + d, :] = jnp.where(odd, bottom, top)
     for copy in copies:
@@ -155,8 +156,8 @@
             target[r + shift : r + shift + 8, :, c : c + LANES] = jnp.swapaxes(block, 0, 1)
 
 
-def front_kernel(effects, intercepts, latent, covariates, zones, kappa, counts,
-                 field, image, eta, tally, covs, raw, cov_sem, sem):
+def front_kernel(effects, intercepts, latent, covariates, zones, kappa_flat, land_flat, counts,
+                 field, image, eta, tally, kappa, land, grad, weight, inv, search, covs, raw, cov_sem, sem):
     weeks, rows, cols = latent.shape
     mask = masks(weeks)
     copy = pltpu.make_async_copy(counts, raw, sem)
@@ -164,6 +165,9 @@
     cov_copy.start()
     copy.start()
     rows_first(latent, field, 2)
+    for r in range(rows):
+        kappa[r + 3] = kappa_flat[r : r + 1, :]
+        land[r] = land_flat[r : r + 1, :].astype(F32)
 
     def inner_image(r, _):
         put_row(image, r + 1, laplace_row(
@@ -183,23 +187,29 @@
             eta[r, :, c : c + width] = total[r : r + 1]
     copy.wait()
     rows_first(raw, tally, 0)
+    for r in (0, 1, rows - 2, rows - 1):
+        gradient_row(r, field, tally, eta, land, kappa, None, grad, weight, inv, search, mask)
+    for r in (2, 3, rows - 4, rows - 3):
+        gradient_row(r, field, tally, eta, land, kappa, image, grad, weight, inv, search, mask)
 
 
 def gradient_row(r, field, tally, eta, land, kappa, image, grad, weight, inv, search, mask):
-    outer = laplace_row(row_of(image, r), row_of(image, r + 1), row_of(image, r + 2), map_row(kappa, r + 3), mask)
     eta_row, land_row, kap, count_row = map_row(eta, r), map_row(land, r), map_row(kappa, r + 3), row_of(tally, r)
+    if image is not None:
+        outer = laplace_row(row_of(image, r), row_of(image, r + 1), row_of(image, r + 2), kap, mask)
     for j, tile in enumerate(row_of(field, r + 2)):
         on = land_row[j]
         curve = jnp.tanh(0.5 * (tile + eta_row[j]))
         heavy = on * (1.0 - curve * curve)
         inverse = 1.0 / (diag_base(kap[j]) + heavy)
         out = on * (count_row[j] - 2.0 - 2.0 * curve) - time_coupling * temporal_tile(tile, mask)
-        out = out - prior_scale * outer[j]
         part = slice(j * LANES, (j + 1) * LANES)
         weight[r + 2, :, part] = heavy
         inv[r + 2, :, part] = inverse
+        if image is not None:
+            out = out - prior_scale * outer[j]
+            search[r + 4, :, part] = out * inverse
         grad[r, :, part] = out
-        search[r + 4, :, part] = out * inverse
 
 
 def keep_inside(r, rows, tiles):
@@ -225,8 +235,8 @@
             for c in range(0, first.shape[1], LANES)]
 
 
-def edge_kernel(got_first, got_second, eta, land, tally, kappa_in, field_in, image_in,
-                kappa, field, image, grad, weight, inv, search, first, second):
+def edge_kernel(got_second, got_first, eta, inv, kappa_in, field_in, image_in, grad_in, search_in,
+                kappa, field, image, grad, search, first, second):
     weeks = field.shape[1]
     rows, _, cols = eta.shape
     mask = masks(weeks)
@@ -240,8 +250,11 @@
     for r in (-1, 0, rows - 1, rows):
         put_row(image, r + 1, keep_inside(r, rows, laplace_row(
             row_of(field, r + 1), row_of(field, r + 2), row_of(field, r + 3), map_row(kappa, r + 3), mask)))
-    for r in (0, 1, 2, 3, rows - 4, rows - 3, rows - 2, rows - 1):
-        gradient_row(r, field, tally, eta, land, kappa, image, grad, weight, inv, search, mask)
+    for r in (0, 1, rows - 2, rows - 1):
+        outer = laplace_row(row_of(image, r), row_of(image, r + 1), row_of(image, r + 2), map_row(kappa, r + 3), mask)
+        out = [a - prior_scale * b for a, b in zip(row_of(grad, r), outer)]
+        put_row(grad, r, out)
+        put_row(search, r + 4, [a * b for a, b in zip(out, row_of(inv, r + 2))])
     at = 4 * weeks
     for c in range(0, cols, LANES):
         part = slice(c, c + LANES)
@@ -312,7 +325,7 @@
         sums[8 * k : 8 * k + 8, :] = value
 
 
-def outer_kernel(old_first, old_second, got_first, got_second, kappa, field, grad, partial,
+def outer_kernel(old_second, old_first, got_second, got_first, kappa, field, grad, partial,
                  weight_in, inv_in, search_in, first_in, image_in, second_in, second_image_in,
                  weight, inv, search, first, image, second, second_image, sums):
     weeks = grad.shape[1]
@@ -424,29 +437,29 @@
     cells = weeks * rows * cols
     SMEM, ANY, HBM, DMA = pltpu.SMEM, pl.ANY, pltpu.HBM, pltpu.SemaphoreType.DMA
     packed = ((2 * weeks + 5, cols), VMEM)
-    near, far, kappa, land = call(
+    near, far = call(
         pack_kernel,
-        [packed, packed, maps(3), maps(0)],
+        [packed, packed],
         [(latent, HBM), (kappa_sq, HBM), (land_mask, HBM)],
-        scratch=[pltpu.VMEM((rows, cols), F32), pltpu.VMEM((rows, cols), jnp.int32), DMA((6,))],
+        scratch=[pltpu.VMEM((16, cols), F32), pltpu.VMEM((16, cols), jnp.int32), DMA((8,))],
         flops=cells // 16, moved=cells,
     )
     old_near, old_far = swap_rows(near, far)
-    field, image, eta, tally = call(
+    field, image, eta, tally, kappa, land, grad, weight, inv, search = call(
         front_kernel,
-        [ext(2), ext(1), maps(0), ext(0)],
+        [ext(2), ext(1), maps(0), ext(0), maps(3), maps(0), ext(0), ext(2), ext(2), ext(4)],
         [(effects.astype(F32), SMEM), (intercepts, SMEM), (latent, VMEM), (covariates, HBM),
-         (region_ids, VMEM), (kappa, VMEM), (counts, HBM)],
+         (region_ids, VMEM), (kappa_sq, VMEM), (land_mask, VMEM), (counts, HBM)],
         scratch=[pltpu.VMEM(covariates.shape, covariates.dtype), pltpu.VMEM(counts.shape, jnp.int32), DMA, DMA],
         flops=40 * cells, moved=12 * cells, limit=8,
     )
     packed = ((4 * weeks + 2, cols), VMEM)
-    kappa, field, image, grad, weight, inv, search, near, far = call(
+    kappa, field, image, grad, search, near, far = call(
         edge_kernel,
-        [maps(3), ext(2), ext(1), ext(0), ext(2), ext(2), ext(4), packed, packed],
-        [(old_near, VMEM), (old_far, VMEM), (eta, VMEM), (land, VMEM), (tally, VMEM),
-         (kappa, VMEM), (field, VMEM), (image, VMEM)],
-        aliases={5 + k: k for k in range(3)},
+        [maps(3), ext(2), ext(1), ext(0), ext(4), packed, packed],
+        [(old_far, VMEM), (old_near, VMEM), (eta, VMEM), (inv, VMEM),
+         (kappa, VMEM), (field, VMEM), (image, VMEM), (grad, VMEM), (search, VMEM)],
+        aliases={4 + k: k for k in range(5)},
         flops=10 * cells, moved=cells,
     )
     near, far = swap_rows(near, far)
@@ -461,7 +474,7 @@
     weight, inv, search, first, image, second, second_image, sums = call(
         outer_kernel,
         [ext(2), ext(2), ext(4), ext(3), ext(0), ext(2), ext(1), ((8, LANES), VMEM)],
-        [(old_near, VMEM), (old_far, VMEM), (near, VMEM), (far, VMEM), (kappa, VMEM), (field, VMEM),
+        [(old_far, VMEM), (old_near, VMEM), (far, VMEM), (near, VMEM), (kappa, VMEM), (field, VMEM),
          (grad, VMEM), (partial, VMEM), (weight, VMEM), (inv, VMEM), (search, VMEM), (first, VMEM), (image, VMEM),
          (second, VMEM), (second_image, VMEM)],
         aliases={8 + k: k for k in range(7)},

time: 40.9 us -> 39.9 us (0.976)
  starting transfers between devices: 18 us -> 15.3 us
  local copies, waits for them, and re-layouts: 0.02 us -> 0.92 us
  waiting for transfers between devices: 3.86 us -> 4.62 us
    ppermute x4, starting transfers between devices: 12.3 us -> 6.66 us  [all_sum(): got = lax.ppermute(values, AX, [(i, i ^ step) for i in range(count)])]
    ppermute x2, starting transfers between devices: 4.45 us -> 7.31 us  [swap_rows(): return (lax.ppermute(near, AX, swap), far)]
    unnamed x8 -> x12, local copies, waits for them, and re-layouts: 0.02 us -> 0.92 us
    ppermute x4, waiting for transfers between devices: 3.85 us -> 4.6 us  [all_sum(): got = lax.ppermute(values, AX, [(i, i ^ step) for i in range(count)])]
  transfers between devices with their start and end apart: 8 -> 8, of which waited for: 4 -> 4; matrix products, arithmetic and copies ran while one was open for 0% -> 0% of each run, Pallas kernels for 29% -> 31%
where the time goes in v6:
time: 39.9 us; the launch traced here: 39.8 us
  Pallas kernels  18.1 us (45%)
  starting transfers between devices  15.3 us (38%)
  waiting for transfers between devices  4.62 us (12%)
  local copies, waits for them, and re-layouts  0.92 us (2%)
  between operations  0.8 us (2%)
    pallas_call x8, Pallas kernels, call(): pl.pallas_call(kernel, out_shape=shapes, in_specs=[pl.BlockSpec(memory_sp...  18.1 us
    ppermute x2, starting transfers between devices, swap_rows(): return (lax.ppermute(near, AX, swap), far)  7.31 us
    ppermute x4, starting transfers between devices, all_sum(): got = lax.ppermute(values, AX, [(i, i ^ step) for i in range(count)])  6.66 us
    ppermute x4, waiting for transfers between devices, all_sum(): got = lax.ppermute(values, AX, [(i, i ^ step) for i in range(count)])  4.6 us
    ppermute x2, starting transfers between devices, swap_rows(): far = lax.ppermute(far, AX, cross)  1.35 us
    unnamed x12, local copies, waits for them, and re-layouts  0.92 us
  transfers between devices with their start and end apart: 8, of which 4 were waited for; matrix products, arithmetic and copies ran while one was open for 0% of the time, Pallas kernels for 31%

profile of v6, /device:TPU:0, one launch (start us, length us, event | category | flops | bytes accessed | tf_op | source)
XLA Modules:
  0.0 39.8 jit_solution(5994287349009655138)
XLA Ops:
  0.6 0.0 copy-start.1
  0.6 0.0 copy-start.2
  0.7 0.0 copy-start
  0.7 0.0 copy-start.5
  0.7 0.0 copy-start.4
  0.7 1.2 %shard_map.95 = (f32[37,1024]{1,0:T(8,128)S(1)}, f32[37,1024]{1,0:T(8,128)S(1)}) custom-call(f32[16,32,1024]{2,1,0:T(8,128)} %latent.3, f32[32,1024]{1,0:T(8,128)} %kappa_flat.1, s32[32,1024]{1,0:T(8,128)} %land_flat.1), custom_call_target="tpu_custom_call" | custom-call | flops 32768 | bytes 524288 | tf_op jit(solution)/shard_map/pallas_call | solution.py:416
  1.9 0.7 %collective-permute-start = (f32[37,1024]{1,0:T(8,128)S(1)}, f32[37,1024]{1,0:T(8,128)S(1)}, u32[]{:S(2)}, u32[]{:S(2)}) collective-permute-start(f32[37,1024]{1,0:T(8,128)S(1)} %get-tuple-element.40), channel_id=1, source_target_pairs={{1,2},{2,1},{3,4},{4,3},{5,6},{6,5},{7,8},{8,7},{9,10},{10,9},{11,... | collective-permute-start | bytes 454664 | tf_op jit(solution)/shard_map/ppermute | solution.py:27
  2.6 4.4 %collective-permute-start.1 = (f32[37,1024]{1,0:T(8,128)S(1)}, f32[37,1024]{1,0:T(8,128)S(1)}, u32[]{:S(2)}, u32[]{:S(2)}) collective-permute-start(f32[37,1024]{1,0:T(8,128)S(1)} %get-tuple-element.41), channel_id=1, source_target_pairs={{0,1},{1,0},{2,3},{3,2},{4,5},{5,4},{6,7},{7,6},{8,9},{9,8},{10,11... | collective-permute-start | bytes 454664 | tf_op jit(solution)/shard_map/ppermute | solution.py:28
  6.9 0.0 copy-done.5
  6.9 0.0 copy-done.1
  7.0 0.0 copy-done.2
  7.0 0.0 copy-done
  7.0 0.0 copy-done.4
  7.0 0.0 copy-start.3
  7.0 0.9 %copy-done.3 = s32[32,1024]{1,0:T(8,128)S(1)} copy-done((s32[32,1024]{1,0:T(8,128)S(1)}, s32[32,1024]{1,0:T(8,128)}, u32[]{:S(2)}) %copy-start.3) | copy-done | bytes 131096
  7.9 3.8 %shard_map.96 = (f32[36,16,1024]{2,1,0:T(8,128)S(1)}, f32[34,16,1024]{2,1,0:T(8,128)S(1)}, f32[32,1,1024]{2,1,0:T(1,128)S(1)}, f32[32,16,1024]{2,1,0:T(8,128)S(1...) custom-call(f32[32]{0:T(128)S(1)} %convert_element_type.3.effects, ...), custom_call_target="tpu_custom_call" | custom-call | flops 20971520 | bytes 6291456 | tf_op jit(solution)/shard_map/pallas_call | solution.py:416
  11.7 0.0 collective-permute-done.got_second.old_second
  11.7 0.0 collective-permute-done.1.got_first.old_first
  11.7 0.4 %shard_map.97 = (f32[38,1,1024]{2,1,0:T(1,128)S(1)}, f32[36,16,1024]{2,1,0:T(8,128)S(1)}, f32[34,16,1024]{2,1,0:T(8,128)S(1)}, f32[32,16,1024]{2,1,0:T(8,128)S(1...) custom-call(f32[37,1024]{1,0:T(8,128)S(1)} %collective-permute-done., ...), custom_call_target="tpu_custom_call", output_to_operand_aliasing={{0}: (4, {}), {1}: (5, {}), {2}: (6, {}), {3}: (7, {}), {4}... | custom-call | flops 5242880 | bytes 524288 | tf_op jit(solution)/shard_map/pallas_call | solution.py:416
  12.1 0.7 %collective-permute-start.2 = (f32[66,1024]{1,0:T(8,128)S(1)}, f32[66,1024]{1,0:T(8,128)S(1)}, u32[]{:S(2)}, u32[]{:S(2)}) collective-permute-start(f32[66,1024]{1,0:T(8,128)S(1)} %get-tuple-element.49), channel_id=1, source_target_pairs={{1,2},{2,1},{3,4},{4,3},{5,6},{6,5},{7,8},{8,7},{9,10},{10,9},{11,... | collective-permute-start | bytes 811016 | tf_op jit(solution)/shard_map/ppermute | solution.py:27
  12.8 3.0 %collective-permute-start.3 = (f32[66,1024]{1,0:T(8,128)S(1)}, f32[66,1024]{1,0:T(8,128)S(1)}, u32[]{:S(2)}, u32[]{:S(2)}) collective-permute-start(f32[66,1024]{1,0:T(8,128)S(1)} %get-tuple-element.50), channel_id=1, source_target_pairs={{0,1},{1,0},{2,3},{3,2},{4,5},{5,4},{6,7},{7,6},{8,9},{9,8},{10,11... | collective-permute-start | bytes 811016 | tf_op jit(solution)/shard_map/ppermute | solution.py:28
  15.8 7.0 %shard_map.98 = (f32[32,16,1024]{2,1,0:T(8,128)S(1)}, f32[36,16,1024]{2,1,0:T(8,128)S(1)}, f32[36,16,1024]{2,1,0:T(8,128)S(1)}, f32[40,16,1024]{2,1,0:T(8,128)S(...) custom-call(f32[38,1,1024]{2,1,0:T(1,128)S(1)} %get-tuple-element.51, ...), custom_call_target="tpu_custom_call", output_to_operand_aliasing={{0}: (6, {}), {1}: (7, {}), {2}: (8, {}), {3}: (9, {})} | custom-call | flops 62914560 | bytes 6291456 | tf_op jit(solution)/shard_map/pallas_call | solution.py:416
  22.8 0.0 collective-permute-done.2.got_second
  22.8 0.0 collective-permute-done.3.got_first
  22.8 1.3 %shard_map.99 = (f32[36,16,1024]{2,1,0:T(8,128)S(1)}, f32[36,16,1024]{2,1,0:T(8,128)S(1)}, f32[40,16,1024]{2,1,0:T(8,128)S(1)}, f32[38,16,1024]{2,1,0:T(8,128)S(...) custom-call(f32[37,1024]{1,0:T(8,128)S(1)} %collective-permute-done., ...), custom_call_target="tpu_custom_call", output_to_operand_aliasing={{0}: (8, {}), {1}: (9, {}), {2}: (10, {}), {3}: (11, {}), {... | custom-call | flops 10485760 | bytes 524288 | tf_op jit(solution)/shard_map/pallas_call | solution.py:416
  24.1 0.1 collective-permute-start.4
  24.2 1.1 %collective-permute-done.4 = f32[8,128]{1,0:T(8,128)S(1)} collective-permute-done((f32[8,128]{1,0:T(8,128)S(1)}, f32[8,128]{1,0:T(8,128)S(1)}, u32[]{:S(2)}, u32[]{:S(2)}) %collective-permute-start.4) | collective-permute-done | bytes 4128 | tf_op jit(solution)/shard_map/ppermute | solution.py:38
  25.3 2.1 %collective-permute-start.5 = (f32[8,128]{1,0:T(8,128)S(1)}, f32[8,128]{1,0:T(8,128)S(1)}, u32[]{:S(2)}, u32[]{:S(2)}) collective-permute-start(f32[8,128]{1,0:T(8,128)S(1)} %add.12.gate), channel_id=1, source_target_pairs={{0,2},{1,3},{2,0},{3,1},{4,6},{5,7},{6,4},{7,5},{8,10},{9,11},{10,... | collective-permute-start | bytes 12296 | tf_op jit(solution)/shard_map/ppermute | solution.py:38
  27.4 0.9 %shard_map.100.upper = f32[16,16,1024]{2,1,0:T(8,128)S(1)} custom-call(f32[8,128]{1,0:T(8,128)S(1)} %add.12.gate, f32[38,1,1024]{2,1,0:T(1,128)S(1)} %get-tuple-element.51.kappa, f32[36,16,1024]{2,1,0:T(8,128)S(1)} %get-tuple-element.69.weight, f32[36,16,1024]{2,1,0:T(8,128)S(1)} %get-tuple-element.70.second, f32[34,16,1024]{2,1,0:T(8,128)S(1)} %get-tuple-element.71.second_image), custom_call_target="tpu_custom_call" | custom-call | flops 2097152 | bytes 524288 | tf_op jit(solution)/shard_map/pallas_call | solution.py:416
  28.3 0.7 %collective-permute-done.5 = f32[8,128]{1,0:T(8,128)S(1)} collective-permute-done((f32[8,128]{1,0:T(8,128)S(1)}, f32[8,128]{1,0:T(8,128)S(1)}, u32[]{:S(2)}, u32[]{:S(2)}) %collective-permute-start.5) | collective-permute-done | bytes 4128 | tf_op jit(solution)/shard_map/ppermute | solution.py:38
  29.0 1.7 %collective-permute-start.6 = (f32[8,128]{1,0:T(8,128)S(1)}, f32[8,128]{1,0:T(8,128)S(1)}, u32[]{:S(2)}, u32[]{:S(2)}) collective-permute-start(f32[8,128]{1,0:T(8,128)S(1)} %add.13.gate), channel_id=1, source_target_pairs={{0,4},{1,5},{2,6},{3,7},{4,0},{5,1},{6,2},{7,3},{8,12},{9,13},{10,... | collective-permute-start | bytes 12296 | tf_op jit(solution)/shard_map/ppermute | solution.py:38
  30.7 0.9 %shard_map.101.lower = f32[16,16,1024]{2,1,0:T(8,128)S(1)} custom-call(f32[8,128]{1,0:T(8,128)S(1)} %add.13.gate, f32[38,1,1024]{2,1,0:T(1,128)S(1)} %get-tuple-element.51.kappa, f32[36,16,1024]{2,1,0:T(8,128)S(1)} %get-tuple-element.69.weight, f32[36,16,1024]{2,1,0:T(8,128)S(1)} %get-tuple-element.70.second, f32[34,16,1024]{2,1,0:T(8,128)S(1)} %get-tuple-element.71.second_image), custom_call_target="tpu_custom_call" | custom-call | flops 2097152 | bytes 524288 | tf_op jit(solution)/shard_map/pallas_call | solution.py:416
  31.6 1.0 %collective-permute-done.6 = f32[8,128]{1,0:T(8,128)S(1)} collective-permute-done((f32[8,128]{1,0:T(8,128)S(1)}, f32[8,128]{1,0:T(8,128)S(1)}, u32[]{:S(2)}, u32[]{:S(2)}) %collective-permute-start.6) | collective-permute-done | bytes 4128 | tf_op jit(solution)/shard_map/ppermute | solution.py:38
  32.6 2.8 %collective-permute-start.7 = (f32[8,128]{1,0:T(8,128)S(1)}, f32[8,128]{1,0:T(8,128)S(1)}, u32[]{:S(2)}, u32[]{:S(2)}) collective-permute-start(f32[8,128]{1,0:T(8,128)S(1)} %add.14), channel_id=1, source_target_pairs={{0,8},{1,9},{2,10},{3,11},{4,12},{5,13},{6,14},{7,15},{8,0},{9,1},... | collective-permute-start | bytes 12296 | tf_op jit(solution)/shard_map/ppermute | solution.py:38
  35.4 1.7 %collective-permute-done.7 = f32[8,128]{1,0:T(8,128)S(1)} collective-permute-done((f32[8,128]{1,0:T(8,128)S(1)}, f32[8,128]{1,0:T(8,128)S(1)}, u32[]{:S(2)}, u32[]{:S(2)}) %collective-permute-start.7) | collective-permute-done | bytes 4128 | tf_op jit(solution)/shard_map/ppermute | solution.py:38
  37.1 2.7 %shard_map.102 = (f32[16,32,1024]{2,1,0:T(8,128)}, f32[16,32,1024]{2,1,0:T(8,128)}) custom-call(f32[8,128]{1,0:T(8,128)S(1)} %add.15.sums, f32[32,16,1024]{2,1,0:T(8,128)S(1)} %get-tuple-element.59.grad, f32[40,16,1024]{2,1,0:T(8,128)S(1)} %get-tuple-element.74.search, f32[32,16,1024]{2,1,0:T(8,128)S(1)} %get-tuple-element.75.image, ...), custom_call_target="tpu_custom_call" | custom-call | flops 4194304 | bytes 4194304 | tf_op jit(solution)/shard_map/pallas_call | solution.py:416
  (5 shorter events, 0.0 us)
Async XLA Ops:
  0.6 6.3 %copy-start.1 = (f32[32,1024]{1,0:T(8,128)S(1)}, f32[32,1024]{1,0:T(8,128)}, u32[]{:S(2)}) copy-start(f32[32,1024]{1,0:T(8,128)} %kappa_flat.1) | copy-start | bytes 393220
  0.6 6.3 %copy-start.2 = (s32[32,1024]{1,0:T(8,128)S(1)}, s32[32,1024]{1,0:T(8,128)}, u32[]{:S(2)}) copy-start(s32[32,1024]{1,0:T(8,128)} %land_flat.1) | copy-start | bytes 393220
  0.7 6.3 %copy-start = (f32[16,32,1024]{2,1,0:T(8,128)S(1)}, f32[16,32,1024]{2,1,0:T(8,128)}, u32[]{:S(2)}) copy-start(f32[16,32,1024]{2,1,0:T(8,128)} %latent.3) | copy-start | bytes 6291460
  0.7 6.3 %copy-start.5 = (bf16[32]{0:T(256)(128)(2,1)S(1)}, bf16[32]{0:T(256)(128)(2,1)}, u32[]{:S(2)}) copy-start(bf16[32]{0:T(256)(128)(2,1)} %param.14) | copy-start | bytes 196
  0.7 6.3 %copy-start.4 = (f32[8]{0:T(128)S(1)}, f32[8]{0:T(128)}, u32[]{:S(2)}) copy-start(f32[8]{0:T(128)} %intercepts.1) | copy-start | bytes 100
  1.9 9.8 %collective-permute-start = (f32[37,1024]{1,0:T(8,128)S(1)}, f32[37,1024]{1,0:T(8,128)S(1)}, u32[]{:S(2)}, u32[]{:S(2)}) collective-permute-start(f32[37,1024]{1,0:T(8,128)S(1)} %get-tuple-element.40), channel_id=1, source_target_pairs={{1,2},{2,1},{3,4},{4,3},{5,6},{6,5},{7,8},{8,7},{9,10},{10,9},{11,... | collective-permute-start | bytes 454664 | tf_op jit(solution)/shard_map/ppermute | solution.py:27
  2.6 9.1 %collective-permute-start.1 = (f32[37,1024]{1,0:T(8,128)S(1)}, f32[37,1024]{1,0:T(8,128)S(1)}, u32[]{:S(2)}, u32[]{:S(2)}) collective-permute-start(f32[37,1024]{1,0:T(8,128)S(1)} %get-tuple-element.41), channel_id=1, source_target_pairs={{0,1},{1,0},{2,3},{3,2},{4,5},{5,4},{6,7},{7,6},{8,9},{9,8},{10,11... | collective-permute-start | bytes 454664 | tf_op jit(solution)/shard_map/ppermute | solution.py:28
  7.0 0.9 %copy-start.3 = (s32[32,1024]{1,0:T(8,128)S(1)}, s32[32,1024]{1,0:T(8,128)}, u32[]{:S(2)}) copy-start(s32[32,1024]{1,0:T(8,128)} %zones.1) | copy-start | bytes 393220
  12.1 10.7 %collective-permute-start.2 = (f32[66,1024]{1,0:T(8,128)S(1)}, f32[66,1024]{1,0:T(8,128)S(1)}, u32[]{:S(2)}, u32[]{:S(2)}) collective-permute-start(f32[66,1024]{1,0:T(8,128)S(1)} %get-tuple-element.49), channel_id=1, source_target_pairs={{1,2},{2,1},{3,4},{4,3},{5,6},{6,5},{7,8},{8,7},{9,10},{10,9},{11,... | collective-permute-start | bytes 811016 | tf_op jit(solution)/shard_map/ppermute | solution.py:27
  12.8 10.0 %collective-permute-start.3 = (f32[66,1024]{1,0:T(8,128)S(1)}, f32[66,1024]{1,0:T(8,128)S(1)}, u32[]{:S(2)}, u32[]{:S(2)}) collective-permute-start(f32[66,1024]{1,0:T(8,128)S(1)} %get-tuple-element.50), channel_id=1, source_target_pairs={{0,1},{1,0},{2,3},{3,2},{4,5},{5,4},{6,7},{7,6},{8,9},{9,8},{10,11... | collective-permute-start | bytes 811016 | tf_op jit(solution)/shard_map/ppermute | solution.py:28
  24.1 1.2 %collective-permute-start.4 = (f32[8,128]{1,0:T(8,128)S(1)}, f32[8,128]{1,0:T(8,128)S(1)}, u32[]{:S(2)}, u32[]{:S(2)}) collective-permute-start(f32[8,128]{1,0:T(8,128)S(1)} %get-tuple-element.68), channel_id=1, source_target_pairs={{0,1},{1,0},{2,3},{3,2},{4,5},{5,4},{6,7},{7,6},{8,9},{9,8},{10,11... | collective-permute-start | bytes 12296 | tf_op jit(solution)/shard_map/ppermute | solution.py:38
  25.3 3.6 %collective-permute-start.5 = (f32[8,128]{1,0:T(8,128)S(1)}, f32[8,128]{1,0:T(8,128)S(1)}, u32[]{:S(2)}, u32[]{:S(2)}) collective-permute-start(f32[8,128]{1,0:T(8,128)S(1)} %add.12.gate), channel_id=1, source_target_pairs={{0,2},{1,3},{2,0},{3,1},{4,6},{5,7},{6,4},{7,5},{8,10},{9,11},{10,... | collective-permute-start | bytes 12296 | tf_op jit(solution)/shard_map/ppermute | solution.py:38
  29.0 3.6 %collective-permute-start.6 = (f32[8,128]{1,0:T(8,128)S(1)}, f32[8,128]{1,0:T(8,128)S(1)}, u32[]{:S(2)}, u32[]{:S(2)}) collective-permute-start(f32[8,128]{1,0:T(8,128)S(1)} %add.13.gate), channel_id=1, source_target_pairs={{0,4},{1,5},{2,6},{3,7},{4,0},{5,1},{6,2},{7,3},{8,12},{9,13},{10,... | collective-permute-start | bytes 12296 | tf_op jit(solution)/shard_map/ppermute | solution.py:38
  32.6 4.5 %collective-permute-start.7 = (f32[8,128]{1,0:T(8,128)S(1)}, f32[8,128]{1,0:T(8,128)S(1)}, u32[]{:S(2)}, u32[]{:S(2)}) collective-permute-start(f32[8,128]{1,0:T(8,128)S(1)} %add.14), channel_id=1, source_target_pairs={{0,8},{1,9},{2,10},{3,11},{4,12},{5,13},{6,14},{7,15},{8,0},{9,1},... | collective-permute-start | bytes 12296 | tf_op jit(solution)/shard_map/ppermute | solution.py:38

commit v7 on v6

--- a/solution.py
+++ b/solution.py
@@ -157,11 +157,13 @@
 
 
 def front_kernel(effects, intercepts, latent, covariates, zones, kappa_flat, land_flat, counts,
-                 field, image, eta, tally, kappa, land, grad, weight, inv, search, covs, raw, cov_sem, sem):
+                 field, image, eta, tally, kappa, land, grad, weight, inv, search, covs, raw, ids_all, cov_sem, sem, zone_sem):
     weeks, rows, cols = latent.shape
     mask = masks(weeks)
     copy = pltpu.make_async_copy(counts, raw, sem)
     cov_copy = pltpu.make_async_copy(covariates, covs, cov_sem)
+    zone_copy = pltpu.make_async_copy(zones, ids_all, zone_sem)
+    zone_copy.start()
     cov_copy.start()
     copy.start()
     rows_first(latent, field, 2)
@@ -174,11 +176,12 @@
             row_of(field, r + 1), row_of(field, r + 2), row_of(field, r + 3), map_row(kappa, r + 3), mask))
 
     row_loop(1, rows - 1, inner_image)
+    zone_copy.wait()
     cov_copy.wait()
     width = 2 * LANES
     for c in range(0, cols, width):
         total = jnp.zeros((rows, width), F32)
-        ids = zones[:, c : c + width]
+        ids = ids_all[:, c : c + width]
         for z in range(intercepts.shape[0]):
             total = jnp.where(ids == z, intercepts[z], total)
         for k in range(covs.shape[0]):
@@ -346,11 +349,11 @@
             put_row(weight, r + 2, heavy)
             put_row(inv, r + 2, [1.0 / (diag_base(k) + h) for k, h in zip(map_row(kappa, r + 3), heavy)])
 
-    for r in (-3, -2, -1, 0, rows - 1, rows, rows + 1, rows + 2):
+    for r in (-2, -1, 0, rows - 1, rows, rows + 1):
         put_row(first, r + 3, keep_inside(r, rows, laplace_row(
             row_of(search, r + 3), row_of(search, r + 4), row_of(search, r + 5), map_row(kappa, r + 3), mask)))
     rz, pq, cross, total = (partial[8 * k : 8 * k + 8, :] for k in range(4))
-    for r in (-2, -1, 0, 1, rows - 2, rows - 1, rows, rows + 1):
+    for r in (-1, 0, 1, rows - 2, rows - 1, rows):
         mid, out = hessian_row(r, search, r + 4, first, 3, kappa, weight, mask)
         other = keep_inside(r, rows, [a * b for a, b in zip(out, row_of(inv, r + 2))])
         put_row(second, r + 2, other)
@@ -359,12 +362,11 @@
             mass = [time_coupling * temporal_tile(y, mask) + h * y for y, h in zip(other, row_of(weight, r + 2))]
             rz, pq, cross = rz + dot_rows(mid, row_of(grad, r)), pq + dot_rows(mid, out), cross + dot_rows(other, out)
             total = total + dot_rows(other, mass)
-    for r in (-1, 0, 1, 2, rows - 3, rows - 2, rows - 1, rows):
-        out = keep_inside(r, rows, laplace_row(
-            row_of(second, r + 1), row_of(second, r + 2), row_of(second, r + 3), map_row(kappa, r + 3), mask))
+    for r in (0, 1, 2, rows - 3, rows - 2, rows - 1):
+        out = laplace_row(
+            row_of(second, r + 1), row_of(second, r + 2), row_of(second, r + 3), map_row(kappa, r + 3), mask)
         put_row(second_image, r + 1, out)
-        if 0 <= r < rows:
-            total = total + prior_scale * dot_rows(out, out)
+        total = total + prior_scale * dot_rows(out, out)
     sums[...] = jnp.zeros_like(sums)
     for k, value in enumerate((rz, pq, cross, total)):
         sums[k : k + 1, :] = jnp.sum(value, axis=0, keepdims=True)
@@ -379,15 +381,39 @@
     row_loop(0, last.shape[0], apply, most=8)
 
 
-def final_kernel(sums, grad, search, image, second, upper, lower, newton_out, residual_out, newton, residual, newton_sem, residual_sem):
+def rim_kernel(gate, kappa, weight, inv, search, first, second, second_image, last):
+    rows = second_image.shape[0] - 2
+    count = last.shape[0] - 1
+    mask = masks(last.shape[1])
+    for r, away in ((0, -1), (rows - 1, 1)):
+        rim = [r + away * d for d in range(5)]
+        tiles = keep_inside(rim[3], rows, laplace_row(
+            row_of(search, rim[4] + 4), row_of(search, rim[3] + 4), row_of(search, rim[2] + 4),
+            map_row(kappa, rim[3] + 3), mask))
+        outer = laplace_row(tiles, row_of(first, rim[2] + 3), row_of(first, rim[1] + 3), map_row(kappa, rim[2] + 3), mask)
+        mass = mass_row(rim[2], search, rim[2] + 4, weight, mask)[1]
+        tiles = keep_inside(rim[2], rows, [
+            (prior_scale * o + m) * d for o, m, d in zip(outer, mass, row_of(inv, rim[2] + 2))])
+        tiles = keep_inside(rim[1], rows, laplace_row(
+            tiles, row_of(second, rim[1] + 2), row_of(second, r + 2), map_row(kappa, rim[1] + 3), mask))
+        outer = laplace_row(
+            tiles, row_of(second_image, r + 1), row_of(second_image, r - away + 1), map_row(kappa, r + 3), mask)
+        mass = mass_row(r, second, r + 2, weight, mask)[1]
+        put_row(last, 0 if r == 0 else count, [prior_scale * o + m for o, m in zip(outer, mass)])
+
+    def apply(r, _):
+        put_row(last, r, hessian_row(r, second, r + 2, second_image, 1, kappa, weight, mask)[1])
+
+    row_loop(1, count, apply, most=8)
+
+
+def final_kernel(sums, grad, search, image, second, rim, upper, lower, newton_out, residual_out, newton, residual, newton_sem, residual_sem):
     rows, weeks, cols = grad.shape
     rz, pq, cross, total = (jnp.sum(sums[k : k + 1, :], axis=1, keepdims=True) for k in range(4))
-    first_step = rz / pq
-    rz_next = first_step * first_step * cross - rz
-    turn = 1.0 + rz_next / rz
-    second_step = rz_next / (turn * (turn * pq - 2.0 * first_step * cross) + first_step * first_step * total)
-    along = jnp.broadcast_to(first_step + second_step * turn, (weeks, LANES))
-    across = jnp.broadcast_to(second_step * first_step, (weeks, LANES))
+    first, cross, total = rz / pq, cross / pq, total / pq
+    scale = 1.0 / (total - cross * cross)
+    along = jnp.broadcast_to((first * total - cross) * scale, (weeks, LANES))
+    across = jnp.broadcast_to((first * cross - 1.0) * scale, (weeks, LANES))
 
     def copies(r):
         return (
@@ -395,7 +421,8 @@
             pltpu.make_async_copy(residual.at[r], residual_out.at[:, r, :], residual_sem.at[r]),
         )
 
-    half = upper.shape[0]
+    one = rim.shape[0] - 1
+    two = one + upper.shape[0]
 
     def combine(r, last, at):
         put_row(newton, r, [along * p - across * y for p, y in zip(row_of(search, r + 4), row_of(second, r + 2))])
@@ -404,8 +431,10 @@
         for copy in copies(r):
             copy.start()
 
-    row_loop(0, half, lambda r, _: combine(r, upper, 0), most=8)
-    row_loop(half, rows, lambda r, _: combine(r, lower, half), most=8)
+    row_loop(0, one, lambda r, _: combine(r, rim, 0), most=7)
+    row_loop(one, two, lambda r, _: combine(r, upper, one), most=7)
+    row_loop(two, rows - 1, lambda r, _: combine(r, lower, two), most=7)
+    combine(rows - 1, rim, rows - 1 - one)
     for r in range(rows):
         for copy in copies(r):
             copy.wait()
@@ -449,8 +478,9 @@
         front_kernel,
         [ext(2), ext(1), maps(0), ext(0), maps(3), maps(0), ext(0), ext(2), ext(2), ext(4)],
         [(effects.astype(F32), SMEM), (intercepts, SMEM), (latent, VMEM), (covariates, HBM),
-         (region_ids, VMEM), (kappa_sq, VMEM), (land_mask, VMEM), (counts, HBM)],
-        scratch=[pltpu.VMEM(covariates.shape, covariates.dtype), pltpu.VMEM(counts.shape, jnp.int32), DMA, DMA],
+         (region_ids, HBM), (kappa_sq, VMEM), (land_mask, VMEM), (counts, HBM)],
+        scratch=[pltpu.VMEM(covariates.shape, covariates.dtype), pltpu.VMEM(counts.shape, jnp.int32),
+                 pltpu.VMEM((rows, cols), jnp.int32), DMA, DMA, DMA],
         flops=40 * cells, moved=12 * cells, limit=8,
     )
     packed = ((4 * weeks + 2, cols), VMEM)
@@ -480,7 +510,17 @@
         aliases={8 + k: k for k in range(7)},
         flops=20 * cells, moved=cells,
     )
-    half = rows // 2
+    one = 1 + (rows - 2) // 5
+    two = one + (rows - 1 - one) // 2
+
+    def rim_rows(gate):
+        return call(
+            rim_kernel,
+            [((one + 1, weeks, cols), VMEM)],
+            [(gate, VMEM), (kappa, VMEM), (weight, VMEM), (inv, VMEM), (search, VMEM), (first, VMEM), (second, VMEM),
+             (second_image, VMEM)],
+            flops=4 * cells, moved=cells,
+        )[0]
 
     def last_rows(low, count):
         return lambda gate: call(
@@ -490,11 +530,12 @@
             flops=4 * cells, moved=cells,
         )[0]
 
-    sums, (upper, lower) = all_sum(sums, [last_rows(0, half), last_rows(half, rows - half)])
+    sums, (rim, upper, lower) = all_sum(sums, [rim_rows, last_rows(one, two - one), last_rows(two, rows - 1 - two)])
     return call(
         final_kernel,
         [(latent.shape, ANY), (latent.shape, ANY)],
-        [(sums, VMEM), (grad, VMEM), (search, VMEM), (image, VMEM), (second, VMEM), (upper, VMEM), (lower, VMEM)],
+        [(sums, VMEM), (grad, VMEM), (search, VMEM), (image, VMEM), (second, VMEM),
+         (rim, VMEM), (upper, VMEM), (lower, VMEM)],
         scratch=[pltpu.VMEM((rows, weeks, cols), F32), pltpu.VMEM((rows, weeks, cols), F32), DMA((rows,)), DMA((rows,))],
         flops=8 * cells, moved=8 * cells, limit=6,
     )

time: 39.9 us -> 39.7 us (level)
  local copies, waits for them, and re-layouts: 0.92 us -> 0.02 us
  starting transfers between devices: 15.3 us -> 15.9 us
    unnamed x12 -> x10, local copies, waits for them, and re-layouts: 0.92 us -> 0.02 us
    ppermute x2, starting transfers between devices: 7.31 us -> 8.12 us  [swap_rows(): return (lax.ppermute(near, AX, swap), far)]
    pallas_call x8 -> x9, Pallas kernels: 18.1 us -> 18.2 us  [call(): pl.pallas_call(kernel, out_shape=shapes, in_specs=[pl.BlockSpec(memory_sp...]
  transfers between devices with their start and end apart: 8 -> 8, of which waited for: 4 -> 4; matrix products, arithmetic and copies ran while one was open for 0% -> 0% of each run, Pallas kernels for 31% -> 33%
where the time goes in v7:
time: 39.7 us; the launch traced here: 39.5 us
  Pallas kernels  18.2 us (46%)
  starting transfers between devices  15.9 us (40%)
  waiting for transfers between devices  4.57 us (12%)
  between operations  0.8 us (2%)
    pallas_call x9, Pallas kernels, call(): pl.pallas_call(kernel, out_shape=shapes, in_specs=[pl.BlockSpec(memory_sp...  18.2 us
    ppermute x2, starting transfers between devices, swap_rows(): return (lax.ppermute(near, AX, swap), far)  8.12 us
    ppermute x4, starting transfers between devices, all_sum(): got = lax.ppermute(values, AX, [(i, i ^ step) for i in range(count)])  6.4 us
    ppermute x4, waiting for transfers between devices, all_sum(): got = lax.ppermute(values, AX, [(i, i ^ step) for i in range(count)])  4.56 us
    ppermute x2, starting transfers between devices, swap_rows(): far = lax.ppermute(far, AX, cross)  1.35 us
  transfers between devices with their start and end apart: 8, of which 4 were waited for; matrix products, arithmetic and copies ran while one was open for 0% of the time, Pallas kernels for 33%

profile of v7, /device:TPU:0, one launch (start us, length us, event | category | flops | bytes accessed | tf_op | source)
XLA Modules:
  0.0 39.5 jit_solution(4568283099185667532)
XLA Ops:
  0.6 0.0 copy-start.1
  0.6 0.0 copy-start.2
  0.7 0.0 copy-start
  0.7 0.0 copy-start.4
  0.7 0.0 copy-start.3
  0.7 1.2 %shard_map.95 = (f32[37,1024]{1,0:T(8,128)S(1)}, f32[37,1024]{1,0:T(8,128)S(1)}) custom-call(f32[16,32,1024]{2,1,0:T(8,128)} %latent.3, f32[32,1024]{1,0:T(8,128)} %kappa_flat.1, s32[32,1024]{1,0:T(8,128)} %land_flat.1), custom_call_target="tpu_custom_call" | custom-call | flops 32768 | bytes 524288 | tf_op jit(solution)/shard_map/pallas_call | solution.py:445
  1.9 0.7 %collective-permute-start = (f32[37,1024]{1,0:T(8,128)S(1)}, f32[37,1024]{1,0:T(8,128)S(1)}, u32[]{:S(2)}, u32[]{:S(2)}) collective-permute-start(f32[37,1024]{1,0:T(8,128)S(1)} %get-tuple-element.44), channel_id=1, source_target_pairs={{1,2},{2,1},{3,4},{4,3},{5,6},{6,5},{7,8},{8,7},{9,10},{10,9},{11,... | collective-permute-start | bytes 454664 | tf_op jit(solution)/shard_map/ppermute | solution.py:27
  2.6 4.4 %collective-permute-start.1 = (f32[37,1024]{1,0:T(8,128)S(1)}, f32[37,1024]{1,0:T(8,128)S(1)}, u32[]{:S(2)}, u32[]{:S(2)}) collective-permute-start(f32[37,1024]{1,0:T(8,128)S(1)} %get-tuple-element.45), channel_id=1, source_target_pairs={{0,1},{1,0},{2,3},{3,2},{4,5},{5,4},{6,7},{7,6},{8,9},{9,8},{10,11... | collective-permute-start | bytes 454664 | tf_op jit(solution)/shard_map/ppermute | solution.py:28
  6.9 0.0 copy-done.4
  6.9 0.0 copy-done.1
  7.0 0.0 copy-done.2
  7.0 0.0 copy-done
  7.0 0.0 copy-done.3
  7.0 3.9 %shard_map.96 = (f32[36,16,1024]{2,1,0:T(8,128)S(1)}, f32[34,16,1024]{2,1,0:T(8,128)S(1)}, f32[32,1,1024]{2,1,0:T(1,128)S(1)}, f32[32,16,1024]{2,1,0:T(8,128)S(1...) custom-call(f32[32]{0:T(128)S(1)} %convert_element_type.3.effects, ...), custom_call_target="tpu_custom_call" | custom-call | flops 20971520 | bytes 6291456 | tf_op jit(solution)/shard_map/pallas_call | solution.py:445
  10.9 0.0 collective-permute-done.got_second.old_second
  10.9 0.0 collective-permute-done.1.got_first.old_first
  10.9 0.4 %shard_map.97 = (f32[38,1,1024]{2,1,0:T(1,128)S(1)}, f32[36,16,1024]{2,1,0:T(8,128)S(1)}, f32[34,16,1024]{2,1,0:T(8,128)S(1)}, f32[32,16,1024]{2,1,0:T(8,128)S(1...) custom-call(f32[37,1024]{1,0:T(8,128)S(1)} %collective-permute-done., ...), custom_call_target="tpu_custom_call", output_to_operand_aliasing={{0}: (4, {}), {1}: (5, {}), {2}: (6, {}), {3}: (7, {}), {4}... | custom-call | flops 5242880 | bytes 524288 | tf_op jit(solution)/shard_map/pallas_call | solution.py:445
  11.3 0.7 %collective-permute-start.2 = (f32[66,1024]{1,0:T(8,128)S(1)}, f32[66,1024]{1,0:T(8,128)S(1)}, u32[]{:S(2)}, u32[]{:S(2)}) collective-permute-start(f32[66,1024]{1,0:T(8,128)S(1)} %get-tuple-element.53), channel_id=1, source_target_pairs={{1,2},{2,1},{3,4},{4,3},{5,6},{6,5},{7,8},{8,7},{9,10},{10,9},{11,... | collective-permute-start | bytes 811016 | tf_op jit(solution)/shard_map/ppermute | solution.py:27
  12.0 3.8 %collective-permute-start.3 = (f32[66,1024]{1,0:T(8,128)S(1)}, f32[66,1024]{1,0:T(8,128)S(1)}, u32[]{:S(2)}, u32[]{:S(2)}) collective-permute-start(f32[66,1024]{1,0:T(8,128)S(1)} %get-tuple-element.54), channel_id=1, source_target_pairs={{0,1},{1,0},{2,3},{3,2},{4,5},{5,4},{6,7},{7,6},{8,9},{9,8},{10,11... | collective-permute-start | bytes 811016 | tf_op jit(solution)/shard_map/ppermute | solution.py:28
  15.8 7.0 %shard_map.98 = (f32[32,16,1024]{2,1,0:T(8,128)S(1)}, f32[36,16,1024]{2,1,0:T(8,128)S(1)}, f32[36,16,1024]{2,1,0:T(8,128)S(1)}, f32[40,16,1024]{2,1,0:T(8,128)S(...) custom-call(f32[38,1,1024]{2,1,0:T(1,128)S(1)} %get-tuple-element.55, ...), custom_call_target="tpu_custom_call", output_to_operand_aliasing={{0}: (6, {}), {1}: (7, {}), {2}: (8, {}), {3}: (9, {})} | custom-call | flops 62914560 | bytes 6291456 | tf_op jit(solution)/shard_map/pallas_call | solution.py:445
  22.8 0.0 collective-permute-done.2.got_second
  22.8 0.0 collective-permute-done.3.got_first
  22.8 1.1 %shard_map.99 = (f32[36,16,1024]{2,1,0:T(8,128)S(1)}, f32[36,16,1024]{2,1,0:T(8,128)S(1)}, f32[40,16,1024]{2,1,0:T(8,128)S(1)}, f32[38,16,1024]{2,1,0:T(8,128)S(...) custom-call(f32[37,1024]{1,0:T(8,128)S(1)} %collective-permute-done., ...), custom_call_target="tpu_custom_call", output_to_operand_aliasing={{0}: (8, {}), {1}: (9, {}), {2}: (10, {}), {3}: (11, {}), {... | custom-call | flops 10485760 | bytes 524288 | tf_op jit(solution)/shard_map/pallas_call | solution.py:445
  23.9 0.1 collective-permute-start.4
  24.0 1.1 %collective-permute-done.4 = f32[8,128]{1,0:T(8,128)S(1)} collective-permute-done((f32[8,128]{1,0:T(8,128)S(1)}, f32[8,128]{1,0:T(8,128)S(1)}, u32[]{:S(2)}, u32[]{:S(2)}) %collective-permute-start.4) | collective-permute-done | bytes 4128 | tf_op jit(solution)/shard_map/ppermute | solution.py:38
  25.1 2.0 %collective-permute-start.5 = (f32[8,128]{1,0:T(8,128)S(1)}, f32[8,128]{1,0:T(8,128)S(1)}, u32[]{:S(2)}, u32[]{:S(2)}) collective-permute-start(f32[8,128]{1,0:T(8,128)S(1)} %add.12.gate), channel_id=1, source_target_pairs={{0,2},{1,3},{2,0},{3,1},{4,6},{5,7},{6,4},{7,5},{8,10},{9,11},{10,... | collective-permute-start | bytes 12296 | tf_op jit(solution)/shard_map/ppermute | solution.py:38
  27.2 0.7 %shard_map.100.rim = f32[8,16,1024]{2,1,0:T(8,128)S(1)} custom-call(f32[8,128]{1,0:T(8,128)S(1)} %add.12.gate, f32[38,1,1024]{2,1,0:T(1,128)S(1)} %get-tuple-element.55.kappa, f32[36,16,1024]{2,1,0:T(8,128)S(1)} %get-tuple-element.73.weight, f32[36,16,1024]{2,1,0:T(8,128)S(1)} %get-tuple-element.74.inv, f32[40,16,1024]{2,1,0:T(8,128)S(1)} %get-tuple-element.75.search, ...), custom_call_target="tpu_custom_call" | custom-call | flops 2097152 | bytes 524288 | tf_op jit(solution)/shard_map/pallas_call | solution.py:445
  27.8 0.9 %collective-permute-done.5 = f32[8,128]{1,0:T(8,128)S(1)} collective-permute-done((f32[8,128]{1,0:T(8,128)S(1)}, f32[8,128]{1,0:T(8,128)S(1)}, u32[]{:S(2)}, u32[]{:S(2)}) %collective-permute-start.5) | collective-permute-done | bytes 4128 | tf_op jit(solution)/shard_map/ppermute | solution.py:38
  28.7 1.6 %collective-permute-start.6 = (f32[8,128]{1,0:T(8,128)S(1)}, f32[8,128]{1,0:T(8,128)S(1)}, u32[]{:S(2)}, u32[]{:S(2)}) collective-permute-start(f32[8,128]{1,0:T(8,128)S(1)} %add.13.gate), channel_id=1, source_target_pairs={{0,4},{1,5},{2,6},{3,7},{4,0},{5,1},{6,2},{7,3},{8,12},{9,13},{10,... | collective-permute-start | bytes 12296 | tf_op jit(solution)/shard_map/ppermute | solution.py:38
  30.4 0.7 %shard_map.101.upper = f32[12,16,1024]{2,1,0:T(8,128)S(1)} custom-call(f32[8,128]{1,0:T(8,128)S(1)} %add.13.gate, f32[38,1,1024]{2,1,0:T(1,128)S(1)} %get-tuple-element.55.kappa, f32[36,16,1024]{2,1,0:T(8,128)S(1)} %get-tuple-element.73.weight, f32[36,16,1024]{2,1,0:T(8,128)S(1)} %get-tuple-element.77.second, f32[34,16,1024]{2,1,0:T(8,128)S(1)} %get-tuple-element.78.second_image), custom_call_target="tpu_custom_call" | custom-call | flops 2097152 | bytes 524288 | tf_op jit(solution)/shard_map/pallas_call | solution.py:445
  31.0 1.3 %collective-permute-done.6 = f32[8,128]{1,0:T(8,128)S(1)} collective-permute-done((f32[8,128]{1,0:T(8,128)S(1)}, f32[8,128]{1,0:T(8,128)S(1)}, u32[]{:S(2)}, u32[]{:S(2)}) %collective-permute-start.6) | collective-permute-done | bytes 4128 | tf_op jit(solution)/shard_map/ppermute | solution.py:38
  32.4 2.7 %collective-permute-start.7 = (f32[8,128]{1,0:T(8,128)S(1)}, f32[8,128]{1,0:T(8,128)S(1)}, u32[]{:S(2)}, u32[]{:S(2)}) collective-permute-start(f32[8,128]{1,0:T(8,128)S(1)} %add.14.gate), channel_id=1, source_target_pairs={{0,8},{1,9},{2,10},{3,11},{4,12},{5,13},{6,14},{7,15},{8,0},{9,1},... | collective-permute-start | bytes 12296 | tf_op jit(solution)/shard_map/ppermute | solution.py:38
  35.0 0.7 %shard_map.102.lower = f32[12,16,1024]{2,1,0:T(8,128)S(1)} custom-call(f32[8,128]{1,0:T(8,128)S(1)} %add.14.gate, f32[38,1,1024]{2,1,0:T(1,128)S(1)} %get-tuple-element.55.kappa, f32[36,16,1024]{2,1,0:T(8,128)S(1)} %get-tuple-element.73.weight, f32[36,16,1024]{2,1,0:T(8,128)S(1)} %get-tuple-element.77.second, f32[34,16,1024]{2,1,0:T(8,128)S(1)} %get-tuple-element.78.second_image), custom_call_target="tpu_custom_call" | custom-call | flops 2097152 | bytes 524288 | tf_op jit(solution)/shard_map/pallas_call | solution.py:445
  35.7 1.2 %collective-permute-done.7 = f32[8,128]{1,0:T(8,128)S(1)} collective-permute-done((f32[8,128]{1,0:T(8,128)S(1)}, f32[8,128]{1,0:T(8,128)S(1)}, u32[]{:S(2)}, u32[]{:S(2)}) %collective-permute-start.7) | collective-permute-done | bytes 4128 | tf_op jit(solution)/shard_map/ppermute | solution.py:38
  36.9 2.6 %shard_map.103 = (f32[16,32,1024]{2,1,0:T(8,128)}, f32[16,32,1024]{2,1,0:T(8,128)}) custom-call(f32[8,128]{1,0:T(8,128)S(1)} %add.15.sums, f32[32,16,1024]{2,1,0:T(8,128)S(1)} %get-tuple-element.63.grad, f32[40,16,1024]{2,1,0:T(8,128)S(1)} %get-tuple-element.75.search, f32[32,16,1024]{2,1,0:T(8,128)S(1)} %get-tuple-element.82.image, ...), custom_call_target="tpu_custom_call" | custom-call | flops 4194304 | bytes 4194304 | tf_op jit(solution)/shard_map/pallas_call | solution.py:445
  (5 shorter events, 0.0 us)
Async XLA Ops:
  0.6 6.3 %copy-start.1 = (f32[32,1024]{1,0:T(8,128)S(1)}, f32[32,1024]{1,0:T(8,128)}, u32[]{:S(2)}) copy-start(f32[32,1024]{1,0:T(8,128)} %kappa_flat.1) | copy-start | bytes 393220
  0.6 6.3 %copy-start.2 = (s32[32,1024]{1,0:T(8,128)S(1)}, s32[32,1024]{1,0:T(8,128)}, u32[]{:S(2)}) copy-start(s32[32,1024]{1,0:T(8,128)} %land_flat.1) | copy-start | bytes 393220
  0.7 6.3 %copy-start = (f32[16,32,1024]{2,1,0:T(8,128)S(1)}, f32[16,32,1024]{2,1,0:T(8,128)}, u32[]{:S(2)}) copy-start(f32[16,32,1024]{2,1,0:T(8,128)} %latent.3) | copy-start | bytes 6291460
  0.7 6.3 %copy-start.4 = (bf16[32]{0:T(256)(128)(2,1)S(1)}, bf16[32]{0:T(256)(128)(2,1)}, u32[]{:S(2)}) copy-start(bf16[32]{0:T(256)(128)(2,1)} %param.14) | copy-start | bytes 196
  0.7 6.3 %copy-start.3 = (f32[8]{0:T(128)S(1)}, f32[8]{0:T(128)}, u32[]{:S(2)}) copy-start(f32[8]{0:T(128)} %intercepts.1) | copy-start | bytes 100
  1.9 9.0 %collective-permute-start = (f32[37,1024]{1,0:T(8,128)S(1)}, f32[37,1024]{1,0:T(8,128)S(1)}, u32[]{:S(2)}, u32[]{:S(2)}) collective-permute-start(f32[37,1024]{1,0:T(8,128)S(1)} %get-tuple-element.44), channel_id=1, source_target_pairs={{1,2},{2,1},{3,4},{4,3},{5,6},{6,5},{7,8},{8,7},{9,10},{10,9},{11,... | collective-permute-start | bytes 454664 | tf_op jit(solution)/shard_map/ppermute | solution.py:27
  2.6 8.3 %collective-permute-start.1 = (f32[37,1024]{1,0:T(8,128)S(1)}, f32[37,1024]{1,0:T(8,128)S(1)}, u32[]{:S(2)}, u32[]{:S(2)}) collective-permute-start(f32[37,1024]{1,0:T(8,128)S(1)} %get-tuple-element.45), channel_id=1, source_target_pairs={{0,1},{1,0},{2,3},{3,2},{4,5},{5,4},{6,7},{7,6},{8,9},{9,8},{10,11... | collective-permute-start | bytes 454664 | tf_op jit(solution)/shard_map/ppermute | solution.py:28
  11.3 11.5 %collective-permute-start.2 = (f32[66,1024]{1,0:T(8,128)S(1)}, f32[66,1024]{1,0:T(8,128)S(1)}, u32[]{:S(2)}, u32[]{:S(2)}) collective-permute-start(f32[66,1024]{1,0:T(8,128)S(1)} %get-tuple-element.53), channel_id=1, source_target_pairs={{1,2},{2,1},{3,4},{4,3},{5,6},{6,5},{7,8},{8,7},{9,10},{10,9},{11,... | collective-permute-start | bytes 811016 | tf_op jit(solution)/shard_map/ppermute | solution.py:27
  12.0 10.8 %collective-permute-start.3 = (f32[66,1024]{1,0:T(8,128)S(1)}, f32[66,1024]{1,0:T(8,128)S(1)}, u32[]{:S(2)}, u32[]{:S(2)}) collective-permute-start(f32[66,1024]{1,0:T(8,128)S(1)} %get-tuple-element.54), channel_id=1, source_target_pairs={{0,1},{1,0},{2,3},{3,2},{4,5},{5,4},{6,7},{7,6},{8,9},{9,8},{10,11... | collective-permute-start | bytes 811016 | tf_op jit(solution)/shard_map/ppermute | solution.py:28
  23.9 1.2 %collective-permute-start.4 = (f32[8,128]{1,0:T(8,128)S(1)}, f32[8,128]{1,0:T(8,128)S(1)}, u32[]{:S(2)}, u32[]{:S(2)}) collective-permute-start(f32[8,128]{1,0:T(8,128)S(1)} %get-tuple-element.72), channel_id=1, source_target_pairs={{0,1},{1,0},{2,3},{3,2},{4,5},{5,4},{6,7},{7,6},{8,9},{9,8},{10,11... | collective-permute-start | bytes 12296 | tf_op jit(solution)/shard_map/ppermute | solution.py:38
  25.1 3.6 %collective-permute-start.5 = (f32[8,128]{1,0:T(8,128)S(1)}, f32[8,128]{1,0:T(8,128)S(1)}, u32[]{:S(2)}, u32[]{:S(2)}) collective-permute-start(f32[8,128]{1,0:T(8,128)S(1)} %add.12.gate), channel_id=1, source_target_pairs={{0,2},{1,3},{2,0},{3,1},{4,6},{5,7},{6,4},{7,5},{8,10},{9,11},{10,... | collective-permute-start | bytes 12296 | tf_op jit(solution)/shard_map/ppermute | solution.py:38
  28.7 3.6 %collective-permute-start.6 = (f32[8,128]{1,0:T(8,128)S(1)}, f32[8,128]{1,0:T(8,128)S(1)}, u32[]{:S(2)}, u32[]{:S(2)}) collective-permute-start(f32[8,128]{1,0:T(8,128)S(1)} %add.13.gate), channel_id=1, source_target_pairs={{0,4},{1,5},{2,6},{3,7},{4,0},{5,1},{6,2},{7,3},{8,12},{9,13},{10,... | collective-permute-start | bytes 12296 | tf_op jit(solution)/shard_map/ppermute | solution.py:38
  32.4 4.5 %collective-permute-start.7 = (f32[8,128]{1,0:T(8,128)S(1)}, f32[8,128]{1,0:T(8,128)S(1)}, u32[]{:S(2)}, u32[]{:S(2)}) collective-permute-start(f32[8,128]{1,0:T(8,128)S(1)} %add.14.gate), channel_id=1, source_target_pairs={{0,8},{1,9},{2,10},{3,11},{4,12},{5,13},{6,14},{7,15},{8,0},{9,1},... | collective-permute-start | bytes 12296 | tf_op jit(solution)/shard_map/ppermute | solution.py:38

commit v8 on v7

--- a/solution.py
+++ b/solution.py
@@ -33,15 +33,21 @@
     results = []
     if count & (count - 1):
         return lax.psum(values, AX), [work(values) for work in works]
-    step = 1
+    rounds = [(1,)] if count > 1 else []
+    step = 2
     while step < count:
-        got = lax.ppermute(values, AX, [(i, i ^ step) for i in range(count)])
-        if step > 1 and len(results) < len(works):
+        wide = 2 * step < count
+        rounds.append((step, 2 * step, 3 * step) if wide else (step,))
+        step *= 4 if wide else 2
+    for number, partners in enumerate(rounds):
+        got = [lax.ppermute(values, AX, [(i, i ^ k) for i in range(count)]) for k in partners]
+        if number > 0 and len(results) < len(works):
             piece = works[len(results)](values)
             got, piece = lax.optimization_barrier((got, piece))
             results.append(piece)
-        values = values + got
-        step *= 2
+        values = values + got[0]
+        if len(got) > 1:
+            values = values + (got[1] + got[2])
     while len(results) < len(works):
         results.append(works[len(results)](values))
     return values, results
@@ -407,7 +413,7 @@
     row_loop(1, count, apply, most=8)
 
 
-def final_kernel(sums, grad, search, image, second, rim, upper, lower, newton_out, residual_out, newton, residual, newton_sem, residual_sem):
+def final_kernel(sums, grad, search, image, second, rim, lower, newton_out, residual_out, newton, residual, newton_sem, residual_sem):
     rows, weeks, cols = grad.shape
     rz, pq, cross, total = (jnp.sum(sums[k : k + 1, :], axis=1, keepdims=True) for k in range(4))
     first, cross, total = rz / pq, cross / pq, total / pq
@@ -422,7 +428,6 @@
         )
 
     one = rim.shape[0] - 1
-    two = one + upper.shape[0]
 
     def combine(r, last, at):
         put_row(newton, r, [along * p - across * y for p, y in zip(row_of(search, r + 4), row_of(second, r + 2))])
@@ -431,9 +436,8 @@
         for copy in copies(r):
             copy.start()
 
-    row_loop(0, one, lambda r, _: combine(r, rim, 0), most=7)
-    row_loop(one, two, lambda r, _: combine(r, upper, one), most=7)
-    row_loop(two, rows - 1, lambda r, _: combine(r, lower, two), most=7)
+    row_loop(0, one, lambda r, _: combine(r, rim, 0), most=8)
+    row_loop(one, rows - 1, lambda r, _: combine(r, lower, one), most=8)
     combine(rows - 1, rim, rows - 1 - one)
     for r in range(rows):
         for copy in copies(r):
@@ -510,8 +514,7 @@
         aliases={8 + k: k for k in range(7)},
         flops=20 * cells, moved=cells,
     )
-    one = 1 + (rows - 2) // 5
-    two = one + (rows - 1 - one) // 2
+    one = rows // 2 - 1
 
     def rim_rows(gate):
         return call(
@@ -530,12 +533,12 @@
             flops=4 * cells, moved=cells,
         )[0]
 
-    sums, (rim, upper, lower) = all_sum(sums, [rim_rows, last_rows(one, two - one), last_rows(two, rows - 1 - two)])
+    sums, (rim, lower) = all_sum(sums, [rim_rows, last_rows(one, rows - 1 - one)])
     return call(
         final_kernel,
         [(latent.shape, ANY), (latent.shape, ANY)],
         [(sums, VMEM), (grad, VMEM), (search, VMEM), (image, VMEM), (second, VMEM),
-         (rim, VMEM), (upper, VMEM), (lower, VMEM)],
+         (rim, VMEM), (lower, VMEM)],
         scratch=[pltpu.VMEM((rows, weeks, cols), F32), pltpu.VMEM((rows, weeks, cols), F32), DMA((rows,)), DMA((rows,))],
         flops=8 * cells, moved=8 * cells, limit=6,
     )

time: 39.7 us -> 39.6 us (level)
    ppermute x4 -> x5, starting transfers between devices: 6.4 us -> 6.28 us  [all_sum(): lax.ppermute(values, AX, [(i, i ^ k) for i in range(count)])]
    ppermute x4 -> x5, waiting for transfers between devices: 4.56 us -> 4.55 us  [all_sum(): lax.ppermute(values, AX, [(i, i ^ k) for i in range(count)])]
    pallas_call x9 -> x8, Pallas kernels: 18.2 us -> 18.2 us  [call(): pl.pallas_call(kernel, out_shape=shapes, in_specs=[pl.BlockSpec(memory_sp...]
  transfers between devices with their start and end apart: 8 -> 9, of which waited for: 4 -> 4; matrix products, arithmetic and copies ran while one was open for 0% -> 0% of each run, Pallas kernels for 33% -> 33%
where the time goes in v8:
time: 39.6 us; the launch traced here: 39.4 us
  Pallas kernels  18.2 us (46%)
  starting transfers between devices  15.7 us (40%)
  waiting for transfers between devices  4.57 us (12%)
  between operations  0.8 us (2%)
    pallas_call x8, Pallas kernels, call(): pl.pallas_call(kernel, out_shape=shapes, in_specs=[pl.BlockSpec(memory_sp...  18.2 us
    ppermute x2, starting transfers between devices, swap_rows(): return (lax.ppermute(near, AX, swap), far)  8.12 us
    ppermute x5, starting transfers between devices, all_sum(): lax.ppermute(values, AX, [(i, i ^ k) for i in range(count)])  6.28 us
    ppermute x5, waiting for transfers between devices, all_sum(): lax.ppermute(values, AX, [(i, i ^ k) for i in range(count)])  4.55 us
    ppermute x2, starting transfers between devices, swap_rows(): far = lax.ppermute(far, AX, cross)  1.35 us
  transfers between devices with their start and end apart: 9, of which 4 were waited for; matrix products, arithmetic and copies ran while one was open for 0% of the time, Pallas kernels for 33%

profile of v8, /device:TPU:0, one launch (start us, length us, event | category | flops | bytes accessed | tf_op | source)
XLA Modules:
  0.0 39.4 jit_solution(4655973931767566839)
XLA Ops:
  0.6 0.0 copy-start.1
  0.6 0.0 copy-start.2
  0.7 0.0 copy-start
  0.7 0.0 copy-start.4
  0.7 0.0 copy-start.3
  0.7 1.2 %shard_map.95 = (f32[37,1024]{1,0:T(8,128)S(1)}, f32[37,1024]{1,0:T(8,128)S(1)}) custom-call(f32[16,32,1024]{2,1,0:T(8,128)} %latent.3, f32[32,1024]{1,0:T(8,128)} %kappa_flat.1, s32[32,1024]{1,0:T(8,128)} %land_flat.1), custom_call_target="tpu_custom_call" | custom-call | flops 32768 | bytes 524288 | tf_op jit(solution)/shard_map/pallas_call | solution.py:449
  1.9 0.7 %collective-permute-start = (f32[37,1024]{1,0:T(8,128)S(1)}, f32[37,1024]{1,0:T(8,128)S(1)}, u32[]{:S(2)}, u32[]{:S(2)}) collective-permute-start(f32[37,1024]{1,0:T(8,128)S(1)} %get-tuple-element.44), channel_id=1, source_target_pairs={{1,2},{2,1},{3,4},{4,3},{5,6},{6,5},{7,8},{8,7},{9,10},{10,9},{11,... | collective-permute-start | bytes 454664 | tf_op jit(solution)/shard_map/ppermute | solution.py:27
  2.6 4.4 %collective-permute-start.1 = (f32[37,1024]{1,0:T(8,128)S(1)}, f32[37,1024]{1,0:T(8,128)S(1)}, u32[]{:S(2)}, u32[]{:S(2)}) collective-permute-start(f32[37,1024]{1,0:T(8,128)S(1)} %get-tuple-element.45), channel_id=1, source_target_pairs={{0,1},{1,0},{2,3},{3,2},{4,5},{5,4},{6,7},{7,6},{8,9},{9,8},{10,11... | collective-permute-start | bytes 454664 | tf_op jit(solution)/shard_map/ppermute | solution.py:28
  6.9 0.0 copy-done.4
  6.9 0.0 copy-done.1
  7.0 0.0 copy-done.2
  7.0 0.0 copy-done
  7.0 0.0 copy-done.3
  7.0 3.9 %shard_map.96 = (f32[36,16,1024]{2,1,0:T(8,128)S(1)}, f32[34,16,1024]{2,1,0:T(8,128)S(1)}, f32[32,1,1024]{2,1,0:T(1,128)S(1)}, f32[32,16,1024]{2,1,0:T(8,128)S(1...) custom-call(f32[32]{0:T(128)S(1)} %convert_element_type.3.effects, ...), custom_call_target="tpu_custom_call" | custom-call | flops 20971520 | bytes 6291456 | tf_op jit(solution)/shard_map/pallas_call | solution.py:449
  10.9 0.0 collective-permute-done.got_second.old_second
  10.9 0.0 collective-permute-done.1.got_first.old_first
  10.9 0.4 %shard_map.97 = (f32[38,1,1024]{2,1,0:T(1,128)S(1)}, f32[36,16,1024]{2,1,0:T(8,128)S(1)}, f32[34,16,1024]{2,1,0:T(8,128)S(1)}, f32[32,16,1024]{2,1,0:T(8,128)S(1...) custom-call(f32[37,1024]{1,0:T(8,128)S(1)} %collective-permute-done., ...), custom_call_target="tpu_custom_call", output_to_operand_aliasing={{0}: (4, {}), {1}: (5, {}), {2}: (6, {}), {3}: (7, {}), {4}... | custom-call | flops 5242880 | bytes 524288 | tf_op jit(solution)/shard_map/pallas_call | solution.py:449
  11.3 0.7 %collective-permute-start.2 = (f32[66,1024]{1,0:T(8,128)S(1)}, f32[66,1024]{1,0:T(8,128)S(1)}, u32[]{:S(2)}, u32[]{:S(2)}) collective-permute-start(f32[66,1024]{1,0:T(8,128)S(1)} %get-tuple-element.53), channel_id=1, source_target_pairs={{1,2},{2,1},{3,4},{4,3},{5,6},{6,5},{7,8},{8,7},{9,10},{10,9},{11,... | collective-permute-start | bytes 811016 | tf_op jit(solution)/shard_map/ppermute | solution.py:27
  12.0 3.8 %collective-permute-start.3 = (f32[66,1024]{1,0:T(8,128)S(1)}, f32[66,1024]{1,0:T(8,128)S(1)}, u32[]{:S(2)}, u32[]{:S(2)}) collective-permute-start(f32[66,1024]{1,0:T(8,128)S(1)} %get-tuple-element.54), channel_id=1, source_target_pairs={{0,1},{1,0},{2,3},{3,2},{4,5},{5,4},{6,7},{7,6},{8,9},{9,8},{10,11... | collective-permute-start | bytes 811016 | tf_op jit(solution)/shard_map/ppermute | solution.py:28
  15.8 7.0 %shard_map.98 = (f32[32,16,1024]{2,1,0:T(8,128)S(1)}, f32[36,16,1024]{2,1,0:T(8,128)S(1)}, f32[36,16,1024]{2,1,0:T(8,128)S(1)}, f32[40,16,1024]{2,1,0:T(8,128)S(...) custom-call(f32[38,1,1024]{2,1,0:T(1,128)S(1)} %get-tuple-element.55, ...), custom_call_target="tpu_custom_call", output_to_operand_aliasing={{0}: (6, {}), {1}: (7, {}), {2}: (8, {}), {3}: (9, {})} | custom-call | flops 62914560 | bytes 6291456 | tf_op jit(solution)/shard_map/pallas_call | solution.py:449
  22.8 0.0 collective-permute-done.2.got_second
  22.8 0.0 collective-permute-done.3.got_first
  22.8 1.1 %shard_map.99 = (f32[36,16,1024]{2,1,0:T(8,128)S(1)}, f32[36,16,1024]{2,1,0:T(8,128)S(1)}, f32[40,16,1024]{2,1,0:T(8,128)S(1)}, f32[38,16,1024]{2,1,0:T(8,128)S(...) custom-call(f32[37,1024]{1,0:T(8,128)S(1)} %collective-permute-done., ...), custom_call_target="tpu_custom_call", output_to_operand_aliasing={{0}: (8, {}), {1}: (9, {}), {2}: (10, {}), {3}: (11, {}), {... | custom-call | flops 10485760 | bytes 524288 | tf_op jit(solution)/shard_map/pallas_call | solution.py:449
  23.9 0.1 collective-permute-start.4
  24.0 1.1 %collective-permute-done.4 = f32[8,128]{1,0:T(8,128)S(1)} collective-permute-done((f32[8,128]{1,0:T(8,128)S(1)}, f32[8,128]{1,0:T(8,128)S(1)}, u32[]{:S(2)}, u32[]{:S(2)}) %collective-permute-start.4) | collective-permute-done | bytes 4128 | tf_op jit(solution)/shard_map/ppermute | solution.py:43
  25.1 3.0 %collective-permute-start.7 = (f32[8,128]{1,0:T(8,128)S(1)}, f32[8,128]{1,0:T(8,128)S(1)}, u32[]{:S(2)}, u32[]{:S(2)}) collective-permute-start(f32[8,128]{1,0:T(8,128)S(1)} %add.15.gate), channel_id=1, source_target_pairs={{0,6},{1,7},{2,4},{3,5},{4,2},{5,3},{6,0},{7,1},{8,14},{9,15},{10,... | collective-permute-start | bytes 12296 | tf_op jit(solution)/shard_map/ppermute | solution.py:43
  28.2 0.4 %collective-permute-start.6 = (f32[8,128]{1,0:T(8,128)S(1)}, f32[8,128]{1,0:T(8,128)S(1)}, u32[]{:S(2)}, u32[]{:S(2)}) collective-permute-start(f32[8,128]{1,0:T(8,128)S(1)} %add.15.gate), channel_id=1, source_target_pairs={{0,4},{1,5},{2,6},{3,7},{4,0},{5,1},{6,2},{7,3},{8,12},{9,13},{10,... | collective-permute-start | bytes 12296 | tf_op jit(solution)/shard_map/ppermute | solution.py:43
  28.6 0.1 collective-permute-start.5
  28.7 1.1 %shard_map.100.rim = f32[16,16,1024]{2,1,0:T(8,128)S(1)} custom-call(f32[8,128]{1,0:T(8,128)S(1)} %add.15.gate, f32[38,1,1024]{2,1,0:T(1,128)S(1)} %get-tuple-element.55.kappa, f32[36,16,1024]{2,1,0:T(8,128)S(1)} %get-tuple-element.73.weight, f32[36,16,1024]{2,1,0:T(8,128)S(1)} %get-tuple-element.74.inv, f32[40,16,1024]{2,1,0:T(8,128)S(1)} %get-tuple-element.75.search, ...), custom_call_target="tpu_custom_call" | custom-call | flops 2097152 | bytes 524288 | tf_op jit(solution)/shard_map/pallas_call | solution.py:449
  29.9 0.0 collective-permute-done.7
  29.9 1.9 %collective-permute-done.6 = f32[8,128]{1,0:T(8,128)S(1)} collective-permute-done((f32[8,128]{1,0:T(8,128)S(1)}, f32[8,128]{1,0:T(8,128)S(1)}, u32[]{:S(2)}, u32[]{:S(2)}) %collective-permute-start.6) | collective-permute-done | bytes 4128 | tf_op jit(solution)/shard_map/ppermute | solution.py:43
  31.8 0.4 %collective-permute-done.5 = f32[8,128]{1,0:T(8,128)S(1)} collective-permute-done((f32[8,128]{1,0:T(8,128)S(1)}, f32[8,128]{1,0:T(8,128)S(1)}, u32[]{:S(2)}, u32[]{:S(2)}) %collective-permute-start.5) | collective-permute-done | bytes 4128 | tf_op jit(solution)/shard_map/ppermute | solution.py:43
  32.2 2.6 %collective-permute-start.8 = (f32[8,128]{1,0:T(8,128)S(1)}, f32[8,128]{1,0:T(8,128)S(1)}, u32[]{:S(2)}, u32[]{:S(2)}) collective-permute-start(f32[8,128]{1,0:T(8,128)S(1)} %add_add_fusion.gate), channel_id=1, source_target_pairs={{0,8},{1,9},{2,10},{3,11},{4,12},{5,13},{6,14},{7,15},{8,0},{9,1},... | collective-permute-start | bytes 12296 | tf_op jit(solution)/shard_map/ppermute | solution.py:43
  34.8 0.8 %shard_map.101.lower = f32[16,16,1024]{2,1,0:T(8,128)S(1)} custom-call(f32[8,128]{1,0:T(8,128)S(1)} %add_add_fusion.gate, f32[38,1,1024]{2,1,0:T(1,128)S(1)} %get-tuple-element.55.kappa, f32[36,16,1024]{2,1,0:T(8,128)S(1)} %get-tuple-element.73.weight, f32[36,16,1024]{2,1,0:T(8,128)S(1)} %get-tuple-element.77.second, ...), custom_call_target="tpu_custom_call" | custom-call | flops 2097152 | bytes 524288 | tf_op jit(solution)/shard_map/pallas_call | solution.py:449
  35.7 1.1 %collective-permute-done.8 = f32[8,128]{1,0:T(8,128)S(1)} collective-permute-done((f32[8,128]{1,0:T(8,128)S(1)}, f32[8,128]{1,0:T(8,128)S(1)}, u32[]{:S(2)}, u32[]{:S(2)}) %collective-permute-start.8) | collective-permute-done | bytes 4128 | tf_op jit(solution)/shard_map/ppermute | solution.py:43
  36.7 2.6 %shard_map.102 = (f32[16,32,1024]{2,1,0:T(8,128)}, f32[16,32,1024]{2,1,0:T(8,128)}) custom-call(f32[8,128]{1,0:T(8,128)S(1)} %add.19.sums, f32[32,16,1024]{2,1,0:T(8,128)S(1)} %get-tuple-element.63.grad, f32[40,16,1024]{2,1,0:T(8,128)S(1)} %get-tuple-element.75.search, f32[32,16,1024]{2,1,0:T(8,128)S(1)} %get-tuple-element.83.image, ...), custom_call_target="tpu_custom_call" | custom-call | flops 4194304 | bytes 4194304 | tf_op jit(solution)/shard_map/pallas_call | solution.py:449
  (4 shorter events, 0.0 us)
Async XLA Ops:
  0.6 6.3 %copy-start.1 = (f32[32,1024]{1,0:T(8,128)S(1)}, f32[32,1024]{1,0:T(8,128)}, u32[]{:S(2)}) copy-start(f32[32,1024]{1,0:T(8,128)} %kappa_flat.1) | copy-start | bytes 393220
  0.6 6.3 %copy-start.2 = (s32[32,1024]{1,0:T(8,128)S(1)}, s32[32,1024]{1,0:T(8,128)}, u32[]{:S(2)}) copy-start(s32[32,1024]{1,0:T(8,128)} %land_flat.1) | copy-start | bytes 393220
  0.7 6.3 %copy-start = (f32[16,32,1024]{2,1,0:T(8,128)S(1)}, f32[16,32,1024]{2,1,0:T(8,128)}, u32[]{:S(2)}) copy-start(f32[16,32,1024]{2,1,0:T(8,128)} %latent.3) | copy-start | bytes 6291460
  0.7 6.3 %copy-start.4 = (bf16[32]{0:T(256)(128)(2,1)S(1)}, bf16[32]{0:T(256)(128)(2,1)}, u32[]{:S(2)}) copy-start(bf16[32]{0:T(256)(128)(2,1)} %param.14) | copy-start | bytes 196
  0.7 6.3 %copy-start.3 = (f32[8]{0:T(128)S(1)}, f32[8]{0:T(128)}, u32[]{:S(2)}) copy-start(f32[8]{0:T(128)} %intercepts.1) | copy-start | bytes 100
  1.9 9.0 %collective-permute-start = (f32[37,1024]{1,0:T(8,128)S(1)}, f32[37,1024]{1,0:T(8,128)S(1)}, u32[]{:S(2)}, u32[]{:S(2)}) collective-permute-start(f32[37,1024]{1,0:T(8,128)S(1)} %get-tuple-element.44), channel_id=1, source_target_pairs={{1,2},{2,1},{3,4},{4,3},{5,6},{6,5},{7,8},{8,7},{9,10},{10,9},{11,... | collective-permute-start | bytes 454664 | tf_op jit(solution)/shard_map/ppermute | solution.py:27
  2.6 8.3 %collective-permute-start.1 = (f32[37,1024]{1,0:T(8,128)S(1)}, f32[37,1024]{1,0:T(8,128)S(1)}, u32[]{:S(2)}, u32[]{:S(2)}) collective-permute-start(f32[37,1024]{1,0:T(8,128)S(1)} %get-tuple-element.45), channel_id=1, source_target_pairs={{0,1},{1,0},{2,3},{3,2},{4,5},{5,4},{6,7},{7,6},{8,9},{9,8},{10,11... | collective-permute-start | bytes 454664 | tf_op jit(solution)/shard_map/ppermute | solution.py:28
  11.3 11.5 %collective-permute-start.2 = (f32[66,1024]{1,0:T(8,128)S(1)}, f32[66,1024]{1,0:T(8,128)S(1)}, u32[]{:S(2)}, u32[]{:S(2)}) collective-permute-start(f32[66,1024]{1,0:T(8,128)S(1)} %get-tuple-element.53), channel_id=1, source_target_pairs={{1,2},{2,1},{3,4},{4,3},{5,6},{6,5},{7,8},{8,7},{9,10},{10,9},{11,... | collective-permute-start | bytes 811016 | tf_op jit(solution)/shard_map/ppermute | solution.py:27
  12.0 10.8 %collective-permute-start.3 = (f32[66,1024]{1,0:T(8,128)S(1)}, f32[66,1024]{1,0:T(8,128)S(1)}, u32[]{:S(2)}, u32[]{:S(2)}) collective-permute-start(f32[66,1024]{1,0:T(8,128)S(1)} %get-tuple-element.54), channel_id=1, source_target_pairs={{0,1},{1,0},{2,3},{3,2},{4,5},{5,4},{6,7},{7,6},{8,9},{9,8},{10,11... | collective-permute-start | bytes 811016 | tf_op jit(solution)/shard_map/ppermute | solution.py:28
  23.9 1.2 %collective-permute-start.4 = (f32[8,128]{1,0:T(8,128)S(1)}, f32[8,128]{1,0:T(8,128)S(1)}, u32[]{:S(2)}, u32[]{:S(2)}) collective-permute-start(f32[8,128]{1,0:T(8,128)S(1)} %get-tuple-element.72), channel_id=1, source_target_pairs={{0,1},{1,0},{2,3},{3,2},{4,5},{5,4},{6,7},{7,6},{8,9},{9,8},{10,11... | collective-permute-start | bytes 12296 | tf_op jit(solution)/shard_map/ppermute | solution.py:43
  25.1 4.7 %collective-permute-start.7 = (f32[8,128]{1,0:T(8,128)S(1)}, f32[8,128]{1,0:T(8,128)S(1)}, u32[]{:S(2)}, u32[]{:S(2)}) collective-permute-start(f32[8,128]{1,0:T(8,128)S(1)} %add.15.gate), channel_id=1, source_target_pairs={{0,6},{1,7},{2,4},{3,5},{4,2},{5,3},{6,0},{7,1},{8,14},{9,15},{10,... | collective-permute-start | bytes 12296 | tf_op jit(solution)/shard_map/ppermute | solution.py:43
  28.2 3.6 %collective-permute-start.6 = (f32[8,128]{1,0:T(8,128)S(1)}, f32[8,128]{1,0:T(8,128)S(1)}, u32[]{:S(2)}, u32[]{:S(2)}) collective-permute-start(f32[8,128]{1,0:T(8,128)S(1)} %add.15.gate), channel_id=1, source_target_pairs={{0,4},{1,5},{2,6},{3,7},{4,0},{5,1},{6,2},{7,3},{8,12},{9,13},{10,... | collective-permute-start | bytes 12296 | tf_op jit(solution)/shard_map/ppermute | solution.py:43
  28.6 3.6 %collective-permute-start.5 = (f32[8,128]{1,0:T(8,128)S(1)}, f32[8,128]{1,0:T(8,128)S(1)}, u32[]{:S(2)}, u32[]{:S(2)}) collective-permute-start(f32[8,128]{1,0:T(8,128)S(1)} %add.15.gate), channel_id=1, source_target_pairs={{0,2},{1,3},{2,0},{3,1},{4,6},{5,7},{6,4},{7,5},{8,10},{9,11},{10,... | collective-permute-start | bytes 12296 | tf_op jit(solution)/shard_map/ppermute | solution.py:43
  32.2 4.5 %collective-permute-start.8 = (f32[8,128]{1,0:T(8,128)S(1)}, f32[8,128]{1,0:T(8,128)S(1)}, u32[]{:S(2)}, u32[]{:S(2)}) collective-permute-start(f32[8,128]{1,0:T(8,128)S(1)} %add_add_fusion.gate), channel_id=1, source_target_pairs={{0,8},{1,9},{2,10},{3,11},{4,12},{5,13},{6,14},{7,15},{8,0},{9,1},... | collective-permute-start | bytes 12296 | tf_op jit(solution)/shard_map/ppermute | solution.py:43

commit v9 on v8

--- a/solution.py
+++ b/solution.py
@@ -277,6 +277,18 @@
             second[at + d : at + d + 1, part] = jnp.where(odd, bottom, top)
 
 
+def halo_weight(r, rows, field, kappa, old_first, old_second, got_first, got_second):
+    weeks = field.shape[1]
+    d = r + 2 if r < 0 else r - rows
+    eta_row = halo_line(r < 0, 4 * weeks + d, got_first, got_second)
+    land_row = halo_line(r < 0, 2 * weeks + 3 + d, old_first, old_second)
+    heavy = []
+    for j, tile in enumerate(row_of(field, r + 2)):
+        curve = jnp.tanh(0.5 * (tile + eta_row[j]))
+        heavy.append(land_row[j] * (1.0 - curve * curve))
+    return heavy, [1.0 / (diag_base(k) + h) for k, h in zip(map_row(kappa, r + 3), heavy)]
+
+
 def mass_row(r, source, at, weight, mask):
     mid = row_of(source, at)
     return mid, [time_coupling * temporal_tile(m, mask) + h * m for m, h in zip(mid, row_of(weight, r + 2))]
@@ -340,20 +352,12 @@
     weeks = grad.shape[1]
     rows = grad.shape[0]
     mask = masks(weeks)
-    for d in range(4):
-        put_row(search, d, halo_row(d - 4, rows, 4, weeks, got_first, got_second))
-        put_row(search, rows + 4 + d, halo_row(rows + d, rows, 4, weeks, got_first, got_second))
-    for above in (True, False):
-        for d in range(2):
-            r = d - 2 if above else rows + d
-            eta_row = halo_line(above, 4 * weeks + d, got_first, got_second)
-            land_row = halo_line(above, 2 * weeks + 3 + d, old_first, old_second)
-            heavy = []
-            for j, tile in enumerate(row_of(field, r + 2)):
-                curve = jnp.tanh(0.5 * (tile + eta_row[j]))
-                heavy.append(land_row[j] * (1.0 - curve * curve))
-            put_row(weight, r + 2, heavy)
-            put_row(inv, r + 2, [1.0 / (diag_base(k) + h) for k, h in zip(map_row(kappa, r + 3), heavy)])
+    for r in (-3, -2, -1, rows, rows + 1, rows + 2):
+        put_row(search, r + 4, halo_row(r, rows, 4, weeks, got_first, got_second))
+    for r in (-1, rows):
+        heavy, inverse = halo_weight(r, rows, field, kappa, old_first, old_second, got_first, got_second)
+        put_row(weight, r + 2, heavy)
+        put_row(inv, r + 2, inverse)
 
     for r in (-2, -1, 0, rows - 1, rows, rows + 1):
         put_row(first, r + 3, keep_inside(r, rows, laplace_row(
@@ -387,19 +391,22 @@
     row_loop(0, last.shape[0], apply, most=8)
 
 
-def rim_kernel(gate, kappa, weight, inv, search, first, second, second_image, last):
+def rim_kernel(gate, old_first, old_second, got_first, got_second, kappa, field, weight, search, first, second,
+               second_image, last):
     rows = second_image.shape[0] - 2
     count = last.shape[0] - 1
     mask = masks(last.shape[1])
     for r, away in ((0, -1), (rows - 1, 1)):
         rim = [r + away * d for d in range(5)]
         tiles = keep_inside(rim[3], rows, laplace_row(
-            row_of(search, rim[4] + 4), row_of(search, rim[3] + 4), row_of(search, rim[2] + 4),
+            halo_row(rim[4], rows, 4, last.shape[1], got_first, got_second),
+            row_of(search, rim[3] + 4), row_of(search, rim[2] + 4),
             map_row(kappa, rim[3] + 3), mask))
         outer = laplace_row(tiles, row_of(first, rim[2] + 3), row_of(first, rim[1] + 3), map_row(kappa, rim[2] + 3), mask)
-        mass = mass_row(rim[2], search, rim[2] + 4, weight, mask)[1]
+        heavy, inverse = halo_weight(rim[2], rows, field, kappa, old_first, old_second, got_first, got_second)
         tiles = keep_inside(rim[2], rows, [
-            (prior_scale * o + m) * d for o, m, d in zip(outer, mass, row_of(inv, rim[2] + 2))])
+            (prior_scale * o + (time_coupling * temporal_tile(m, mask) + h * m)) * d
+            for o, m, h, d in zip(outer, row_of(search, rim[2] + 4), heavy, inverse)])
         tiles = keep_inside(rim[1], rows, laplace_row(
             tiles, row_of(second, rim[1] + 2), row_of(second, r + 2), map_row(kappa, rim[1] + 3), mask))
         outer = laplace_row(
@@ -436,8 +443,8 @@
         for copy in copies(r):
             copy.start()
 
-    row_loop(0, one, lambda r, _: combine(r, rim, 0), most=8)
-    row_loop(one, rows - 1, lambda r, _: combine(r, lower, one), most=8)
+    row_loop(0, one, lambda r, _: combine(r, rim, 0), most=5)
+    row_loop(one, rows - 1, lambda r, _: combine(r, lower, one), most=5)
     combine(rows - 1, rim, rows - 1 - one)
     for r in range(rows):
         for copy in copies(r):
@@ -520,8 +527,8 @@
         return call(
             rim_kernel,
             [((one + 1, weeks, cols), VMEM)],
-            [(gate, VMEM), (kappa, VMEM), (weight, VMEM), (inv, VMEM), (search, VMEM), (first, VMEM), (second, VMEM),
-             (second_image, VMEM)],
+            [(gate, VMEM), (old_near, VMEM), (old_far, VMEM), (near, VMEM), (far, VMEM), (kappa, VMEM), (field, VMEM),
+             (weight, VMEM), (search, VMEM), (first, VMEM), (second, VMEM), (second_image, VMEM)],
             flops=4 * cells, moved=cells,
         )[0]
 

time: 39.6 us -> 39.5 us (level)
  no operation moved by 1% of the time
where the time goes in v9:
time: 39.5 us; the launch traced here: 39.3 us
  Pallas kernels  18.3 us (46%)
  starting transfers between devices  15.7 us (40%)
  waiting for transfers between devices  4.55 us (12%)
  between operations  0.8 us (2%)
    pallas_call x8, Pallas kernels, call(): pl.pallas_call(kernel, out_shape=shapes, in_specs=[pl.BlockSpec(memory_sp...  18.3 us
    ppermute x2, starting transfers between devices, swap_rows(): return (lax.ppermute(near, AX, swap), far)  8.11 us
    ppermute x5, starting transfers between devices, all_sum(): lax.ppermute(values, AX, [(i, i ^ k) for i in range(count)])  6.23 us
    ppermute x5, waiting for transfers between devices, all_sum(): lax.ppermute(values, AX, [(i, i ^ k) for i in range(count)])  4.54 us
    ppermute x2, starting transfers between devices, swap_rows(): far = lax.ppermute(far, AX, cross)  1.35 us
  transfers between devices with their start and end apart: 9, of which 4 were waited for; matrix products, arithmetic and copies ran while one was open for 0% of the time, Pallas kernels for 33%

profile of v9, /device:TPU:0, one launch (start us, length us, event | category | flops | bytes accessed | tf_op | source)
XLA Modules:
  0.0 39.3 jit_solution(6337356884637815959)
XLA Ops:
  0.6 0.0 copy-start.1
  0.6 0.0 copy-start.2
  0.7 0.0 copy-start
  0.7 0.0 copy-start.4
  0.7 0.0 copy-start.3
  0.7 1.2 %shard_map.95 = (f32[37,1024]{1,0:T(8,128)S(1)}, f32[37,1024]{1,0:T(8,128)S(1)}) custom-call(f32[16,32,1024]{2,1,0:T(8,128)} %latent.3, f32[32,1024]{1,0:T(8,128)} %kappa_flat.1, s32[32,1024]{1,0:T(8,128)} %land_flat.1), custom_call_target="tpu_custom_call" | custom-call | flops 32768 | bytes 524288 | tf_op jit(solution)/shard_map/pallas_call | solution.py:456
  1.9 0.7 %collective-permute-start = (f32[37,1024]{1,0:T(8,128)S(1)}, f32[37,1024]{1,0:T(8,128)S(1)}, u32[]{:S(2)}, u32[]{:S(2)}) collective-permute-start(f32[37,1024]{1,0:T(8,128)S(1)} %get-tuple-element.43), channel_id=1, source_target_pairs={{1,2},{2,1},{3,4},{4,3},{5,6},{6,5},{7,8},{8,7},{9,10},{10,9},{11,... | collective-permute-start | bytes 454664 | tf_op jit(solution)/shard_map/ppermute | solution.py:27
  2.6 4.4 %collective-permute-start.1 = (f32[37,1024]{1,0:T(8,128)S(1)}, f32[37,1024]{1,0:T(8,128)S(1)}, u32[]{:S(2)}, u32[]{:S(2)}) collective-permute-start(f32[37,1024]{1,0:T(8,128)S(1)} %get-tuple-element.44), channel_id=1, source_target_pairs={{0,1},{1,0},{2,3},{3,2},{4,5},{5,4},{6,7},{7,6},{8,9},{9,8},{10,11... | collective-permute-start | bytes 454664 | tf_op jit(solution)/shard_map/ppermute | solution.py:28
  6.9 0.0 copy-done.4
  6.9 0.0 copy-done.1
  7.0 0.0 copy-done.2
  7.0 0.0 copy-done
  7.0 0.0 copy-done.3
  7.0 3.9 %shard_map.96 = (f32[36,16,1024]{2,1,0:T(8,128)S(1)}, f32[34,16,1024]{2,1,0:T(8,128)S(1)}, f32[32,1,1024]{2,1,0:T(1,128)S(1)}, f32[32,16,1024]{2,1,0:T(8,128)S(1...) custom-call(f32[32]{0:T(128)S(1)} %convert_element_type.3.effects, ...), custom_call_target="tpu_custom_call" | custom-call | flops 20971520 | bytes 6291456 | tf_op jit(solution)/shard_map/pallas_call | solution.py:456
  10.9 0.0 collective-permute-done.got_second.old_second
  10.9 0.0 collective-permute-done.1.got_first.old_first
  10.9 0.4 %shard_map.97 = (f32[38,1,1024]{2,1,0:T(1,128)S(1)}, f32[36,16,1024]{2,1,0:T(8,128)S(1)}, f32[34,16,1024]{2,1,0:T(8,128)S(1)}, f32[32,16,1024]{2,1,0:T(8,128)S(1...) custom-call(f32[37,1024]{1,0:T(8,128)S(1)} %collective-permute-done., ...), custom_call_target="tpu_custom_call", output_to_operand_aliasing={{0}: (4, {}), {1}: (5, {}), {2}: (6, {}), {3}: (7, {}), {4}... | custom-call | flops 5242880 | bytes 524288 | tf_op jit(solution)/shard_map/pallas_call | solution.py:456
  11.3 0.7 %collective-permute-start.2 = (f32[66,1024]{1,0:T(8,128)S(1)}, f32[66,1024]{1,0:T(8,128)S(1)}, u32[]{:S(2)}, u32[]{:S(2)}) collective-permute-start(f32[66,1024]{1,0:T(8,128)S(1)} %get-tuple-element.52), channel_id=1, source_target_pairs={{1,2},{2,1},{3,4},{4,3},{5,6},{6,5},{7,8},{8,7},{9,10},{10,9},{11,... | collective-permute-start | bytes 811016 | tf_op jit(solution)/shard_map/ppermute | solution.py:27
  12.0 3.8 %collective-permute-start.3 = (f32[66,1024]{1,0:T(8,128)S(1)}, f32[66,1024]{1,0:T(8,128)S(1)}, u32[]{:S(2)}, u32[]{:S(2)}) collective-permute-start(f32[66,1024]{1,0:T(8,128)S(1)} %get-tuple-element.53), channel_id=1, source_target_pairs={{0,1},{1,0},{2,3},{3,2},{4,5},{5,4},{6,7},{7,6},{8,9},{9,8},{10,11... | collective-permute-start | bytes 811016 | tf_op jit(solution)/shard_map/ppermute | solution.py:28
  15.8 7.1 %shard_map.98 = (f32[32,16,1024]{2,1,0:T(8,128)S(1)}, f32[36,16,1024]{2,1,0:T(8,128)S(1)}, f32[36,16,1024]{2,1,0:T(8,128)S(1)}, f32[40,16,1024]{2,1,0:T(8,128)S(...) custom-call(f32[38,1,1024]{2,1,0:T(1,128)S(1)} %get-tuple-element.54, ...), custom_call_target="tpu_custom_call", output_to_operand_aliasing={{0}: (6, {}), {1}: (7, {}), {2}: (8, {}), {3}: (9, {})} | custom-call | flops 62914560 | bytes 6291456 | tf_op jit(solution)/shard_map/pallas_call | solution.py:456
  22.9 0.0 collective-permute-done.2.got_second
  22.9 0.0 collective-permute-done.3.got_first
  22.9 1.0 %shard_map.99 = (f32[36,16,1024]{2,1,0:T(8,128)S(1)}, f32[36,16,1024]{2,1,0:T(8,128)S(1)}, f32[40,16,1024]{2,1,0:T(8,128)S(1)}, f32[38,16,1024]{2,1,0:T(8,128)S(...) custom-call(f32[37,1024]{1,0:T(8,128)S(1)} %collective-permute-done., ...), custom_call_target="tpu_custom_call", output_to_operand_aliasing={{0}: (8, {}), {1}: (9, {}), {2}: (10, {}), {3}: (11, {}), {... | custom-call | flops 10485760 | bytes 524288 | tf_op jit(solution)/shard_map/pallas_call | solution.py:456
  23.9 0.1 collective-permute-start.4
  24.0 1.1 %collective-permute-done.4 = f32[8,128]{1,0:T(8,128)S(1)} collective-permute-done((f32[8,128]{1,0:T(8,128)S(1)}, f32[8,128]{1,0:T(8,128)S(1)}, u32[]{:S(2)}, u32[]{:S(2)}) %collective-permute-start.4) | collective-permute-done | bytes 4128 | tf_op jit(solution)/shard_map/ppermute | solution.py:43
  25.1 3.0 %collective-permute-start.7 = (f32[8,128]{1,0:T(8,128)S(1)}, f32[8,128]{1,0:T(8,128)S(1)}, u32[]{:S(2)}, u32[]{:S(2)}) collective-permute-start(f32[8,128]{1,0:T(8,128)S(1)} %add.15.gate), channel_id=1, source_target_pairs={{0,6},{1,7},{2,4},{3,5},{4,2},{5,3},{6,0},{7,1},{8,14},{9,15},{10,... | collective-permute-start | bytes 12296 | tf_op jit(solution)/shard_map/ppermute | solution.py:43
  28.1 0.4 %collective-permute-start.6 = (f32[8,128]{1,0:T(8,128)S(1)}, f32[8,128]{1,0:T(8,128)S(1)}, u32[]{:S(2)}, u32[]{:S(2)}) collective-permute-start(f32[8,128]{1,0:T(8,128)S(1)} %add.15.gate), channel_id=1, source_target_pairs={{0,4},{1,5},{2,6},{3,7},{4,0},{5,1},{6,2},{7,3},{8,12},{9,13},{10,... | collective-permute-start | bytes 12296 | tf_op jit(solution)/shard_map/ppermute | solution.py:43
  28.6 0.1 collective-permute-start.5
  28.7 1.1 %shard_map.100.rim = f32[16,16,1024]{2,1,0:T(8,128)S(1)} custom-call(f32[8,128]{1,0:T(8,128)S(1)} %add.15.gate, f32[37,1024]{1,0:T(8,128)S(1)} %collective-permute-done.1.got_first.old_first, f32[37,1024]{1,0:T(8,128)S(1)} %collective-permute-done.got_second.old_second, f32[66,1024]{1,0:T(8,128)S(1)} %collective-permute-done.3.got_first, ...), custom_call_target="tpu_custom_call" | custom-call | flops 2097152 | bytes 524288 | tf_op jit(solution)/shard_map/pallas_call | solution.py:456
  29.8 0.0 collective-permute-done.7
  29.8 1.9 %collective-permute-done.6 = f32[8,128]{1,0:T(8,128)S(1)} collective-permute-done((f32[8,128]{1,0:T(8,128)S(1)}, f32[8,128]{1,0:T(8,128)S(1)}, u32[]{:S(2)}, u32[]{:S(2)}) %collective-permute-start.6) | collective-permute-done | bytes 4128 | tf_op jit(solution)/shard_map/ppermute | solution.py:43
  31.7 0.4 %collective-permute-done.5 = f32[8,128]{1,0:T(8,128)S(1)} collective-permute-done((f32[8,128]{1,0:T(8,128)S(1)}, f32[8,128]{1,0:T(8,128)S(1)}, u32[]{:S(2)}, u32[]{:S(2)}) %collective-permute-start.5) | collective-permute-done | bytes 4128 | tf_op jit(solution)/shard_map/ppermute | solution.py:43
  32.2 2.6 %collective-permute-start.8 = (f32[8,128]{1,0:T(8,128)S(1)}, f32[8,128]{1,0:T(8,128)S(1)}, u32[]{:S(2)}, u32[]{:S(2)}) collective-permute-start(f32[8,128]{1,0:T(8,128)S(1)} %add_add_fusion.gate), channel_id=1, source_target_pairs={{0,8},{1,9},{2,10},{3,11},{4,12},{5,13},{6,14},{7,15},{8,0},{9,1},... | collective-permute-start | bytes 12296 | tf_op jit(solution)/shard_map/ppermute | solution.py:43
  34.8 0.8 %shard_map.101.lower = f32[16,16,1024]{2,1,0:T(8,128)S(1)} custom-call(f32[8,128]{1,0:T(8,128)S(1)} %add_add_fusion.gate, f32[38,1,1024]{2,1,0:T(1,128)S(1)} %get-tuple-element.54.kappa, f32[36,16,1024]{2,1,0:T(8,128)S(1)} %get-tuple-element.72.weight, f32[36,16,1024]{2,1,0:T(8,128)S(1)} %get-tuple-element.75.second, ...), custom_call_target="tpu_custom_call" | custom-call | flops 2097152 | bytes 524288 | tf_op jit(solution)/shard_map/pallas_call | solution.py:456
  35.6 1.1 %collective-permute-done.8 = f32[8,128]{1,0:T(8,128)S(1)} collective-permute-done((f32[8,128]{1,0:T(8,128)S(1)}, f32[8,128]{1,0:T(8,128)S(1)}, u32[]{:S(2)}, u32[]{:S(2)}) %collective-permute-start.8) | collective-permute-done | bytes 4128 | tf_op jit(solution)/shard_map/ppermute | solution.py:43
  36.7 2.6 %shard_map.102 = (f32[16,32,1024]{2,1,0:T(8,128)}, f32[16,32,1024]{2,1,0:T(8,128)}) custom-call(f32[8,128]{1,0:T(8,128)S(1)} %add.19.sums, f32[32,16,1024]{2,1,0:T(8,128)S(1)} %get-tuple-element.62.grad, f32[40,16,1024]{2,1,0:T(8,128)S(1)} %get-tuple-element.73.search, f32[32,16,1024]{2,1,0:T(8,128)S(1)} %get-tuple-element.81.image, ...), custom_call_target="tpu_custom_call" | custom-call | flops 4194304 | bytes 4194304 | tf_op jit(solution)/shard_map/pallas_call | solution.py:456
  (4 shorter events, 0.0 us)
Async XLA Ops:
  0.6 6.3 %copy-start.1 = (f32[32,1024]{1,0:T(8,128)S(1)}, f32[32,1024]{1,0:T(8,128)}, u32[]{:S(2)}) copy-start(f32[32,1024]{1,0:T(8,128)} %kappa_flat.1) | copy-start | bytes 393220
  0.6 6.3 %copy-start.2 = (s32[32,1024]{1,0:T(8,128)S(1)}, s32[32,1024]{1,0:T(8,128)}, u32[]{:S(2)}) copy-start(s32[32,1024]{1,0:T(8,128)} %land_flat.1) | copy-start | bytes 393220
  0.7 6.3 %copy-start = (f32[16,32,1024]{2,1,0:T(8,128)S(1)}, f32[16,32,1024]{2,1,0:T(8,128)}, u32[]{:S(2)}) copy-start(f32[16,32,1024]{2,1,0:T(8,128)} %latent.3) | copy-start | bytes 6291460
  0.7 6.3 %copy-start.4 = (bf16[32]{0:T(256)(128)(2,1)S(1)}, bf16[32]{0:T(256)(128)(2,1)}, u32[]{:S(2)}) copy-start(bf16[32]{0:T(256)(128)(2,1)} %param.14) | copy-start | bytes 196
  0.7 6.3 %copy-start.3 = (f32[8]{0:T(128)S(1)}, f32[8]{0:T(128)}, u32[]{:S(2)}) copy-start(f32[8]{0:T(128)} %intercepts.1) | copy-start | bytes 100
  1.9 9.0 %collective-permute-start = (f32[37,1024]{1,0:T(8,128)S(1)}, f32[37,1024]{1,0:T(8,128)S(1)}, u32[]{:S(2)}, u32[]{:S(2)}) collective-permute-start(f32[37,1024]{1,0:T(8,128)S(1)} %get-tuple-element.43), channel_id=1, source_target_pairs={{1,2},{2,1},{3,4},{4,3},{5,6},{6,5},{7,8},{8,7},{9,10},{10,9},{11,... | collective-permute-start | bytes 454664 | tf_op jit(solution)/shard_map/ppermute | solution.py:27
  2.6 8.3 %collective-permute-start.1 = (f32[37,1024]{1,0:T(8,128)S(1)}, f32[37,1024]{1,0:T(8,128)S(1)}, u32[]{:S(2)}, u32[]{:S(2)}) collective-permute-start(f32[37,1024]{1,0:T(8,128)S(1)} %get-tuple-element.44), channel_id=1, source_target_pairs={{0,1},{1,0},{2,3},{3,2},{4,5},{5,4},{6,7},{7,6},{8,9},{9,8},{10,11... | collective-permute-start | bytes 454664 | tf_op jit(solution)/shard_map/ppermute | solution.py:28
  11.3 11.5 %collective-permute-start.2 = (f32[66,1024]{1,0:T(8,128)S(1)}, f32[66,1024]{1,0:T(8,128)S(1)}, u32[]{:S(2)}, u32[]{:S(2)}) collective-permute-start(f32[66,1024]{1,0:T(8,128)S(1)} %get-tuple-element.52), channel_id=1, source_target_pairs={{1,2},{2,1},{3,4},{4,3},{5,6},{6,5},{7,8},{8,7},{9,10},{10,9},{11,... | collective-permute-start | bytes 811016 | tf_op jit(solution)/shard_map/ppermute | solution.py:27
  12.0 10.9 %collective-permute-start.3 = (f32[66,1024]{1,0:T(8,128)S(1)}, f32[66,1024]{1,0:T(8,128)S(1)}, u32[]{:S(2)}, u32[]{:S(2)}) collective-permute-start(f32[66,1024]{1,0:T(8,128)S(1)} %get-tuple-element.53), channel_id=1, source_target_pairs={{0,1},{1,0},{2,3},{3,2},{4,5},{5,4},{6,7},{7,6},{8,9},{9,8},{10,11... | collective-permute-start | bytes 811016 | tf_op jit(solution)/shard_map/ppermute | solution.py:28
  23.9 1.2 %collective-permute-start.4 = (f32[8,128]{1,0:T(8,128)S(1)}, f32[8,128]{1,0:T(8,128)S(1)}, u32[]{:S(2)}, u32[]{:S(2)}) collective-permute-start(f32[8,128]{1,0:T(8,128)S(1)} %get-tuple-element.71), channel_id=1, source_target_pairs={{0,1},{1,0},{2,3},{3,2},{4,5},{5,4},{6,7},{7,6},{8,9},{9,8},{10,11... | collective-permute-start | bytes 12296 | tf_op jit(solution)/shard_map/ppermute | solution.py:43
  25.1 4.7 %collective-permute-start.7 = (f32[8,128]{1,0:T(8,128)S(1)}, f32[8,128]{1,0:T(8,128)S(1)}, u32[]{:S(2)}, u32[]{:S(2)}) collective-permute-start(f32[8,128]{1,0:T(8,128)S(1)} %add.15.gate), channel_id=1, source_target_pairs={{0,6},{1,7},{2,4},{3,5},{4,2},{5,3},{6,0},{7,1},{8,14},{9,15},{10,... | collective-permute-start | bytes 12296 | tf_op jit(solution)/shard_map/ppermute | solution.py:43
  28.1 3.6 %collective-permute-start.6 = (f32[8,128]{1,0:T(8,128)S(1)}, f32[8,128]{1,0:T(8,128)S(1)}, u32[]{:S(2)}, u32[]{:S(2)}) collective-permute-start(f32[8,128]{1,0:T(8,128)S(1)} %add.15.gate), channel_id=1, source_target_pairs={{0,4},{1,5},{2,6},{3,7},{4,0},{5,1},{6,2},{7,3},{8,12},{9,13},{10,... | collective-permute-start | bytes 12296 | tf_op jit(solution)/shard_map/ppermute | solution.py:43
  28.6 3.6 %collective-permute-start.5 = (f32[8,128]{1,0:T(8,128)S(1)}, f32[8,128]{1,0:T(8,128)S(1)}, u32[]{:S(2)}, u32[]{:S(2)}) collective-permute-start(f32[8,128]{1,0:T(8,128)S(1)} %add.15.gate), channel_id=1, source_target_pairs={{0,2},{1,3},{2,0},{3,1},{4,6},{5,7},{6,4},{7,5},{8,10},{9,11},{10,... | collective-permute-start | bytes 12296 | tf_op jit(solution)/shard_map/ppermute | solution.py:43
  32.2 4.5 %collective-permute-start.8 = (f32[8,128]{1,0:T(8,128)S(1)}, f32[8,128]{1,0:T(8,128)S(1)}, u32[]{:S(2)}, u32[]{:S(2)}) collective-permute-start(f32[8,128]{1,0:T(8,128)S(1)} %add_add_fusion.gate), channel_id=1, source_target_pairs={{0,8},{1,9},{2,10},{3,11},{4,12},{5,13},{6,14},{7,15},{8,0},{9,1},... | collective-permute-start | bytes 12296 | tf_op jit(solution)/shard_map/ppermute | solution.py:43

commit v10 on v9

--- a/solution.py
+++ b/solution.py
@@ -39,6 +39,7 @@
         wide = 2 * step < count
         rounds.append((step, 2 * step, 3 * step) if wide else (step,))
         step *= 4 if wide else 2
+    rounds = rounds[:1] + rounds[:0:-1]
     for number, partners in enumerate(rounds):
         got = [lax.ppermute(values, AX, [(i, i ^ k) for i in range(count)]) for k in partners]
         if number > 0 and len(results) < len(works):

time: 39.5 us -> 39.5 us (level)
  transfers between devices with their start and end apart: 9 -> 9, of which waited for: 4 -> 5; matrix products, arithmetic and copies ran while one was open for 0% -> 0% of each run, Pallas kernels for 33% -> 33%
where the time goes in v10:
time: 39.5 us; the launch traced here: 39.3 us
  Pallas kernels  18.3 us (46%)
  starting transfers between devices  15.7 us (40%)
  waiting for transfers between devices  4.54 us (11%)
  between operations  0.79 us (2%)
    pallas_call x8, Pallas kernels, call(): pl.pallas_call(kernel, out_shape=shapes, in_specs=[pl.BlockSpec(memory_sp...  18.3 us
    ppermute x2, starting transfers between devices, swap_rows(): return (lax.ppermute(near, AX, swap), far)  8.11 us
    ppermute x5, starting transfers between devices, all_sum(): lax.ppermute(values, AX, [(i, i ^ k) for i in range(count)])  6.24 us
    ppermute x5, waiting for transfers between devices, all_sum(): lax.ppermute(values, AX, [(i, i ^ k) for i in range(count)])  4.53 us
    ppermute x2, starting transfers between devices, swap_rows(): far = lax.ppermute(far, AX, cross)  1.35 us
  transfers between devices with their start and end apart: 9, of which 5 were waited for; matrix products, arithmetic and copies ran while one was open for 0% of the time, Pallas kernels for 33%

profile of v10, /device:TPU:0, one launch (start us, length us, event | category | flops | bytes accessed | tf_op | source)
XLA Modules:
  0.0 39.3 jit_solution(453768641108545861)
XLA Ops:
  0.6 0.0 copy-start.1
  0.6 0.0 copy-start.2
  0.7 0.0 copy-start
  0.7 0.0 copy-start.4
  0.7 0.0 copy-start.3
  0.7 1.2 %shard_map.95 = (f32[37,1024]{1,0:T(8,128)S(1)}, f32[37,1024]{1,0:T(8,128)S(1)}) custom-call(f32[16,32,1024]{2,1,0:T(8,128)} %latent.3, f32[32,1024]{1,0:T(8,128)} %kappa_flat.1, s32[32,1024]{1,0:T(8,128)} %land_flat.1), custom_call_target="tpu_custom_call" | custom-call | flops 32768 | bytes 524288 | tf_op jit(solution)/shard_map/pallas_call | solution.py:457
  1.9 0.7 %collective-permute-start = (f32[37,1024]{1,0:T(8,128)S(1)}, f32[37,1024]{1,0:T(8,128)S(1)}, u32[]{:S(2)}, u32[]{:S(2)}) collective-permute-start(f32[37,1024]{1,0:T(8,128)S(1)} %get-tuple-element.43), channel_id=1, source_target_pairs={{1,2},{2,1},{3,4},{4,3},{5,6},{6,5},{7,8},{8,7},{9,10},{10,9},{11,... | collective-permute-start | bytes 454664 | tf_op jit(solution)/shard_map/ppermute | solution.py:27
  2.6 4.4 %collective-permute-start.1 = (f32[37,1024]{1,0:T(8,128)S(1)}, f32[37,1024]{1,0:T(8,128)S(1)}, u32[]{:S(2)}, u32[]{:S(2)}) collective-permute-start(f32[37,1024]{1,0:T(8,128)S(1)} %get-tuple-element.44), channel_id=1, source_target_pairs={{0,1},{1,0},{2,3},{3,2},{4,5},{5,4},{6,7},{7,6},{8,9},{9,8},{10,11... | collective-permute-start | bytes 454664 | tf_op jit(solution)/shard_map/ppermute | solution.py:28
  6.9 0.0 copy-done.4
  6.9 0.0 copy-done.1
  7.0 0.0 copy-done.2
  7.0 0.0 copy-done
  7.0 0.0 copy-done.3
  7.0 3.9 %shard_map.96 = (f32[36,16,1024]{2,1,0:T(8,128)S(1)}, f32[34,16,1024]{2,1,0:T(8,128)S(1)}, f32[32,1,1024]{2,1,0:T(1,128)S(1)}, f32[32,16,1024]{2,1,0:T(8,128)S(1...) custom-call(f32[32]{0:T(128)S(1)} %convert_element_type.3.effects, ...), custom_call_target="tpu_custom_call" | custom-call | flops 20971520 | bytes 6291456 | tf_op jit(solution)/shard_map/pallas_call | solution.py:457
  10.9 0.0 collective-permute-done.got_second.old_second
  10.9 0.0 collective-permute-done.1.got_first.old_first
  10.9 0.4 %shard_map.97 = (f32[38,1,1024]{2,1,0:T(1,128)S(1)}, f32[36,16,1024]{2,1,0:T(8,128)S(1)}, f32[34,16,1024]{2,1,0:T(8,128)S(1)}, f32[32,16,1024]{2,1,0:T(8,128)S(1...) custom-call(f32[37,1024]{1,0:T(8,128)S(1)} %collective-permute-done., ...), custom_call_target="tpu_custom_call", output_to_operand_aliasing={{0}: (4, {}), {1}: (5, {}), {2}: (6, {}), {3}: (7, {}), {4}... | custom-call | flops 5242880 | bytes 524288 | tf_op jit(solution)/shard_map/pallas_call | solution.py:457
  11.3 0.7 %collective-permute-start.2 = (f32[66,1024]{1,0:T(8,128)S(1)}, f32[66,1024]{1,0:T(8,128)S(1)}, u32[]{:S(2)}, u32[]{:S(2)}) collective-permute-start(f32[66,1024]{1,0:T(8,128)S(1)} %get-tuple-element.52), channel_id=1, source_target_pairs={{1,2},{2,1},{3,4},{4,3},{5,6},{6,5},{7,8},{8,7},{9,10},{10,9},{11,... | collective-permute-start | bytes 811016 | tf_op jit(solution)/shard_map/ppermute | solution.py:27
  12.0 3.8 %collective-permute-start.3 = (f32[66,1024]{1,0:T(8,128)S(1)}, f32[66,1024]{1,0:T(8,128)S(1)}, u32[]{:S(2)}, u32[]{:S(2)}) collective-permute-start(f32[66,1024]{1,0:T(8,128)S(1)} %get-tuple-element.53), channel_id=1, source_target_pairs={{0,1},{1,0},{2,3},{3,2},{4,5},{5,4},{6,7},{7,6},{8,9},{9,8},{10,11... | collective-permute-start | bytes 811016 | tf_op jit(solution)/shard_map/ppermute | solution.py:28
  15.8 7.1 %shard_map.98 = (f32[32,16,1024]{2,1,0:T(8,128)S(1)}, f32[36,16,1024]{2,1,0:T(8,128)S(1)}, f32[36,16,1024]{2,1,0:T(8,128)S(1)}, f32[40,16,1024]{2,1,0:T(8,128)S(...) custom-call(f32[38,1,1024]{2,1,0:T(1,128)S(1)} %get-tuple-element.54, ...), custom_call_target="tpu_custom_call", output_to_operand_aliasing={{0}: (6, {}), {1}: (7, {}), {2}: (8, {}), {3}: (9, {})} | custom-call | flops 62914560 | bytes 6291456 | tf_op jit(solution)/shard_map/pallas_call | solution.py:457
  22.9 0.0 collective-permute-done.2.got_second
  22.9 0.0 collective-permute-done.3.got_first
  22.9 1.0 %shard_map.99 = (f32[36,16,1024]{2,1,0:T(8,128)S(1)}, f32[36,16,1024]{2,1,0:T(8,128)S(1)}, f32[40,16,1024]{2,1,0:T(8,128)S(1)}, f32[38,16,1024]{2,1,0:T(8,128)S(...) custom-call(f32[37,1024]{1,0:T(8,128)S(1)} %collective-permute-done., ...), custom_call_target="tpu_custom_call", output_to_operand_aliasing={{0}: (8, {}), {1}: (9, {}), {2}: (10, {}), {3}: (11, {}), {... | custom-call | flops 10485760 | bytes 524288 | tf_op jit(solution)/shard_map/pallas_call | solution.py:457
  23.9 0.1 collective-permute-start.4
  24.0 1.1 %collective-permute-done.4 = f32[8,128]{1,0:T(8,128)S(1)} collective-permute-done((f32[8,128]{1,0:T(8,128)S(1)}, f32[8,128]{1,0:T(8,128)S(1)}, u32[]{:S(2)}, u32[]{:S(2)}) %collective-permute-start.4) | collective-permute-done | bytes 4128 | tf_op jit(solution)/shard_map/ppermute | solution.py:44
  25.1 2.6 %collective-permute-start.5 = (f32[8,128]{1,0:T(8,128)S(1)}, f32[8,128]{1,0:T(8,128)S(1)}, u32[]{:S(2)}, u32[]{:S(2)}) collective-permute-start(f32[8,128]{1,0:T(8,128)S(1)} %add.15.gate), channel_id=1, source_target_pairs={{0,8},{1,9},{2,10},{3,11},{4,12},{5,13},{6,14},{7,15},{8,0},{9,1},... | collective-permute-start | bytes 12296 | tf_op jit(solution)/shard_map/ppermute | solution.py:44
  27.7 1.1 %shard_map.100.rim = f32[16,16,1024]{2,1,0:T(8,128)S(1)} custom-call(f32[8,128]{1,0:T(8,128)S(1)} %add.15.gate, f32[37,1024]{1,0:T(8,128)S(1)} %collective-permute-done.1.got_first.old_first, f32[37,1024]{1,0:T(8,128)S(1)} %collective-permute-done.got_second.old_second, f32[66,1024]{1,0:T(8,128)S(1)} %collective-permute-done.3.got_first, ...), custom_call_target="tpu_custom_call" | custom-call | flops 2097152 | bytes 524288 | tf_op jit(solution)/shard_map/pallas_call | solution.py:457
  28.9 0.7 %collective-permute-done.5 = f32[8,128]{1,0:T(8,128)S(1)} collective-permute-done((f32[8,128]{1,0:T(8,128)S(1)}, f32[8,128]{1,0:T(8,128)S(1)}, u32[]{:S(2)}, u32[]{:S(2)}) %collective-permute-start.5) | collective-permute-done | bytes 4128 | tf_op jit(solution)/shard_map/ppermute | solution.py:44
  29.6 3.0 %collective-permute-start.8 = (f32[8,128]{1,0:T(8,128)S(1)}, f32[8,128]{1,0:T(8,128)S(1)}, u32[]{:S(2)}, u32[]{:S(2)}) collective-permute-start(f32[8,128]{1,0:T(8,128)S(1)} %add.16.gate), channel_id=1, source_target_pairs={{0,6},{1,7},{2,4},{3,5},{4,2},{5,3},{6,0},{7,1},{8,14},{9,15},{10,... | collective-permute-start | bytes 12296 | tf_op jit(solution)/shard_map/ppermute | solution.py:44
  32.6 0.4 %collective-permute-start.7 = (f32[8,128]{1,0:T(8,128)S(1)}, f32[8,128]{1,0:T(8,128)S(1)}, u32[]{:S(2)}, u32[]{:S(2)}) collective-permute-start(f32[8,128]{1,0:T(8,128)S(1)} %add.16.gate), channel_id=1, source_target_pairs={{0,4},{1,5},{2,6},{3,7},{4,0},{5,1},{6,2},{7,3},{8,12},{9,13},{10,... | collective-permute-start | bytes 12296 | tf_op jit(solution)/shard_map/ppermute | solution.py:44
  33.1 0.1 collective-permute-start.6
  33.2 0.8 %shard_map.101.lower = f32[16,16,1024]{2,1,0:T(8,128)S(1)} custom-call(f32[8,128]{1,0:T(8,128)S(1)} %add.16.gate, f32[38,1,1024]{2,1,0:T(1,128)S(1)} %get-tuple-element.54.kappa, f32[36,16,1024]{2,1,0:T(8,128)S(1)} %get-tuple-element.72.weight, f32[36,16,1024]{2,1,0:T(8,128)S(1)} %get-tuple-element.75.second, f32[34,16,1024]{2,1,0:T(8,128)S(1)} %get-tuple-element.76.second_image), custom_call_target="tpu_custom_call" | custom-call | flops 2097152 | bytes 524288 | tf_op jit(solution)/shard_map/pallas_call | solution.py:457
  34.0 0.2 collective-permute-done.8
  34.2 2.0 %collective-permute-done.7 = f32[8,128]{1,0:T(8,128)S(1)} collective-permute-done((f32[8,128]{1,0:T(8,128)S(1)}, f32[8,128]{1,0:T(8,128)S(1)}, u32[]{:S(2)}, u32[]{:S(2)}) %collective-permute-start.7) | collective-permute-done | bytes 4128 | tf_op jit(solution)/shard_map/ppermute | solution.py:44
  36.2 0.4 %collective-permute-done.6 = f32[8,128]{1,0:T(8,128)S(1)} collective-permute-done((f32[8,128]{1,0:T(8,128)S(1)}, f32[8,128]{1,0:T(8,128)S(1)}, u32[]{:S(2)}, u32[]{:S(2)}) %collective-permute-start.6) | collective-permute-done | bytes 4128 | tf_op jit(solution)/shard_map/ppermute | solution.py:44
  36.7 2.6 %shard_map.102 = (f32[16,32,1024]{2,1,0:T(8,128)}, f32[16,32,1024]{2,1,0:T(8,128)}) custom-call(f32[8,128]{1,0:T(8,128)S(1)} %add_add_fusion.sums, f32[32,16,1024]{2,1,0:T(8,128)S(1)} %get-tuple-element.62.grad, f32[40,16,1024]{2,1,0:T(8,128)S(1)} %get-tuple-element.73.search, f32[32,16,1024]{2,1,0:T(8,128)S(1)} %get-tuple-element.81.image, ...), custom_call_target="tpu_custom_call" | custom-call | flops 4194304 | bytes 4194304 | tf_op jit(solution)/shard_map/pallas_call | solution.py:457
  (4 shorter events, 0.0 us)
Async XLA Ops:
  0.6 6.3 %copy-start.1 = (f32[32,1024]{1,0:T(8,128)S(1)}, f32[32,1024]{1,0:T(8,128)}, u32[]{:S(2)}) copy-start(f32[32,1024]{1,0:T(8,128)} %kappa_flat.1) | copy-start | bytes 393220
  0.6 6.3 %copy-start.2 = (s32[32,1024]{1,0:T(8,128)S(1)}, s32[32,1024]{1,0:T(8,128)}, u32[]{:S(2)}) copy-start(s32[32,1024]{1,0:T(8,128)} %land_flat.1) | copy-start | bytes 393220
  0.7 6.3 %copy-start = (f32[16,32,1024]{2,1,0:T(8,128)S(1)}, f32[16,32,1024]{2,1,0:T(8,128)}, u32[]{:S(2)}) copy-start(f32[16,32,1024]{2,1,0:T(8,128)} %latent.3) | copy-start | bytes 6291460
  0.7 6.3 %copy-start.4 = (bf16[32]{0:T(256)(128)(2,1)S(1)}, bf16[32]{0:T(256)(128)(2,1)}, u32[]{:S(2)}) copy-start(bf16[32]{0:T(256)(128)(2,1)} %param.14) | copy-start | bytes 196
  0.7 6.3 %copy-start.3 = (f32[8]{0:T(128)S(1)}, f32[8]{0:T(128)}, u32[]{:S(2)}) copy-start(f32[8]{0:T(128)} %intercepts.1) | copy-start | bytes 100
  1.9 9.0 %collective-permute-start = (f32[37,1024]{1,0:T(8,128)S(1)}, f32[37,1024]{1,0:T(8,128)S(1)}, u32[]{:S(2)}, u32[]{:S(2)}) collective-permute-start(f32[37,1024]{1,0:T(8,128)S(1)} %get-tuple-element.43), channel_id=1, source_target_pairs={{1,2},{2,1},{3,4},{4,3},{5,6},{6,5},{7,8},{8,7},{9,10},{10,9},{11,... | collective-permute-start | bytes 454664 | tf_op jit(solution)/shard_map/ppermute | solution.py:27
  2.6 8.3 %collective-permute-start.1 = (f32[37,1024]{1,0:T(8,128)S(1)}, f32[37,1024]{1,0:T(8,128)S(1)}, u32[]{:S(2)}, u32[]{:S(2)}) collective-permute-start(f32[37,1024]{1,0:T(8,128)S(1)} %get-tuple-element.44), channel_id=1, source_target_pairs={{0,1},{1,0},{2,3},{3,2},{4,5},{5,4},{6,7},{7,6},{8,9},{9,8},{10,11... | collective-permute-start | bytes 454664 | tf_op jit(solution)/shard_map/ppermute | solution.py:28
  11.3 11.5 %collective-permute-start.2 = (f32[66,1024]{1,0:T(8,128)S(1)}, f32[66,1024]{1,0:T(8,128)S(1)}, u32[]{:S(2)}, u32[]{:S(2)}) collective-permute-start(f32[66,1024]{1,0:T(8,128)S(1)} %get-tuple-element.52), channel_id=1, source_target_pairs={{1,2},{2,1},{3,4},{4,3},{5,6},{6,5},{7,8},{8,7},{9,10},{10,9},{11,... | collective-permute-start | bytes 811016 | tf_op jit(solution)/shard_map/ppermute | solution.py:27
  12.0 10.9 %collective-permute-start.3 = (f32[66,1024]{1,0:T(8,128)S(1)}, f32[66,1024]{1,0:T(8,128)S(1)}, u32[]{:S(2)}, u32[]{:S(2)}) collective-permute-start(f32[66,1024]{1,0:T(8,128)S(1)} %get-tuple-element.53), channel_id=1, source_target_pairs={{0,1},{1,0},{2,3},{3,2},{4,5},{5,4},{6,7},{7,6},{8,9},{9,8},{10,11... | collective-permute-start | bytes 811016 | tf_op jit(solution)/shard_map/ppermute | solution.py:28
  23.9 1.2 %collective-permute-start.4 = (f32[8,128]{1,0:T(8,128)S(1)}, f32[8,128]{1,0:T(8,128)S(1)}, u32[]{:S(2)}, u32[]{:S(2)}) collective-permute-start(f32[8,128]{1,0:T(8,128)S(1)} %get-tuple-element.71), channel_id=1, source_target_pairs={{0,1},{1,0},{2,3},{3,2},{4,5},{5,4},{6,7},{7,6},{8,9},{9,8},{10,11... | collective-permute-start | bytes 12296 | tf_op jit(solution)/shard_map/ppermute | solution.py:44
  25.1 4.5 %collective-permute-start.5 = (f32[8,128]{1,0:T(8,128)S(1)}, f32[8,128]{1,0:T(8,128)S(1)}, u32[]{:S(2)}, u32[]{:S(2)}) collective-permute-start(f32[8,128]{1,0:T(8,128)S(1)} %add.15.gate), channel_id=1, source_target_pairs={{0,8},{1,9},{2,10},{3,11},{4,12},{5,13},{6,14},{7,15},{8,0},{9,1},... | collective-permute-start | bytes 12296 | tf_op jit(solution)/shard_map/ppermute | solution.py:44
  29.6 4.6 %collective-permute-start.8 = (f32[8,128]{1,0:T(8,128)S(1)}, f32[8,128]{1,0:T(8,128)S(1)}, u32[]{:S(2)}, u32[]{:S(2)}) collective-permute-start(f32[8,128]{1,0:T(8,128)S(1)} %add.16.gate), channel_id=1, source_target_pairs={{0,6},{1,7},{2,4},{3,5},{4,2},{5,3},{6,0},{7,1},{8,14},{9,15},{10,... | collective-permute-start | bytes 12296 | tf_op jit(solution)/shard_map/ppermute | solution.py:44
  32.6 3.6 %collective-permute-start.7 = (f32[8,128]{1,0:T(8,128)S(1)}, f32[8,128]{1,0:T(8,128)S(1)}, u32[]{:S(2)}, u32[]{:S(2)}) collective-permute-start(f32[8,128]{1,0:T(8,128)S(1)} %add.16.gate), channel_id=1, source_target_pairs={{0,4},{1,5},{2,6},{3,7},{4,0},{5,1},{6,2},{7,3},{8,12},{9,13},{10,... | collective-permute-start | bytes 12296 | tf_op jit(solution)/shard_map/ppermute | solution.py:44
  33.1 3.6 %collective-permute-start.6 = (f32[8,128]{1,0:T(8,128)S(1)}, f32[8,128]{1,0:T(8,128)S(1)}, u32[]{:S(2)}, u32[]{:S(2)}) collective-permute-start(f32[8,128]{1,0:T(8,128)S(1)} %add.16.gate), channel_id=1, source_target_pairs={{0,2},{1,3},{2,0},{3,1},{4,6},{5,7},{6,4},{7,5},{8,10},{9,11},{10,... | collective-permute-start | bytes 12296 | tf_op jit(solution)/shard_map/ppermute | solution.py:44
